TPU v7x, 256 devices: a whole 4x4x8 slice. The times are simulated.
256 devices in a mesh: gx: 16 (over y, x), gy: 16 (over z, core).
Axes of the slice: x: 4, y: 4, z: 8, core: 2. Of those that a mesh axis runs over, the one named last changes fastest.
Arguments:
- points: float32 [64, 128, 3, 256], P('gx', 'gy'), may hold values from 0 to 128, as said below
- right_sides: float32 [64, 128, 4, 256], P('gx', 'gy'), may hold values from -6 to 6
- leaf_counts: int32 [64, 128], P('gx', 'gy'), may hold values from 128 to 256, as said below
- near_mask: int32 [64, 128, 9], P('gx', 'gy'), may hold values from 0 to 1, as said below
- leaf_basis: float32 [64, 128, 64, 256], P('gx', 'gy'), may hold values from -0.375 to 0.375
- leaf_transfer: float32 [64, 128, 64, 64], P('gx', 'gy'), may hold values from -0.75 to 0.75
- upper_transfer: float32 [2, 64, 64], replicated, may hold values from -0.75 to 0.75
- proxy_nodes: float32 [3, 64], replicated, may hold values from -1 to 1
Outputs:
- solution: float32 [64, 128, 4, 256], P('gx', 'gy')
- residual: float32 [64, 128, 4, 256], P('gx', 'gy')
Inputs may be any that keep to these rules, and one draw needn't show every extreme that they name: Coordinates of the points of leaf (a, b): the first lies in [a, a + 1), the second in [b, b + 1), the third in [0, 1). `leaf_counts`: the first leaf of every tile of 4 x 8 leaves is full. `near_mask`: entry 3 i + j is 1 where leaf (a + i - 1, b + j - 1) lies in the near field of leaf (a, b); the entry of the leaf itself is 1, entries of leaves outside the grid are 0, and the relation is symmetric.
All inputs are finite; a program needn't handle non-finite values.
Results may differ from a plain program's by a relative error of at most 0.0003.
Values sent between devices are 32-bit elements; how exact they have to be, the bound alone decides.
No kernel may reach another device: no remote copies, remote signals or barrier semaphores. Data moves between devices by JAX's collectives and lax.ppermute only.
A program may use at most 128 MiB of HBM per device.

v0:
```python
import jax
import jax.numpy as jnp
from jax import lax
from jax.sharding import PartitionSpec as P

ITERS = 2


PRECISE = lax.Precision.HIGHEST
NEAR_LENGTH = 0.5
FAR_LENGTH = 16.0
NOISE_LEVEL = 1.0
COUPLING_SCALE = 1.0 / 128.0


def from_partner(x, axis, bit):
    return lax.ppermute(x, axis, [(i, i ^ 1 << bit) for i in range(lax.axis_size(axis))])


def with_halo(x, sides, width):
    for axis, dim in sides:
        count, length = (lax.axis_size(axis), x.shape[dim])
        up = [(i, (i + 1) % count) for i in range(count - 1)]
        down = [(j, i) for i, j in up]
        last = lax.slice_in_dim(x, length - width, length, axis=dim)
        first = lax.slice_in_dim(x, 0, width, axis=dim)
        before = lax.ppermute(last, axis, up)
        after = lax.ppermute(first, axis, down)
        x = jnp.concatenate([before, x, after], axis=dim)
    return x


def matern(squared, length_value):
    scaled = jnp.sqrt(3.0 * squared) / length_value
    return (1.0 + scaled) * jnp.exp(-scaled)


def kernel_block(target, source):
    squared = (target[..., 0, :, None] - source[..., 0, None, :]) ** 2
    squared = squared + (target[..., 1, :, None] - source[..., 1, None, :]) ** 2
    squared = squared + (target[..., 2, :, None] - source[..., 2, None, :]) ** 2
    return matern(squared, NEAR_LENGTH)


def cluster_nodes(cluster_index, span_width, anchors, tile_rows, tile_cols, count_cols):
    first_device = cluster_index * span_width
    if span_width <= count_cols:
        extent_rows = 1
        extent_cols = span_width
    else:
        extent_rows = span_width // count_cols
        extent_cols = count_cols
    start_row = (first_device // count_cols).astype(jnp.float32)
    start_col = (first_device % count_cols).astype(jnp.float32)
    centre_first = tile_rows * (start_row + 0.5 * extent_rows)
    centre_second = tile_cols * (start_col + 0.5 * extent_cols)
    spots_first = centre_first[..., None] + 0.5 * tile_rows * extent_rows * anchors[0]
    spots_second = centre_second[..., None] + 0.5 * tile_cols * extent_cols * anchors[1]
    spots_third = 0.5 + 0.5 * anchors[2] + 0.0 * spots_first
    return (spots_first, spots_second, spots_third)


def coupling_matrix(target_spots, source_spots):
    squared = (target_spots[0][..., :, None] - source_spots[0][..., None, :]) ** 2
    squared = squared + (target_spots[1][..., :, None] - source_spots[1][..., None, :]) ** 2
    squared = squared + (target_spots[2][..., :, None] - source_spots[2][..., None, :]) ** 2
    return COUPLING_SCALE * matern(squared, FAR_LENGTH)


def solve_small(matrix, right_block):
    order_size = matrix.shape[0]
    row_list = [matrix[position] for position in range(order_size)]
    rhs_list = [right_block[position] for position in range(order_size)]
    for column in range(order_size):
        pivot = row_list[column][column]
        for lower_row in range(column + 1, order_size):
            factor = row_list[lower_row][column] / pivot
            row_list[lower_row] = row_list[lower_row] - factor * row_list[column]
            rhs_list[lower_row] = rhs_list[lower_row] - factor * rhs_list[column]
    result = [rhs_list[0]] * order_size
    for column in reversed(range(order_size)):
        partial_sum = rhs_list[column]
        for later_row in range(column + 1, order_size):
            partial_sum = partial_sum - row_list[column][later_row] * result[later_row]
        result[column] = partial_sum / row_list[column][column]
    return jnp.stack(result)


def exchange_partner(values, bit_number):
    return from_partner(values, ("gx", "gy"), bit_number)


def on_device(
    points,
    right_sides,
    leaf_counts,
    near_mask,
    leaf_basis,
    leaf_transfer,
    upper_transfer,
    proxy_nodes,
):
    tile_rows = points.shape[0]
    tile_cols = points.shape[1]
    leaf_size = points.shape[3]
    count_cols = lax.axis_size("gy")
    total_devices = lax.axis_size("gx") * count_cols
    levels_count = total_devices.bit_length() - 1
    flat_index = lax.axis_index("gx") * count_cols + lax.axis_index("gy")
    valid_mask = (
        jnp.arange(leaf_size, dtype=jnp.int32)[None, None, :] < leaf_counts[:, :, None]
    ).astype(jnp.float32)[:, :, None, :]
    near_scale = 1.0 / leaf_size**0.5
    extended_points = with_halo(points, (("gx", 0), ("gy", 1)), 1)

    def own_nodes(cluster_index, span_width):
        return cluster_nodes(
            cluster_index, span_width, proxy_nodes, tile_rows, tile_cols, count_cols
        )

    def child_transfer(level_index):
        cluster_index = flat_index // 2**level_index
        return jnp.where(cluster_index % 2 == 1, upper_transfer[1], upper_transfer[0])

    def gram_of(left, right_block):
        local_sum = jnp.einsum("abrp,absp->rs", left, right_block, precision=PRECISE)
        return lax.psum(local_sum, ("gx", "gy"))

    solution = jnp.zeros_like(right_sides)
    residual = valid_mask * right_sides
    direction = residual
    gram_now = gram_of(residual, residual)
    for step_index in range(ITERS):
        extended = with_halo(direction, (("gx", 0), ("gy", 1)), 1)
        accumulated = jnp.zeros_like(direction)
        for offset_code in range(9):
            shift_row = offset_code // 3
            shift_col = offset_code % 3
            source = extended_points[
                shift_row : shift_row + tile_rows, shift_col : shift_col + tile_cols
            ]
            values = extended[shift_row : shift_row + tile_rows, shift_col : shift_col + tile_cols]
            kernel_tile = kernel_block(points, source)
            contribution = jnp.einsum("abpq,abrq->abrp", kernel_tile, values, precision=PRECISE)
            accumulated = (
                accumulated
                + near_mask[:, :, offset_code].astype(jnp.float32)[:, :, None, None] * contribution
            )
        local_part = NOISE_LEVEL * direction + near_scale * accumulated
        leaf_coef_up = jnp.einsum("abrp,abkp->abrk", direction, leaf_basis, precision=PRECISE)
        current = jnp.einsum("abrk,abjk->rj", leaf_coef_up, leaf_transfer, precision=PRECISE)
        far_terms = []
        for far_level_index in range(levels_count - 1):
            far_span_width = 2**far_level_index
            far_cluster_index = flat_index // far_span_width
            partner_coef = exchange_partner(current, far_level_index + 1)
            partner_index = far_cluster_index + 2 - 4 * (far_cluster_index // 2 % 2)
            coupling = coupling_matrix(
                own_nodes(far_cluster_index, far_span_width),
                own_nodes(partner_index, far_span_width),
            )
            far_terms.append(jnp.einsum("rb,ab->ra", partner_coef, coupling, precision=PRECISE))
            if far_level_index + 2 < levels_count:
                lifted = jnp.einsum(
                    "rk,jk->rj", current, child_transfer(far_level_index), precision=PRECISE
                )
                current = lifted + exchange_partner(lifted, far_level_index)
        downward = far_terms[-1]
        for far_level_index in reversed(range(levels_count - 2)):
            downward = far_terms[far_level_index] + jnp.einsum(
                "rj,jk->rk", downward, child_transfer(far_level_index), precision=PRECISE
            )
        leaf_coef_down = jnp.einsum("rj,abjk->abrk", downward, leaf_transfer, precision=PRECISE)
        applied = valid_mask * (
            local_part
            + jnp.einsum("abrk,abkp->abrp", leaf_coef_down, leaf_basis, precision=PRECISE)
        )
        curvature = gram_of(direction, applied)
        step_weights = solve_small(curvature, gram_now)
        solution = solution + jnp.einsum(
            "absp,sr->abrp", direction, step_weights, precision=PRECISE
        )
        residual = residual - jnp.einsum("absp,sr->abrp", applied, step_weights, precision=PRECISE)
        if step_index + 1 < ITERS:
            gram_next = gram_of(residual, residual)
            mix_weights = solve_small(gram_now, gram_next)
            direction = residual + jnp.einsum(
                "absp,sr->abrp", direction, mix_weights, precision=PRECISE
            )
            gram_now = gram_next
    return (solution, residual)


def solution(mesh):
    return jax.shard_map(
        on_device,
        mesh=mesh,
        in_specs=(
            P("gx", "gy", None, None),
            P("gx", "gy", None, None),
            P("gx", "gy"),
            P("gx", "gy", None),
            P("gx", "gy", None, None),
            P("gx", "gy", None, None),
            P(),
            P(),
        ),
        out_specs=(P("gx", "gy", None, None), P("gx", "gy", None, None)),
        check_vma=False,
    )
```

profile of v0, /device:TPU:1, one launch (start us, length us, event | category | flops | bytes accessed | tf_op | source)
XLA Modules:
  0.0 732.9 jit_solution(13899788389332567860)
XLA Ops:
  2.2 4.5 collective-permute-start.3
  22.5 16.7 %fusion.186 = f32[4,8,4,256]{3,2,1,0:T(4,128)} fusion(f32[4,8,4,256]{3,2,1,0:T(4,128)S(1)} %broadcast_multiply_fusion, f32[4,8,256]{2,1,0:T(8,128)} %get-tuple-element.83, f32[4,8,256]{2,1,0:T(8,128)} %get-tuple-element.84, f32[4,8,256]{2,1,0:T(8,128)S(1)} %get-tuple-element.82, f32[4,8]{1,0:T(4,128)} %get-tuple-element.4), kind=kOutput, calls=%fused_computation.217 | convolution fusion | flops 127959040 | bytes 360576 | tf_op jit(solution)/shard_map/abpq,abrq->abrp/dot_general | solution.py:144
  42.0 2.5 collective-permute-done.11
  45.3 3.0 collective-permute-start.13
  50.8 5.4 collective-permute-start.15
  58.3 3.0 collective-permute-start.17
  62.4 3.6 collective-permute-start.19
  67.0 4.7 collective-permute-start.20
  82.2 5.2 collective-permute-start.12
  88.6 2.1 collective-permute-start.10
  91.9 3.1 collective-permute-start
  99.3 13.8 %collective-permute-start.7 = (f32[6,1,3,256]{3,1,2,0:T(1,128)S(1)}, f32[6,1,3,256]{3,1,2,0:T(1,128)S(1)}, u32[]{:S(2)}, u32[]{:S(2)}) collective-permute-start(f32[6,1,3,256]{3,1,2,0:T(1,128)S(1)} %get-tuple-element.68), channel_id=1, source_target_pairs={{1,0},{2,1},{3,2},{4,3},{5,4},{6,5},{7,6},{8,7},{9,8},{10,9},{11,1... | collective-permute-start | bytes 55304 | tf_op jit(solution)/shard_map/ppermute | solution.py:28
  113.1 2.5 collective-permute-start.5
  115.7 1.9 collective-permute-start.6
  117.7 3.6 collective-permute-start.2
  121.4 15.1 %fusion.188 = f32[4,8,4,256]{3,2,1,0:T(4,128)S(1)} fusion(f32[4,8,256]{2,1,0:T(8,128)S(1)} %get-tuple-element.77, f32[4,8,256]{2,1,0:T(8,128)S(1)} %get-tuple-element.78, f32[4,8,256]{2,1,0:T(8,128)S(1)} %get-tuple-element.76, f32[4,8,256]{2,1,0:T(8,128)S(1)} %copy-done.57, f32[4,8,256]{2,1,0:T(8,128)S(1)} %copy-done.59, ...), kind=kOutput, calls=%fused_computation.219 | convolution fusion | flops 128000000 | bytes 491648 | tf_op jit(solution)/shard_map/abpq,abrq->abrp/dot_general | solution.py:144
  136.5 15.5 %fusion.190 = f32[4,8,4,256]{3,2,1,0:T(4,128)S(1)} fusion(f32[4,8,256]{2,1,0:T(8,128)S(1)} %get-tuple-element.74, f32[4,8,256]{2,1,0:T(8,128)S(1)} %get-tuple-element.75, f32[4,8,256]{2,1,0:T(8,128)S(1)} %get-tuple-element.73, f32[4,8,256]{2,1,0:T(8,128)S(1)} %copy-done.57, f32[4,8,256]{2,1,0:T(8,128)S(1)} %copy-done.59, ...), kind=kOutput, calls=%fused_computation.221 | convolution fusion | flops 128000000 | bytes 491648 | tf_op jit(solution)/shard_map/abpq,abrq->abrp/dot_general | solution.py:144
  152.4 13.9 %fusion.192 = f32[4,8,4,256]{3,2,1,0:T(4,128)S(1)} fusion(f32[4,8,256]{2,1,0:T(8,128)S(1)} %get-tuple-element.65, f32[4,8,256]{2,1,0:T(8,128)S(1)} %get-tuple-element.66, f32[4,8,256]{2,1,0:T(8,128)S(1)} %get-tuple-element.64, f32[4,8,256]{2,1,0:T(8,128)S(1)} %copy-done.57, f32[4,8,256]{2,1,0:T(8,128)S(1)} %copy-done.59, ...), kind=kOutput, calls=%fused_computation.223 | convolution fusion | flops 127959040 | bytes 548992 | tf_op jit(solution)/shard_map/abpq,abrq->abrp/dot_general | solution.py:144
  166.4 13.9 %fusion.208 = f32[4,8,4,256]{3,2,1,0:T(4,128)S(1)} fusion(f32[4,8,256]{2,1,0:T(8,128)S(1)} %get-tuple-element.55, f32[4,8,256]{2,1,0:T(8,128)S(1)} %get-tuple-element.54, f32[4,8,256]{2,1,0:T(8,128)S(1)} %get-tuple-element.53, f32[4,8,256]{2,1,0:T(8,128)S(1)} %copy-done.57, f32[4,8,256]{2,1,0:T(8,128)S(1)} %copy-done.59, ...), kind=kOutput, calls=%fused_computation.239 | convolution fusion | flops 127959040 | bytes 548992 | tf_op jit(solution)/shard_map/abpq,abrq->abrp/dot_general | solution.py:144
  180.4 14.1 %fusion.210 = f32[4,8,4,256]{3,2,1,0:T(4,128)S(1)} fusion(f32[4,8,256]{2,1,0:T(8,128)S(1)} %get-tuple-element.61, f32[4,8,256]{2,1,0:T(8,128)S(1)} %get-tuple-element.60, f32[4,8,256]{2,1,0:T(8,128)S(1)} %get-tuple-element.59, f32[4,8,256]{2,1,0:T(8,128)S(1)} %copy-done.57, f32[4,8,256]{2,1,0:T(8,128)S(1)} %copy-done.59, ...), kind=kOutput, calls=%fused_computation.241 | convolution fusion | flops 127959040 | bytes 548992 | tf_op jit(solution)/shard_map/abpq,abrq->abrp/dot_general | solution.py:144
  194.7 13.9 %fusion.216 = f32[4,8,4,256]{3,2,1,0:T(4,128)S(1)} fusion(f32[4,8,4,256]{3,2,1,0:T(4,128)S(1)} %copy-done.126, f32[4,8,4,256]{3,2,1,0:T(4,128)S(1)} %fusion.208, f32[4,8,4,256]{3,2,1,0:T(4,128)S(1)} %fusion.210, f32[4,8,4,256]{3,2,1,0:T(4,128)S(1)} %fusion.190, f32[4,8,256]{2,1,0:T(8,128)S(1)} %get-tuple-element.52, f32[4,8,256]{2,1,0:T(8,128)S(1)} %copy-done.57, ...), kind=kOutput, calls=%fused_computation.247 | convolution fusion | flops 128090112 | bytes 1073280 | tf_op jit(solution)/shard_map/abpq,abrq->abrp/dot_general | solution.py:144
  208.7 13.9 %fusion.205 = f32[4,8,4,256]{3,2,1,0:T(4,128)S(1)} fusion(f32[4,8,4,256]{3,2,1,0:T(4,128)S(1)} %fusion.216, f32[4,8,256]{2,1,0:T(8,128)S(1)} %get-tuple-element.63, f32[4,8,256]{2,1,0:T(8,128)S(1)} %get-tuple-element.62, f32[4,8,256]{2,1,0:T(8,128)S(1)} %get-tuple-element.58, f32[4,8,256]{2,1,0:T(8,128)S(1)} %copy-done.57, ...), kind=kOutput, calls=%fused_computation.236 | convolution fusion | flops 127991808 | bytes 680064 | tf_op jit(solution)/shard_map/abpq,abrq->abrp/dot_general | solution.py:144
  222.8 14.1 %fusion.223 = f32[4,8,4,256]{3,2,1,0:T(4,128)S(1)} fusion(f32[4,8,4,256]{3,2,1,0:T(4,128)S(1)} %broadcast_multiply_fusion, f32[4,8,4,256]{3,2,1,0:T(4,128)S(1)} %fusion.192, f32[4,8,4,256]{3,2,1,0:T(4,128)S(1)} %fusion.188, f32[4,8,4,256]{3,2,1,0:T(4,128)S(1)} %fusion.205, f32[4,8,256]{2,1,0:T(8,128)S(1)} %get-tuple-element.56, ...), kind=kOutput, calls=%fused_computation.254 | convolution fusion | flops 128122880 | bytes 1073280 | tf_op jit(solution)/shard_map/abpq,abrq->abrp/dot_general | solution.py:144
  238.7 79.4 %all-reduce = (f32[4,4]{1,0:T(4,128)S(1)}, f32[4,4]{1,0:T(4,128)S(1)}) all-reduce(f32[4,4]{1,0:T(4,128)S(1)} %copy-done.74, f32[4,4]{1,0:T(4,128)S(1)} %convolution_bitcast_fusion.8), channel_id=1, replica_groups=mesh['gx'=16,'gy'=16] {'gx','gy'}, use_global_device_ids=true, to_apply=%region_0.0 | all-reduce | flops 32 | bytes 256 | tf_op jit(solution)/shard_map/psum | solution.py:127
  335.0 6.4 subtract_divide_fusion.8
  342.7 73.5 %psum.30 = f32[4,4]{1,0:T(4,128)S(1)} all-reduce(f32[4,4]{1,0:T(4,128)S(1)} %convolution_bitcast_fusion.7), channel_id=1, replica_groups=mesh['gx'=16,'gy'=16] {'gx','gy'}, use_global_device_ids=true, to_apply=%region_2.3 | all-reduce | flops 16 | bytes 128 | tf_op jit(solution)/shard_map/psum | solution.py:127
  425.8 6.3 subtract_divide_fusion.4
  443.6 2.2 collective-permute-done.30
  446.6 3.3 collective-permute-start.32
  450.0 3.1 collective-permute-done.32
  459.4 16.0 %fusion.187 = f32[4,8,4,256]{3,2,1,0:T(4,128)S(1)} fusion(f32[4,8,4,256]{3,2,1,0:T(4,128)S(1)} %fusion.182, f32[4,8,256]{2,1,0:T(8,128)} %get-tuple-element.83, f32[4,8,256]{2,1,0:T(8,128)} %get-tuple-element.84, f32[4,8,256]{2,1,0:T(8,128)} %copy-done.55, f32[4,8]{1,0:T(4,128)} %get-tuple-element.4), kind=kOutput, calls=%fused_computation.218 | convolution fusion | flops 127959040 | bytes 360576 | tf_op jit(solution)/shard_map/abpq,abrq->abrp/dot_general | solution.py:144
  478.8 4.0 collective-permute-start.21
  484.1 2.1 collective-permute-start.35
  489.3 2.2 collective-permute-done.33
  494.0 2.5 collective-permute-start.29
  497.5 2.8 collective-permute-done.29
  504.1 12.3 %collective-permute-start.24 = (f32[6,1,4,256]{3,2,1,0:T(4,128)S(1)}, f32[6,1,4,256]{3,2,1,0:T(4,128)S(1)}, u32[]{:S(2)}, u32[]{:S(2)}) collective-permute-start(f32[6,1,4,256]{3,2,1,0:T(4,128)S(1)} %get-tuple-element.46), channel_id=1, source_target_pairs={{1,0},{2,1},{3,2},{4,3},{5,4},{6,5},{7,6},{8,7},{9,8},{10,9},{11,1... | collective-permute-start | bytes 73736 | tf_op jit(solution)/shard_map/ppermute | solution.py:28
  516.5 1.9 collective-permute-start.23
  518.5 15.1 %fusion.189 = f32[4,8,4,256]{3,2,1,0:T(4,128)S(1)} fusion(f32[4,8,256]{2,1,0:T(8,128)S(1)} %copy-done.64, f32[4,8,256]{2,1,0:T(8,128)S(1)} %copy-done.66, f32[4,8,256]{2,1,0:T(8,128)S(1)} %copy-done.62, f32[4,8,256]{2,1,0:T(8,128)S(1)} %copy-done.58, f32[4,8,256]{2,1,0:T(8,128)S(1)} %copy-done.60, f32[4,8,256]{2,1,0:T(8,128)S(1)} %copy-done.56, ...), kind=kOutput, calls=%fused_computation.220 | convolution fusion | flops 128000000 | bytes 491648 | tf_op jit(solution)/shard_map/abpq,abrq->abrp/dot_general | solution.py:144
  533.7 15.5 %fusion.191 = f32[4,8,4,256]{3,2,1,0:T(4,128)S(1)} fusion(f32[4,8,256]{2,1,0:T(8,128)S(1)} %copy-done.70, f32[4,8,256]{2,1,0:T(8,128)S(1)} %copy-done.72, f32[4,8,256]{2,1,0:T(8,128)S(1)} %copy-done.68, f32[4,8,256]{2,1,0:T(8,128)S(1)} %copy-done.58, f32[4,8,256]{2,1,0:T(8,128)S(1)} %copy-done.60, f32[4,8,256]{2,1,0:T(8,128)S(1)} %copy-done.56, ...), kind=kOutput, calls=%fused_computation.222 | convolution fusion | flops 128000000 | bytes 491648 | tf_op jit(solution)/shard_map/abpq,abrq->abrp/dot_general | solution.py:144
  549.3 13.9 %fusion.193 = f32[4,8,4,256]{3,2,1,0:T(4,128)S(1)} fusion(f32[4,8,256]{2,1,0:T(8,128)S(1)} %copy-done.46, f32[4,8,256]{2,1,0:T(8,128)S(1)} %copy-done.48, f32[4,8,256]{2,1,0:T(8,128)S(1)} %copy-done.44, f32[4,8,256]{2,1,0:T(8,128)S(1)} %copy-done.58, f32[4,8,256]{2,1,0:T(8,128)S(1)} %copy-done.60, f32[4,8,256]{2,1,0:T(8,128)S(1)} %copy-done.56, ...), kind=kOutput, calls=%fused_computation.224 | convolution fusion | flops 127959040 | bytes 548992 | tf_op jit(solution)/shard_map/abpq,abrq->abrp/dot_general | solution.py:144
  563.3 13.9 %fusion.209 = f32[4,8,4,256]{3,2,1,0:T(4,128)S(1)} fusion(f32[4,8,256]{2,1,0:T(8,128)S(1)} %copy-done.54, f32[4,8,256]{2,1,0:T(8,128)S(1)} %copy-done.52, f32[4,8,256]{2,1,0:T(8,128)S(1)} %copy-done.50, f32[4,8,256]{2,1,0:T(8,128)S(1)} %copy-done.58, f32[4,8,256]{2,1,0:T(8,128)S(1)} %copy-done.60, f32[4,8,256]{2,1,0:T(8,128)S(1)} %copy-done.56, ...), kind=kOutput, calls=%fused_computation.240 | convolution fusion | flops 127959040 | bytes 548992 | tf_op jit(solution)/shard_map/abpq,abrq->abrp/dot_general | solution.py:144
  577.4 14.1 %fusion.211 = f32[4,8,4,256]{3,2,1,0:T(4,128)S(1)} fusion(f32[4,8,256]{2,1,0:T(8,128)S(1)} %copy-done.36, f32[4,8,256]{2,1,0:T(8,128)S(1)} %copy-done.34, f32[4,8,256]{2,1,0:T(8,128)S(1)} %copy-done.32, f32[4,8,256]{2,1,0:T(8,128)S(1)} %copy-done.58, f32[4,8,256]{2,1,0:T(8,128)S(1)} %copy-done.60, f32[4,8,256]{2,1,0:T(8,128)S(1)} %copy-done.56, ...), kind=kOutput, calls=%fused_computation.242 | convolution fusion | flops 127959040 | bytes 548992 | tf_op jit(solution)/shard_map/abpq,abrq->abrp/dot_general | solution.py:144
  591.7 13.9 %fusion.221 = f32[4,8,4,256]{3,2,1,0:T(4,128)S(1)} fusion(f32[4,8,4,256]{3,2,1,0:T(4,128)S(1)} %fusion.187, f32[4,8,4,256]{3,2,1,0:T(4,128)S(1)} %fusion.209, f32[4,8,4,256]{3,2,1,0:T(4,128)S(1)} %fusion.211, f32[4,8,4,256]{3,2,1,0:T(4,128)S(1)} %fusion.191, f32[4,8,256]{2,1,0:T(8,128)S(1)} %copy-done.42, f32[4,8,256]{2,1,0:T(8,128)S(1)} %copy-done.58, ...), kind=kOutput, calls=%fused_computation.252 | convolution fusion | flops 128090112 | bytes 1073280 | tf_op jit(solution)/shard_map/abpq,abrq->abrp/dot_general | solution.py:144
  605.8 13.9 %fusion.207 = f32[4,8,4,256]{3,2,1,0:T(4,128)S(1)} fusion(f32[4,8,4,256]{3,2,1,0:T(4,128)S(1)} %fusion.221, f32[4,8,256]{2,1,0:T(8,128)S(1)} %copy-done.24, f32[4,8,256]{2,1,0:T(8,128)S(1)} %copy-done.22, f32[4,8,256]{2,1,0:T(8,128)S(1)} %copy-done.20, f32[4,8,256]{2,1,0:T(8,128)S(1)} %copy-done.58, f32[4,8,256]{2,1,0:T(8,128)S(1)} %copy-done.60, ...), kind=kOutput, calls=%fused_computation.238 | convolution fusion | flops 127991808 | bytes 680064 | tf_op jit(solution)/shard_map/abpq,abrq->abrp/dot_general | solution.py:144
  619.8 14.0 %fusion.222 = f32[4,8,4,256]{3,2,1,0:T(4,128)S(1)} fusion(f32[4,8,4,256]{3,2,1,0:T(4,128)S(1)} %fusion.182, f32[4,8,4,256]{3,2,1,0:T(4,128)S(1)} %fusion.193, f32[4,8,4,256]{3,2,1,0:T(4,128)S(1)} %fusion.189, f32[4,8,4,256]{3,2,1,0:T(4,128)S(1)} %fusion.207, f32[4,8,256]{2,1,0:T(8,128)S(1)} %copy-done.28, f32[4,8,256]{2,1,0:T(8,128)S(1)} %copy-done.30, ...), kind=kOutput, calls=%fused_computation.253 | convolution fusion | flops 128122880 | bytes 1073280 | tf_op jit(solution)/shard_map/abpq,abrq->abrp/dot_general | solution.py:144
  636.1 75.8 %psum.31 = f32[4,4]{1,0:T(4,128)S(1)} all-reduce(f32[4,4]{1,0:T(4,128)S(1)} %convolution_bitcast_fusion.5), channel_id=1, replica_groups=mesh['gx'=16,'gy'=16] {'gx','gy'}, use_global_device_ids=true, to_apply=%region_3.4 | all-reduce | flops 16 | bytes 128 | tf_op jit(solution)/shard_map/psum | solution.py:127
  724.1 6.1 subtract_divide_fusion
  (440 shorter events, 101.6 us)
Async XLA Ops:
  2.2 95.5 %collective-permute-start.3 = (f32[1,8,3,256]{3,1,2,0:T(8,128)}, f32[1,8,3,256]{3,1,2,0:T(8,128)}, u32[]{:S(2)}, u32[]{:S(2)}) collective-permute-start(f32[1,8,3,256]{3,1,2,0:T(8,128)} %get-tuple-element.86), channel_id=1, source_target_pairs={{0,16},{16,32},{32,48},{48,64},{64,80},{80,96},{96,112},{112,128},... | collective-permute-start | bytes 73736 | tf_op jit(solution)/shard_map/ppermute | solution.py:27
  6.7 91.8 %collective-permute-start.4 = (f32[1,8,3,256]{3,1,2,0:T(8,128)}, f32[1,8,3,256]{3,1,2,0:T(8,128)}, u32[]{:S(2)}, u32[]{:S(2)}) collective-permute-start(f32[1,8,3,256]{3,1,2,0:T(8,128)} %get-tuple-element.85), channel_id=1, source_target_pairs={{16,0},{32,16},{48,32},{64,48},{80,64},{96,80},{112,96},{128,112},... | collective-permute-start | bytes 73736 | tf_op jit(solution)/shard_map/ppermute | solution.py:28
  10.4 105.3 %collective-permute-start.1 = (f32[1,8,4,256]{3,2,1,0:T(4,128)}, f32[1,8,4,256]{3,2,1,0:T(4,128)S(1)}, u32[]{:S(2)}, u32[]{:S(2)}) collective-permute-start(f32[1,8,4,256]{3,2,1,0:T(4,128)} %get-tuple-element.72), channel_id=1, source_target_pairs={{16,0},{32,16},{48,32},{64,48},{80,64},{96,80},{112,96},{128,112},... | collective-permute-start | bytes 98312 | tf_op jit(solution)/shard_map/ppermute | solution.py:28
  15.2 81.0 %collective-permute-start.8 = (f32[4,64]{1,0:T(4,128)}, f32[4,64]{1,0:T(4,128)}, u32[]{:S(2)}, u32[]{:S(2)}) collective-permute-start(f32[4,64]{1,0:T(4,128)} %convolution_bitcast_fusion.9), channel_id=1, source_target_pairs={{0,2},{1,3},{2,0},{3,1},{4,6},{5,7},{6,4},{7,5},{8,10},{9,11},{10,... | collective-permute-start | bytes 3080 | tf_op jit(solution)/shard_map/ppermute | solution.py:17
  17.6 57.4 %copy-start.13 = (f32[1,64,64]{2,1,0:T(8,128)}, f32[1,64,64]{2,1,0:T(8,128)S(1)}, u32[]{:S(2)}) copy-start(f32[1,64,64]{2,1,0:T(8,128)S(1)} %get-tuple-element.87) | copy-start | bytes 49156
  17.6 60.0 %copy-start.11 = (f32[1,64,64]{2,1,0:T(8,128)}, f32[1,64,64]{2,1,0:T(8,128)S(1)}, u32[]{:S(2)}) copy-start(f32[1,64,64]{2,1,0:T(8,128)S(1)} %get-tuple-element.90) | copy-start | bytes 49156
  17.6 64.1 %copy-start.9 = (f32[1,64,64]{2,1,0:T(8,128)}, f32[1,64,64]{2,1,0:T(8,128)S(1)}, u32[]{:S(2)}) copy-start(f32[1,64,64]{2,1,0:T(8,128)S(1)} %get-tuple-element.89) | copy-start | bytes 49156
  17.6 70.7 %copy-start.7 = (f32[1,64,64]{2,1,0:T(8,128)}, f32[1,64,64]{2,1,0:T(8,128)S(1)}, u32[]{:S(2)}) copy-start(f32[1,64,64]{2,1,0:T(8,128)S(1)} %get-tuple-element.88) | copy-start | bytes 49156
  17.6 74.0 %copy-start.5 = (f32[1,64,64]{2,1,0:T(8,128)}, f32[1,64,64]{2,1,0:T(8,128)S(1)}, u32[]{:S(2)}) copy-start(f32[1,64,64]{2,1,0:T(8,128)S(1)} %get-tuple-element.92) | copy-start | bytes 49156
  17.7 78.3 %copy-start.3 = (f32[1,64,64]{2,1,0:T(8,128)}, f32[1,64,64]{2,1,0:T(8,128)S(1)}, u32[]{:S(2)}) copy-start(f32[1,64,64]{2,1,0:T(8,128)S(1)} %get-tuple-element.91) | copy-start | bytes 49156
  19.1 22.0 %collective-permute-start.9 = (f32[4,64]{1,0:T(4,128)}, f32[4,64]{1,0:T(4,128)}, u32[]{:S(2)}, u32[]{:S(2)}) collective-permute-start(f32[4,64]{1,0:T(4,128)} %fusion.318), channel_id=1, source_target_pairs={{0,1},{1,0},{2,3},{3,2},{4,5},{5,4},{6,7},{7,6},{8,9},{9,8},{10,11... | collective-permute-start | bytes 3080 | tf_op jit(solution)/shard_map/ppermute | solution.py:17
  21.7 201.0 %copy-start.55 = (f32[4,8,256]{2,1,0:T(8,128)}, f32[4,8,256]{2,1,0:T(8,128)S(1)}, u32[]{:S(2)}) copy-start(f32[4,8,256]{2,1,0:T(8,128)S(1)} %get-tuple-element.82) | copy-start | bytes 98308
  41.9 2.6 collective-permute-start.11
  45.3 4.1 collective-permute-start.13
  50.8 6.7 collective-permute-start.15
  58.3 4.0 collective-permute-start.17
  62.4 4.5 collective-permute-start.19
  67.0 6.0 collective-permute-start.20
  73.0 2.4 collective-permute-start.18
  75.4 4.1 collective-permute-start.16
  79.6 2.7 collective-permute-start.14
  82.2 6.3 collective-permute-start.12
  88.6 3.3 collective-permute-start.10
  91.9 23.8 %collective-permute-start = (f32[1,8,4,256]{3,2,1,0:T(4,128)}, f32[1,8,4,256]{3,2,1,0:T(4,128)S(1)}, u32[]{:S(2)}, u32[]{:S(2)}) collective-permute-start(f32[1,8,4,256]{3,2,1,0:T(4,128)} %get-tuple-element.71), channel_id=1, source_target_pairs={{0,16},{16,32},{32,48},{48,64},{64,80},{80,96},{96,112},{112,128},... | collective-permute-start | bytes 98312 | tf_op jit(solution)/shard_map/ppermute | solution.py:27
  99.3 52.7 %collective-permute-start.7 = (f32[6,1,3,256]{3,1,2,0:T(1,128)S(1)}, f32[6,1,3,256]{3,1,2,0:T(1,128)S(1)}, u32[]{:S(2)}, u32[]{:S(2)}) collective-permute-start(f32[6,1,3,256]{3,1,2,0:T(1,128)S(1)} %get-tuple-element.68), channel_id=1, source_target_pairs={{1,0},{2,1},{3,2},{4,3},{5,4},{6,5},{7,6},{8,7},{9,8},{10,9},{11,1... | collective-permute-start | bytes 55304 | tf_op jit(solution)/shard_map/ppermute | solution.py:28
  113.1 39.0 %collective-permute-start.5 = (f32[6,1,3,256]{3,1,2,0:T(1,128)S(1)}, f32[6,1,3,256]{3,1,2,0:T(1,128)S(1)}, u32[]{:S(2)}, u32[]{:S(2)}) collective-permute-start(f32[6,1,3,256]{3,1,2,0:T(1,128)S(1)} %get-tuple-element.67), channel_id=1, source_target_pairs={{0,1},{1,2},{2,3},{3,4},{4,5},{5,6},{6,7},{7,8},{8,9},{9,10},{10,1... | collective-permute-start | bytes 55304 | tf_op jit(solution)/shard_map/ppermute | solution.py:27
  115.7 36.5 %collective-permute-start.6 = (f32[6,1,4,256]{3,2,1,0:T(4,128)S(1)}, f32[6,1,4,256]{3,2,1,0:T(4,128)S(1)}, u32[]{:S(2)}, u32[]{:S(2)}) collective-permute-start(f32[6,1,4,256]{3,2,1,0:T(4,128)S(1)} %get-tuple-element.48), channel_id=1, source_target_pairs={{1,0},{2,1},{3,2},{4,3},{5,4},{6,5},{7,6},{8,7},{9,8},{10,9},{11,1... | collective-permute-start | bytes 73736 | tf_op jit(solution)/shard_map/ppermute | solution.py:28
  117.7 48.6 %collective-permute-start.2 = (f32[6,1,4,256]{3,2,1,0:T(4,128)S(1)}, f32[6,1,4,256]{3,2,1,0:T(4,128)S(1)}, u32[]{:S(2)}, u32[]{:S(2)}) collective-permute-start(f32[6,1,4,256]{3,2,1,0:T(4,128)S(1)} %get-tuple-element.47), channel_id=1, source_target_pairs={{0,1},{1,2},{2,3},{3,4},{4,5},{5,6},{6,7},{7,8},{8,9},{9,10},{10,1... | collective-permute-start | bytes 73736 | tf_op jit(solution)/shard_map/ppermute | solution.py:27
  152.2 70.5 %copy-start.25 = (f32[4,8,256]{2,1,0:T(8,128)}, f32[4,8,256]{2,1,0:T(8,128)S(1)}, u32[]{:S(2)}) copy-start(f32[4,8,256]{2,1,0:T(8,128)S(1)} %get-tuple-element.49) | copy-start | bytes 98308
  152.2 70.5 %copy-start.27 = (f32[4,8,256]{2,1,0:T(8,128)}, f32[4,8,256]{2,1,0:T(8,128)S(1)}, u32[]{:S(2)}) copy-start(f32[4,8,256]{2,1,0:T(8,128)S(1)} %get-tuple-element.56) | copy-start | bytes 98308
  152.3 70.5 %copy-start.29 = (f32[4,8,256]{2,1,0:T(8,128)}, f32[4,8,256]{2,1,0:T(8,128)S(1)}, u32[]{:S(2)}) copy-start(f32[4,8,256]{2,1,0:T(8,128)S(1)} %get-tuple-element.57) | copy-start | bytes 98308
  436.3 1.5 collective-permute-start.26
  438.7 2.8 collective-permute-start.28
  442.4 3.4 collective-permute-start.30
  446.6 6.4 collective-permute-start.32
  453.9 2.5 collective-permute-start.34
  457.6 17.8 %collective-permute-start.36 = (f32[4,64]{1,0:T(4,128)S(1)}, f32[4,64]{1,0:T(4,128)S(1)}, u32[]{:S(2)}, u32[]{:S(2)}) collective-permute-start(f32[4,64]{1,0:T(4,128)S(1)} %fusion.274), channel_id=1, source_target_pairs={{0,32},{1,33},{2,34},{3,35},{4,36},{5,37},{6,38},{7,39},{8,40},{9,... | collective-permute-start | bytes 3080 | tf_op jit(solution)/shard_map/ppermute | solution.py:17
  475.5 8.6 %collective-permute-start.37 = (f32[4,64]{1,0:T(4,128)S(1)}, f32[4,64]{1,0:T(4,128)S(1)}, u32[]{:S(2)}, u32[]{:S(2)}) collective-permute-start(f32[4,64]{1,0:T(4,128)S(1)} %add.1493), channel_id=1, source_target_pairs={{0,128},{1,129},{2,130},{3,131},{4,132},{5,133},{6,134},{7,135},{8... | collective-permute-start | bytes 3080 | tf_op jit(solution)/shard_map/ppermute | solution.py:17
  476.1 26.4 %collective-permute-start.25 = (f32[4,64]{1,0:T(4,128)S(1)}, f32[4,64]{1,0:T(4,128)S(1)}, u32[]{:S(2)}, u32[]{:S(2)}) collective-permute-start(f32[4,64]{1,0:T(4,128)S(1)} %convolution_bitcast_fusion.6), channel_id=1, source_target_pairs={{0,2},{1,3},{2,0},{3,1},{4,6},{5,7},{6,4},{7,5},{8,10},{9,11},{10,... | collective-permute-start | bytes 3080 | tf_op jit(solution)/shard_map/ppermute | solution.py:17
  477.6 26.5 %collective-permute-start.22 = (f32[1,8,4,256]{3,2,1,0:T(4,128)S(1)}, f32[1,8,4,256]{3,2,1,0:T(4,128)S(1)}, u32[]{:S(2)}, u32[]{:S(2)}) collective-permute-start(f32[1,8,4,256]{3,2,1,0:T(4,128)S(1)} %get-tuple-element.70), channel_id=1, source_target_pairs={{16,0},{32,16},{48,32},{64,48},{80,64},{96,80},{112,96},{128,112},... | collective-permute-start | bytes 98312 | tf_op jit(solution)/shard_map/ppermute | solution.py:28
  478.8 25.2 %collective-permute-start.21 = (f32[1,8,4,256]{3,2,1,0:T(4,128)S(1)}, f32[1,8,4,256]{3,2,1,0:T(4,128)S(1)}, u32[]{:S(2)}, u32[]{:S(2)}) collective-permute-start(f32[1,8,4,256]{3,2,1,0:T(4,128)S(1)} %get-tuple-element.69), channel_id=1, source_target_pairs={{0,16},{16,32},{32,48},{48,64},{64,80},{80,96},{96,112},{112,128},... | collective-permute-start | bytes 98312 | tf_op jit(solution)/shard_map/ppermute | solution.py:27
  482.8 18.6 %collective-permute-start.27 = (f32[4,64]{1,0:T(4,128)S(1)}, f32[4,64]{1,0:T(4,128)S(1)}, u32[]{:S(2)}, u32[]{:S(2)}) collective-permute-start(f32[4,64]{1,0:T(4,128)S(1)} %add.1488), channel_id=1, source_target_pairs={{0,4},{1,5},{2,6},{3,7},{4,0},{5,1},{6,2},{7,3},{8,12},{9,13},{10,... | collective-permute-start | bytes 3080 | tf_op jit(solution)/shard_map/ppermute | solution.py:17
  484.1 3.2 collective-permute-start.35
  487.3 4.2 collective-permute-start.33
  491.5 2.5 collective-permute-start.31
  494.0 6.3 collective-permute-start.29
  504.1 45.0 %collective-permute-start.24 = (f32[6,1,4,256]{3,2,1,0:T(4,128)S(1)}, f32[6,1,4,256]{3,2,1,0:T(4,128)S(1)}, u32[]{:S(2)}, u32[]{:S(2)}) collective-permute-start(f32[6,1,4,256]{3,2,1,0:T(4,128)S(1)} %get-tuple-element.46), channel_id=1, source_target_pairs={{1,0},{2,1},{3,2},{4,3},{5,4},{6,5},{7,6},{8,7},{9,8},{10,9},{11,1... | collective-permute-start | bytes 73736 | tf_op jit(solution)/shard_map/ppermute | solution.py:28
  516.5 46.7 %collective-permute-start.23 = (f32[6,1,4,256]{3,2,1,0:T(4,128)S(1)}, f32[6,1,4,256]{3,2,1,0:T(4,128)S(1)}, u32[]{:S(2)}, u32[]{:S(2)}) collective-permute-start(f32[6,1,4,256]{3,2,1,0:T(4,128)S(1)} %get-tuple-element.45), channel_id=1, source_target_pairs={{0,1},{1,2},{2,3},{3,4},{4,5},{5,6},{6,7},{7,8},{8,9},{9,10},{10,1... | collective-permute-start | bytes 73736 | tf_op jit(solution)/shard_map/ppermute | solution.py:27
  (117 other events, 3158.3 us)
where the time goes:
time: 744 us; the launch traced here: 733 us
  matrix products  300 us (40%)
  blocking collectives  229 us (31%)
  starting transfers between devices  105 us (14%)
  other arithmetic  29.5 us (4%)
  between operations  26.9 us (4%)
  waiting for transfers between devices  22.8 us (3%)
  local copies, waits for them, and re-layouts  19.7 us (3%)
    dot_general x18, matrix products, on_device(): jnp.einsum('abpq,abrq->abrp', kernel_tile, values, precision=PRECISE)  261 us
    psum x3, blocking collectives, gram_of(): return lax.psum(local_sum, ('gx', 'gy'))  229 us
    ppermute x26, starting transfers between devices, from_partner(): lax.ppermute(x, axis, [(i, i ^ 1 << bit) for i in range(lax.axis_size(axi...  53.5 us
    ppermute x6, starting transfers between devices, with_halo(): after = lax.ppermute(first, axis, down)  32 us
    ppermute x26, waiting for transfers between devices, from_partner(): lax.ppermute(x, axis, [(i, i ^ 1 << bit) for i in range(lax.axis_size(axi...  22.8 us
    ppermute x6, starting transfers between devices, with_halo(): before = lax.ppermute(last, axis, up)  19.7 us
    div x3, other arithmetic, solve_small(): result[column] = partial_sum / row_list[column][column]  18.8 us
  transfers between devices with their start and end apart: 38, of which 18 were waited for; matrix products, arithmetic and copies ran while one was open for 21% of the time, Pallas kernels for 0%

commit v1 on v0

v1 whole, which is shorter than its diff:
```python
import functools

import jax
import jax.numpy as jnp
import numpy as np
from jax import lax
from jax.experimental import pallas as pl
from jax.experimental.pallas import tpu as pltpu
from jax.sharding import PartitionSpec as P

F32 = jnp.float32
BF = jnp.bfloat16
NEAR_LENGTH = 0.5
FAR_LENGTH = 16.0
NEAR_RATE = 3.0**0.5 / NEAR_LENGTH
FAR_RATE = 3.0**0.5 / FAR_LENGTH
LOG2E = 1.4426950408889634
COUPLING_SCALE = 1.0 / 128.0
UNROLL = 8
CHUNK = 64
VMEM_LIMIT = 48 * 2**20
VM = pl.BlockSpec(memory_space=pltpu.VMEM)
SM = pl.BlockSpec(memory_space=pltpu.SMEM)


def rounded(x):
    return x.astype(BF).astype(F32)


def split2(x):
    high = x.astype(BF)
    return high, (x - high.astype(F32)).astype(BF)


def rows16(x):
    first = rounded(x)
    second = rounded(x - first)
    third = rounded(x - first - second)
    return jnp.concatenate([first, second, third, jnp.zeros_like(x)], axis=0).astype(BF)


def join16(y):
    return y[0:4] + y[4:8] + y[8:12]


def dot(a, b):
    return jnp.dot(a, b, preferred_element_type=F32)


def dot_nt(a, b):
    return lax.dot_general(a, b, (((1,), (1,)), ((), ())), preferred_element_type=F32)


def dot3(a, b):
    a_high, a_low = split2(a)
    b_high, b_low = split2(b)
    return dot(a_high, b_high) + (dot(a_low, b_high) + dot(a_high, b_low))


def feature_tables():
    target = np.zeros((32, 24), np.float32)
    source = np.zeros((32, 24), np.float32)
    factor = np.ones((9, 32), np.float32)
    one = 19
    for c in range(3):
        target[2 * c, c] = target[2 * c + 1, c] = -2
        source[2 * c, c] = source[2 * c + 1, 8 + c] = 1
        target[6 + 2 * c, 8 + c] = target[7 + 2 * c, 8 + c] = -2
        source[6 + 2 * c, c] = source[7 + 2 * c, 8 + c] = 1
    for k in range(3):
        target[12 + k, one] = source[12 + k, 16 + k] = 1
        target[15 + k, 16 + k] = source[15 + k, one] = 1
    for c in range(2):
        target[18 + 2 * c, c] = target[19 + 2 * c, 8 + c] = 1
        source[18 + 2 * c, one] = source[19 + 2 * c, one] = 1
        target[22 + 2 * c, one] = target[23 + 2 * c, one] = 1
        source[22 + 2 * c, c] = source[23 + 2 * c, 8 + c] = 1
    target[26, one] = source[26, one] = 1
    for code in range(9):
        off = (code // 3 - 1, code % 3 - 1)
        for c in range(2):
            factor[code, 18 + 2 * c : 20 + 2 * c] = -2 * off[c]
            factor[code, 22 + 2 * c : 24 + 2 * c] = 2 * off[c]
        factor[code, 26] = off[0] ** 2 + off[1] ** 2
    return target, source, factor


def geometry_kernel(x_ref, target_ref, source_ref, s_ref, t_ref):
    row = lax.broadcasted_iota(jnp.int32, (8, x_ref.shape[2]), 0)

    def body(e, carry):
        x = jnp.where(row < 3, x_ref[e], 0.0)
        first = rounded(x)
        second = rounded(x - first)
        held = first + second
        norm = jnp.sum(held * held, axis=0, keepdims=True)
        n1 = rounded(norm)
        n2 = rounded(norm - n1)
        n3 = rounded(norm - n1 - n2)
        last = jnp.where(row == 0, n1, jnp.where(row == 1, n2, jnp.where(row == 2, n3, jnp.where(row == 3, 1.0, 0.0))))
        f = jnp.concatenate([first, second, last], axis=0).astype(BF)
        t_ref[e] = dot(target_ref[...], f).astype(BF)
        s_ref[e] = lax.dot_general(
            f, source_ref[...], (((0,), (1,)), ((), ())), preferred_element_type=F32
        ).astype(BF)
        return carry

    lax.fori_loop(0, x_ref.shape[0], body, 0, unroll=4)


def geometry(x, target_table, source_table):
    leaves, _, size = x.shape
    return pl.pallas_call(
        geometry_kernel,
        out_shape=[
            jax.ShapeDtypeStruct((leaves, size, 32), BF),
            jax.ShapeDtypeStruct((leaves, 32, size), BF),
        ],
        in_specs=[VM] * 3,
        out_specs=[VM] * 2,
        compiler_params=pltpu.CompilerParams(vmem_limit_bytes=VMEM_LIMIT),
        name="geometry",
    )(x, jnp.asarray(target_table, BF), jnp.asarray(source_table, BF))


def near_kernel(nx, ny, mask_ref, v_ref, s_ref, t_ref, factor_ref, o_ref, v16, acc, todo):
    wide = ny + 2
    leaves = (nx + 2) * wide
    size = v_ref.shape[2]

    def split_leaf(e, carry):
        v16[e] = rows16(v_ref[e])
        return carry

    lax.fori_loop(0, leaves, split_leaf, 0, unroll=4)
    v16[leaves] = jnp.zeros((16, size), BF)
    acc[...] = jnp.zeros_like(acc)

    def note(i, count):
        todo[count] = i
        return count + jnp.where(mask_ref[i] != 0, 1, 0)

    count = lax.fori_loop(0, nx * ny * 9, note, 0, unroll=8)
    for j in range(UNROLL):
        todo[count + j] = -1

    def one_pair(i):
        entry = todo[i]
        pair = jnp.maximum(entry, 0)
        a = pair // 9
        code = pair - a * 9
        row = a // ny
        col = a - row * ny
        code_row = code // 3
        code_col = code - code_row * 3
        source = (row + code_row) * wide + col + code_col
        t = t_ref[(row + 1) * wide + col + 1] * factor_ref[code]
        s = s_ref[source]
        v = v16[jnp.where(entry < 0, leaves, source)]
        total = jnp.zeros((16, size), F32)
        for k in range(size // CHUNK):
            part = slice(k * CHUNK, (k + 1) * CHUNK)
            squared = jnp.maximum(dot(s[part], t), 1e-30)
            distance = squared * lax.rsqrt(squared)
            value = (1.0 + NEAR_RATE * distance) * jnp.exp2((-NEAR_RATE * LOG2E) * distance)
            high, low = split2(value)
            total += dot(v[:, part], high) + dot(v[:, part], low)
        return a, total

    def group(g, carry):
        for a, total in [one_pair(g * UNROLL + j) for j in range(UNROLL)]:
            acc[a] += total
        return carry

    lax.fori_loop(0, (count + UNROLL - 1) // UNROLL, group, 0)

    def finish(a, carry):
        o_ref[a] = join16(acc[a]) * (1.0 / size**0.5)
        return carry

    lax.fori_loop(0, nx * ny, finish, 0, unroll=4)


def near_field(nx, ny, mask, v, s, t, factor):
    leaves, _, size = v.shape
    return pl.pallas_call(
        functools.partial(near_kernel, nx, ny),
        out_shape=jax.ShapeDtypeStruct((nx * ny, 4, size), F32),
        in_specs=[SM, VM, VM, VM, VM],
        out_specs=VM,
        scratch_shapes=[
            pltpu.VMEM((leaves + 1, 16, size), BF),
            pltpu.VMEM((nx * ny, 16, size), F32),
            pltpu.SMEM((nx * ny * 9 + UNROLL,), jnp.int32),
        ],
        compiler_params=pltpu.CompilerParams(vmem_limit_bytes=VMEM_LIMIT),
        name="near",
    )(mask, v, s, t, factor)


def upward_kernel(r_ref, basis_ref, transfer_ref, high_ref, low_ref, c_ref):
    leaves = r_ref.shape[0]

    def body(a, total):
        b_high, b_low = split2(basis_ref[a])
        t_high, t_low = split2(transfer_ref[a])
        joint = dot(t_high, b_high) + (dot(t_low, b_high) + dot(t_high, b_low))
        high, low = split2(joint)
        high_ref[a] = high
        low_ref[a] = low
        v = rows16(r_ref[a])
        return total + (dot_nt(v, high) + dot_nt(v, low))

    total = lax.fori_loop(0, leaves, body, jnp.zeros((16, 64), F32), unroll=4)
    c_ref[...] = jnp.concatenate([join16(total), jnp.zeros((4, 64), F32)], axis=0)


def upward(r, basis, transfer):
    leaves, _, size = r.shape
    terms = basis.shape[1]
    joint = jax.ShapeDtypeStruct((leaves, terms, size), BF)
    return pl.pallas_call(
        upward_kernel,
        out_shape=[joint, joint, jax.ShapeDtypeStruct((8, terms), F32)],
        in_specs=[VM] * 3,
        out_specs=[VM] * 3,
        compiler_params=pltpu.CompilerParams(vmem_limit_bytes=VMEM_LIMIT),
        name="upward",
    )(r, basis, transfer)


def coupling_kernel(levels, cols, tile, place_ref, upper_ref, row_ref, col_ref, b_ref, g_ref):
    place = place_ref[0]
    down = None
    for level in range(levels):
        span = 2**level
        extent = (1, span) if span <= cols else (span // cols, cols)
        half = (0.5 * tile[0] * extent[0], 0.5 * tile[1] * extent[1], 0.5)
        apart = (0.0, 2.0 * span * tile[1]) if 2 * span < cols else (2.0 * span / cols * tile[0], 0.0)

        def matrix(sign):
            squared = jnp.zeros((64, 64), F32)
            for c in range(3):
                step = half[c] * (col_ref[:, c : c + 1] - row_ref[c : c + 1, :])
                if c < 2:
                    step = step + sign * apart[c]
                squared = squared + step * step
            squared = jnp.maximum(squared, 1e-30)
            scaled = FAR_RATE * (squared * lax.rsqrt(squared))
            return COUPLING_SCALE * ((1.0 + scaled) * jnp.exp(-scaled))

        b_ref[level] = matrix(-1.0)
        upper = (place // (2 * span)) % 2
        own = matrix(jnp.where(upper == 1, -1.0, 1.0))
        g_ref[level] = own if down is None else dot3(own, down)
        if level + 1 < levels:
            bit = (place // span) % 2
            step_down = upper_ref[bit]
            down = step_down if down is None else dot3(step_down, down)


def couplings(levels, cols, tile, place, upper, nodes):
    out = jax.ShapeDtypeStruct((levels, 64, 64), F32)
    return pl.pallas_call(
        functools.partial(coupling_kernel, levels, cols, tile),
        out_shape=[out, out],
        in_specs=[SM, VM, VM, VM],
        out_specs=[VM, VM],
        name="couplings",
    )(place, upper, nodes, nodes.T)


def tree(levels, place, c, upper_t, g_ref, b_ref, scratch, energy):
    own = jnp.zeros((8, 64), F32)
    pair_sums = [jnp.zeros((8, 64), F32) for _ in range(4)]
    for level in range(levels):
        count = c.shape[0]
        scratch[0:count] = c
        partner = (place // 2**level) ^ 2
        own = own + dot3(scratch[partner], g_ref[level])
        paired = c.reshape(count // 2, 2, 8, 64)
        if energy:
            quads = c.reshape(count // 4, 4, 8, 64)
            low = quads[:, 0:2].reshape(count // 2 * 8, 64)
            high = quads[:, 2:4].reshape(count // 2, 8, 64)
            carried = dot3(low, b_ref[level]).reshape(count // 2, 8, 64)
            for s in range(4):
                pair_sums[s] = pair_sums[s] + jnp.sum(carried * high[:, s : s + 1, :], axis=0)
        if level + 1 < levels:
            c = (
                dot3(paired[:, 0].reshape(count // 2 * 8, 64), upper_t[0])
                + dot3(paired[:, 1].reshape(count // 2 * 8, 64), upper_t[1])
            ).reshape(count // 2, 8, 64)
    return own[0:4], pair_sums


def middle_kernel(
    levels, place_ref, count_ref, c_ref, upper_ref, g_ref, high_ref, low_ref, r_ref, n_ref, e_ref, out_ref, scratch
):
    leaves, _, size = r_ref.shape
    own, _ = tree(levels, place_ref[0], c_ref[...], upper_ref, g_ref, None, scratch, False)
    y = rows16(own)
    lane = lax.broadcasted_iota(jnp.int32, (4, size), 1)

    def body(a, carry):
        c_total, m_total = carry
        high = high_ref[a]
        low = low_ref[a]
        far = join16(dot(y, high) + dot(y, low))
        e = jnp.where(lane < count_ref[a], n_ref[a] + far, 0.0)
        e_ref[a] = e
        e16 = rows16(e)
        both = jnp.concatenate([rows16(r_ref[a]), e16], axis=0)
        return c_total + (dot_nt(e16, high) + dot_nt(e16, low)), m_total + dot_nt(both, both)

    c_total, m_total = lax.fori_loop(
        0, leaves, body, (jnp.zeros((16, 64), F32), jnp.zeros((32, 32), F32)), unroll=4
    )

    def block(i, j):
        part = m_total[16 * i : 16 * i + 16, 16 * j : 16 * j + 16]
        part = join16(part)
        return part[:, 0:4] + part[:, 4:8] + part[:, 8:12]

    moments = jnp.concatenate([block(0, 0), block(0, 1), block(1, 1), jnp.zeros((4, 52), F32)], axis=1)
    out_ref[...] = jnp.concatenate([join16(c_total), moments], axis=0)


def middle(levels, place, counts, c, upper_t, g, high, low, r, n):
    return pl.pallas_call(
        functools.partial(middle_kernel, levels),
        out_shape=[jax.ShapeDtypeStruct(r.shape, F32), jax.ShapeDtypeStruct((8, 64), F32)],
        in_specs=[SM, SM] + [VM] * 7,
        out_specs=[VM] * 2,
        scratch_shapes=[pltpu.VMEM(c.shape, F32)],
        compiler_params=pltpu.CompilerParams(vmem_limit_bytes=VMEM_LIMIT),
        name="middle",
    )(place, counts, c, upper_t, g, high, low, r, n)


def energy_kernel(e_ref, n_ref, c_ref, out_ref):
    leaves = e_ref.shape[0]
    sums = []
    for s in range(4):
        total = jnp.zeros(e_ref.shape[1:], F32)
        for a in range(leaves):
            total = total + e_ref[a] * n_ref[a, s : s + 1, :]
        sums.append(jnp.sum(total, axis=1, keepdims=True))
    block = jnp.concatenate([jnp.zeros((4, 12), F32)] + sums + [jnp.zeros((4, 48), F32)], axis=1)
    out_ref[...] = c_ref[...] + jnp.concatenate([jnp.zeros((4, 64), F32), block], axis=0)


def energy(e, n, c):
    return pl.pallas_call(
        energy_kernel,
        out_shape=jax.ShapeDtypeStruct((8, 64), F32),
        in_specs=[VM] * 3,
        out_specs=VM,
        name="energy",
    )(e, n, c)


def mat_mul(a, b):
    return [[sum(a[i][k] * b[k][j] for k in range(4)) for j in range(4)] for i in range(4)]


def mat_add(a, b):
    return [[a[i][j] + b[i][j] for j in range(4)] for i in range(4)]


def mat_sub(a, b):
    return [[a[i][j] - b[i][j] for j in range(4)] for i in range(4)]


def mat_t(a):
    return [[a[j][i] for j in range(4)] for i in range(4)]


def mat_solve(a, b):
    a = [list(row) for row in a]
    b = [list(row) for row in b]
    width = len(b[0])
    inverse = []
    for col in range(4):
        inverse.append(1.0 / a[col][col])
        for row in range(col + 1, 4):
            factor = a[row][col] * inverse[col]
            for k in range(col + 1, 4):
                a[row][k] = a[row][k] - factor * a[col][k]
            for k in range(width):
                b[row][k] = b[row][k] - factor * b[col][k]
    result = [None] * 4
    for col in reversed(range(4)):
        row = list(b[col])
        for later in range(col + 1, 4):
            row = [row[k] - a[col][later] * result[later][k] for k in range(width)]
        result[col] = [value * inverse[col] for value in row]
    return result


def weights(gram, cross, square, cubic):
    curvature = mat_add(gram, cross)
    both = mat_solve(curvature, [gram[i] + cross[i] for i in range(4)])
    step = [row[0:4] for row in both]
    rest = [row[4:8] for row in both]
    mixed = mat_mul(mat_t(rest), mat_mul(cross, step))
    gram_next = mat_sub(
        mat_add(mat_mul(mat_t(rest), mat_mul(gram, rest)), mat_mul(mat_t(step), mat_mul(square, step))),
        mat_add(mixed, mat_t(mixed)),
    )
    mix = mat_solve(gram, gram_next)
    lead = mat_add(rest, mix)
    second = mat_sub(lead, step)
    with_r = mat_sub(mat_add(mat_mul(gram, lead), mat_mul(cross, second)), mat_mul(square, step))
    with_e = mat_sub(mat_add(mat_mul(mat_t(cross), lead), mat_mul(square, second)), mat_mul(cubic, step))
    curvature_next = mat_sub(mat_mul(mat_t(lead), with_r), mat_mul(mat_t(step), with_e))
    step_next = mat_solve(curvature_next, gram_next)
    lead_step = mat_mul(lead, step_next)
    step_step = mat_mul(step, step_next)
    second_step = mat_sub(lead_step, step_step)
    solution = (mat_add(step, lead_step), [[-v for v in row] for row in step_step], None)
    residual = (mat_sub(rest, lead_step), [[-(step[i][j] + second_step[i][j]) for j in range(4)] for i in range(4)], step_step)
    return solution, residual


def final_kernel(
    levels, place_ref, count_ref, c_ref, upper_ref, g_ref, b_ref, high_ref, low_ref, r_ref, e_ref, n_ref,
    x_ref, out_ref, scratch,
):
    leaves, _, size = r_ref.shape
    c = c_ref[...]
    own, pair_sums = tree(levels, place_ref[0], c, upper_ref, g_ref, b_ref, scratch, True)
    y = rows16(own)
    moments = jnp.sum(c, axis=0)[4:8]

    def splat(x):
        return jnp.broadcast_to(x, (1, 128))

    def matrix(at):
        return [[splat(moments[i : i + 1, at + j : at + j + 1]) for j in range(4)] for i in range(4)]

    half = [[splat(jnp.sum(pair_sums[j], axis=1, keepdims=True)[i : i + 1]) for j in range(4)] for i in range(4)]
    cubic = mat_add(matrix(12), mat_add(half, mat_t(half)))
    solution, residual = weights(matrix(0), matrix(4), matrix(8), cubic)
    row = lax.broadcasted_iota(jnp.int32, (8, 128), 0)
    col = lax.broadcasted_iota(jnp.int32, (8, 128), 1)
    table = jnp.zeros((8, 128), F32)
    for first, parts in ((0, solution), (4, residual)):
        for k, part in enumerate(parts):
            if part is None:
                continue
            for i in range(4):
                line = jnp.zeros((8, 128), F32)
                for j in range(4):
                    line = jnp.where(row == first + j, part[i][j], line)
                table = jnp.where(col == 4 * k + i, line + table, table)
    table = table[:, 0:16]
    lane = lax.broadcasted_iota(jnp.int32, (4, size), 1)

    def body(a, carry):
        far = join16(dot(y, high_ref[a]) + dot(y, low_ref[a]))
        f = jnp.where(lane < count_ref[a], n_ref[a] + far, 0.0)
        stacked = jnp.concatenate([r_ref[a], e_ref[a], f, jnp.zeros_like(f)], axis=0)
        both = jnp.dot(table, stacked, precision=lax.Precision.HIGHEST, preferred_element_type=F32)
        x_ref[a] = both[0:4]
        out_ref[a] = both[4:8]
        return carry

    lax.fori_loop(0, leaves, body, 0, unroll=4)


def final(levels, place, counts, c, upper_t, g, b, high, low, r, e, n):
    out = jax.ShapeDtypeStruct(r.shape, F32)
    return pl.pallas_call(
        functools.partial(final_kernel, levels),
        out_shape=[out, out],
        in_specs=[SM, SM] + [VM] * 9,
        out_specs=[VM] * 2,
        scratch_shapes=[pltpu.VMEM(c.shape, F32)],
        compiler_params=pltpu.CompilerParams(vmem_limit_bytes=VMEM_LIMIT),
        name="final",
    )(place, counts, c, upper_t, g, b, high, low, r, e, n)


def with_halo(x):
    for axis, dim in (("gx", 0), ("gy", 1)):
        count, length = lax.axis_size(axis), x.shape[dim]
        up = [(i, i + 1) for i in range(count - 1)]
        down = [(j, i) for i, j in up]
        before = lax.ppermute(lax.slice_in_dim(x, length - 1, length, axis=dim), axis, up)
        after = lax.ppermute(lax.slice_in_dim(x, 0, 1, axis=dim), axis, down)
        x = jnp.concatenate([before, x, after], axis=dim)
    return x


def from_all(x):
    for axis in ("gy", "gx"):
        count = lax.axis_size(axis)
        x = lax.all_to_all(jnp.broadcast_to(x[None], (count,) + x.shape), axis, 0, 0, tiled=True)
    return x.reshape((-1,) + x.shape[2:])


def on_device(points, right_sides, leaf_counts, near_mask, leaf_basis, leaf_transfer, upper_transfer, proxy_nodes):
    nx, ny, _, size = points.shape
    leaves = nx * ny
    cols = lax.axis_size("gy")
    devices = lax.axis_size("gx") * cols
    levels = devices.bit_length() - 2
    gx, gy = lax.axis_index("gx"), lax.axis_index("gy")
    place = (gx * cols + gy).astype(jnp.int32).reshape(1)
    target_table, source_table, factor = feature_tables()
    factor = jnp.asarray(np.broadcast_to(factor[:, :, None], (9, 32, size)), BF)

    valid = jnp.arange(size, dtype=jnp.int32) < leaf_counts[:, :, None, None]
    r = jnp.where(valid, right_sides, 0.0)
    corner = jnp.stack(
        [
            jnp.broadcast_to((gx * nx + jnp.arange(nx))[:, None], (nx, ny)).astype(F32) + 0.5,
            jnp.broadcast_to((gy * ny + jnp.arange(ny))[None, :], (nx, ny)).astype(F32) + 0.5,
            jnp.full((nx, ny), 0.5, F32),
        ],
        axis=2,
    )
    packed = jnp.concatenate([points - corner[..., None], jnp.zeros((nx, ny, 1, size), F32), r], axis=2)
    extended = with_halo(packed)
    leaves_out = (nx + 2) * (ny + 2)
    s, t = geometry(extended.reshape(leaves_out, 8, size), target_table, source_table)
    flat_r = r.reshape(leaves, 4, size)
    counts = leaf_counts.reshape(leaves)
    mask = near_mask.reshape(leaves * 9)
    high, low, c = upward(
        flat_r, leaf_basis.reshape((leaves,) + leaf_basis.shape[2:]), leaf_transfer.reshape((leaves,) + leaf_transfer.shape[2:])
    )
    upper_t = jnp.swapaxes(upper_transfer, 1, 2)
    b, g = couplings(levels, cols, (nx, ny), place, upper_transfer, proxy_nodes)
    everyone = from_all(c)
    n = near_field(nx, ny, mask, extended[:, :, 4:8].reshape(leaves_out, 4, size), s, t, factor)
    e, c = middle(levels, place, counts, everyone, upper_t, g, high, low, flat_r, n)
    extended_e = with_halo(e.reshape(nx, ny, 4, size)).reshape(leaves_out, 4, size)
    n = near_field(nx, ny, mask, extended_e, s, t, factor)
    everyone = from_all(energy(e, n, c))
    x, out = final(levels, place, counts, everyone, upper_t, g, b, high, low, flat_r, e, n)
    shape = (nx, ny, 4, size)
    return x.reshape(shape), out.reshape(shape)


def solution(mesh):
    return jax.shard_map(
        on_device,
        mesh=mesh,
        in_specs=(
            P("gx", "gy", None, None),
            P("gx", "gy", None, None),
            P("gx", "gy"),
            P("gx", "gy", None),
            P("gx", "gy", None, None),
            P("gx", "gy", None, None),
            P(),
            P(),
        ),
        out_specs=(P("gx", "gy", None, None), P("gx", "gy", None, None)),
        check_vma=False,
    )
```

time: 744 us -> 215 us (0.29); the launches traced: 733 us -> 216 us
  matrix products: 300 us -> 0 us
  blocking collectives: 229 us -> 41.5 us
  Pallas kernels: 0 us -> 77 us
  starting transfers between devices: 105 us -> 39 us
  between operations: 26.9 us -> 1.1 us
  other arithmetic: 29.5 us -> 9.86 us
  local copies, waits for them, and re-layouts: 19.7 us -> 27.3 us
    dot_general x73 -> x0, matrix products: 300 us -> none  [the longest x18 261 us: on_device(): jnp.einsum('abpq,abrq->abrp', kernel_tile, values, precision=PRECISE)]
    psum x3 -> x0, blocking collectives: 229 us -> none  [gram_of(): return lax.psum(local_sum, ('gx', 'gy'))]
    ppermute x38 -> x8, starting transfers between devices: 105 us -> 22.2 us  [the longest x4 15.3 us: with_halo(): lax.ppermute(lax.slice_in_dim(x, length - 1, length, axis=dim), axis, up)]
    pallas_call x0 -> x8, Pallas kernels: none -> 77 us  [the longest x2 44.7 us: near_field(): pl.pallas_call(functools.partial(near_kernel, nx, ny), out_shape=jax.Shap...]
    all_to_all x0 -> x2, blocking collectives: none -> 41.5 us  [from_all(): lax.all_to_all(jnp.broadcast_to(x[None], (count,) + x.shape), axis, 0, 0,...]
    unnamed x255 -> x64, local copies, waits for them, and re-layouts: 1.54 us -> 23.6 us
    div x3 -> x0, other arithmetic: 18.8 us -> none  [solve_small(): result[column] = partial_sum / row_list[column][column]]
    all_to_all x0 -> x2, starting transfers between devices: none -> 16.8 us  [from_all(): lax.all_to_all(jnp.broadcast_to(x[None], (count,) + x.shape), axis, 0, 0,...]
  transfers between devices with their start and end apart: 38 -> 10, of which waited for: 18 -> 5; matrix products, arithmetic and copies ran while one was open for 21% -> 1% of each run, Pallas kernels for 0% -> 14%
where the time goes in v1:
time: 215 us; the launch traced here: 216 us
  Pallas kernels  77 us (36%)
  blocking collectives  41.5 us (19%)
  starting transfers between devices  39 us (18%)
  local copies, waits for them, and re-layouts  27.3 us (13%)
  waiting for transfers between devices  20.5 us (10%)
  other arithmetic  9.86 us (5%)
    pallas_call x2, Pallas kernels, near_field(): pl.pallas_call(functools.partial(near_kernel, nx, ny), out_shape=jax.Shap...  44.7 us
    all_to_all x2, blocking collectives, from_all(): lax.all_to_all(jnp.broadcast_to(x[None], (count,) + x.shape), axis, 0, 0,...  41.5 us
    unnamed x64, local copies, waits for them, and re-layouts  23.6 us
    all_to_all x2, starting transfers between devices, from_all(): lax.all_to_all(jnp.broadcast_to(x[None], (count,) + x.shape), axis, 0, 0,...  16.8 us
    ppermute x4, starting transfers between devices, with_halo(): lax.ppermute(lax.slice_in_dim(x, length - 1, length, axis=dim), axis, up)  15.3 us
    ppermute x4, waiting for transfers between devices, with_halo(): after = lax.ppermute(lax.slice_in_dim(x, 0, 1, axis=dim), axis, down)  11.4 us
    pallas_call x1, Pallas kernels, final(): pl.pallas_call(functools.partial(final_kernel, levels), out_shape=[out, o...  9.75 us
    pallas_call x1, Pallas kernels, middle(): pl.pallas_call(functools.partial(middle_kernel, levels), out_shape=[jax.S...  9.18 us
  transfers between devices with their start and end apart: 10, of which 5 were waited for; matrix products, arithmetic and copies ran while one was open for 1% of the time, Pallas kernels for 14%

profile of v1, /device:TPU:1, one launch (start us, length us, event | category | flops | bytes accessed | tf_op | source)
XLA Modules:
  0.0 216.4 jit_solution(10485131193367433454)
XLA Ops:
  0.6 0.8 iota_compare_fusion
  1.4 0.9 broadcast_select_fusion
  2.4 1.6 copy-done.6
  4.0 1.2 copy-done.9
  5.2 4.6 %upward.1 = (bf16[32,64,256]{2,1,0:T(8,128)(2,1)S(1)}, bf16[32,64,256]{2,1,0:T(8,128)(2,1)S(1)}, f32[8,64]{1,0:T(8,128)S(1)}) custom-call(f32[32,4,256]{2,1,0:T(4,128)S(1)} %bitcast.19, f32[32,64,256]{2,1,0:T(8,128)S(1)} %bitcast.27, f32[32,64,64]{2,1,0:T(8,128)S(1)} %bitcast.28), custom_call_target="tpu_custom_call" | custom-call | tf_op jit(solution)/shard_map/upward/pallas_call | solution.py:222
  9.9 0.7 reshape.93
  10.6 10.0 %all-to-all-start = ((f32[16,1,512]{2,1,0:T(1,128)}), f32[16,1,512]{2,1,0:T(1,128)S(1)}, u32[]{:S(2)}, u32[]{:S(2)}) async-start(f32[16,1,512]{2,1,0:T(1,128)} %reshape.93), calls=%async_computation | async-start | bytes 65536 | tf_op jit(solution)/shard_map/all_to_all | solution.py:499
  20.9 7.0 %all-to-all-done = f32[16,1,512]{2,1,0:T(1,128)S(1)} async-done(((f32[16,1,512]{2,1,0:T(1,128)}), f32[16,1,512]{2,1,0:T(1,128)S(1)}, u32[]{:S(2)}, u32[]{:S(2)}) %all-to-all-start) | async-done | bytes 32800 | tf_op jit(solution)/shard_map/all_to_all | solution.py:499
  29.2 1.1 broadcast_in_dim.29
  30.3 2.7 %reshape.95 = f32[16,1,8192]{2,1,0:T(1,128)} reshape(f32[16,16,8,64]{3,2,1,0:T(8,128)} %broadcast_in_dim.29) | data formatting | bytes 1048576
  33.0 6.8 %all-to-all-start.1 = ((f32[16,1,8192]{2,1,0:T(1,128)}), f32[16,1,8192]{2,1,0:T(1,128)}, u32[]{:S(2)}, u32[]{:S(2)}) async-start(f32[16,1,8192]{2,1,0:T(1,128)} %reshape.95), calls=%async_computation.1 | async-start | bytes 1048576 | tf_op jit(solution)/shard_map/all_to_all | solution.py:499
  40.0 3.2 %collective-permute-start = (f32[1,8,8,256]{3,2,1,0:T(8,128)S(1)}, f32[1,8,8,256]{3,2,1,0:T(8,128)S(1)}, u32[]{:S(2)}, u32[]{:S(2)}) collective-permute-start(f32[1,8,8,256]{3,2,1,0:T(8,128)S(1)} %get-tuple-element.26), channel_id=1, source_target_pairs={{0,16},{16,32},{32,48},{48,64},{64,80},{80,96},{96,112},{112,128},... | collective-permute-start | bytes 196616 | tf_op jit(solution)/shard_map/ppermute | solution.py:490
  43.2 1.3 collective-permute-start.1
  44.5 2.0 collective-permute-done
  46.5 2.5 %collective-permute-done.1 = f32[1,8,8,256]{3,2,1,0:T(8,128)S(1)} collective-permute-done((f32[1,8,8,256]{3,2,1,0:T(8,128)S(1)}, f32[1,8,8,256]{3,2,1,0:T(8,128)S(1)}, u32[]{:S(2)}, u32[]{:S(2)}) %collective-permute-start.1) | collective-permute-done | bytes 65568 | tf_op jit(solution)/shard_map/ppermute | solution.py:491
  49.0 3.6 %collective-permute-start.2 = (f32[6,1,8,256]{3,2,1,0:T(8,128)S(1)}, f32[6,1,8,256]{3,2,1,0:T(8,128)S(1)}, u32[]{:S(2)}, u32[]{:S(2)}) collective-permute-start(f32[6,1,8,256]{3,2,1,0:T(8,128)S(1)} %get-tuple-element.24), channel_id=1, source_target_pairs={{0,1},{1,2},{2,3},{3,4},{4,5},{5,6},{6,7},{7,8},{8,9},{9,10},{10,1... | collective-permute-start | bytes 147464 | tf_op jit(solution)/shard_map/ppermute | solution.py:490
  52.7 1.9 collective-permute-start.3
  55.6 2.6 %couplings.1 = (f32[7,64,64]{2,1,0:T(8,128)}, f32[7,64,64]{2,1,0:T(8,128)}) custom-call(s32[1]{0:T(128)} %bitcast.place_ref, f32[2,64,64]{2,1,0:T(8,128)} %upper_ref.1, f32[3,64]{1,0:T(4,128)} %row_ref.1, f32[64,3]{1,0:T(8,128)} %bitcast.33), custom_call_target="tpu_custom_call" | custom-call | tf_op jit(solution)/shard_map/couplings/pallas_call | solution.py:264
  58.5 4.4 %geometry.1 = (bf16[60,256,32]{2,1,0:T(8,128)(2,1)S(1)}, bf16[60,32,256]{2,1,0:T(8,128)(2,1)S(1)}) custom-call(f32[60,8,256]{2,1,0:T(8,128)S(1)} %bitcast.24, bf16[32,24]{1,0:T(8,128)(2,1)S(1)} %copy-done.19, bf16[32,24]{1,0:T(8,128)(2,1)S(1)} %copy-done.20), custom_call_target="tpu_custom_call" | custom-call | tf_op jit(solution)/shard_map/geometry/pallas_call | solution.py:113
  62.9 1.1 copy-done.14
  64.0 22.4 %near.2.n_ref = f32[32,4,256]{2,1,0:T(4,128)S(1)} custom-call(s32[288]{0:T(512)S(1)} %reshape.84.mask_ref, f32[60,4,256]{2,1,0:T(4,128)S(1)} %bitcast.30, bf16[60,256,32]{2,1,0:T(8,128)(2,1)S(1)} %get-tuple-element.17.s_ref, bf16[60,32,256]{2,1,0:T(8,128)(2,1)S(1)} %get-tuple-element.18.t_ref, bf16[9,32,256]{2,1,0:T(8,128)(2,1)S(1)} %copy-done.14), custom_call_target="tpu_custom_call" | custom-call | tf_op jit(solution)/shard_map/near/pallas_call | solution.py:186
  86.4 1.9 copy-done
  88.9 3.7 %reduce.1 = f32[16,8192]{1,0:T(8,128)} reduce(f32[16,1,8192]{2,1,0:T(1,128)} %all-to-all-done.1, f32[]{:T(128)} %broadcast.50), dimensions={1}, to_apply=%all_to_all.13.reduce_sub_computation | reduce | bytes 1048580 | tf_op jit(solution)/shard_map/all_to_all | solution.py:499
  92.6 1.5 reshape.96
  94.1 1.1 copy-done.10
  95.2 1.1 copy-done.17
  96.2 9.2 %middle.1 = (f32[32,4,256]{2,1,0:T(4,128)S(1)}, f32[8,64]{1,0:T(8,128)S(1)}) custom-call(s32[1]{0:T(128)} %bitcast.place_ref, s32[32]{0:T(128)S(1)} %reshape.79.count_ref, f32[256,8,64]{2,1,0:T(8,128)S(1)} %bitcast.23, f32[2,64,64]{2,1,0:T(8,128)S(1)} %bitcast.31, f32[7,64,64]{2,1,0:T(8,128)S(1)} %copy-done.10, ...), custom_call_target="tpu_custom_call" | custom-call | tf_op jit(solution)/shard_map/middle/pallas_call | solution.py:330
  105.5 6.6 %collective-permute-start.4 = (f32[1,8,4,256]{3,2,1,0:T(4,128)S(1)}, f32[1,8,4,256]{3,2,1,0:T(4,128)S(1)}, u32[]{:S(2)}, u32[]{:S(2)}) collective-permute-start(f32[1,8,4,256]{3,2,1,0:T(4,128)S(1)} %get-tuple-element.30), channel_id=1, source_target_pairs={{0,16},{16,32},{32,48},{48,64},{64,80},{80,96},{96,112},{112,128},... | collective-permute-start | bytes 98312 | tf_op jit(solution)/shard_map/ppermute | solution.py:490
  112.0 1.3 collective-permute-start.5
  113.3 6.2 %collective-permute-done.5 = f32[1,8,4,256]{3,2,1,0:T(4,128)S(1)} collective-permute-done((f32[1,8,4,256]{3,2,1,0:T(4,128)S(1)}, f32[1,8,4,256]{3,2,1,0:T(4,128)S(1)}, u32[]{:S(2)}, u32[]{:S(2)}) %collective-permute-start.5) | collective-permute-done | bytes 32800 | tf_op jit(solution)/shard_map/ppermute | solution.py:491
  119.6 1.9 collective-permute-start.6
  121.5 2.4 %collective-permute-start.7 = (f32[6,1,4,256]{3,2,1,0:T(4,128)S(1)}, f32[6,1,4,256]{3,2,1,0:T(4,128)S(1)}, u32[]{:S(2)}, u32[]{:S(2)}) collective-permute-start(f32[6,1,4,256]{3,2,1,0:T(4,128)S(1)} %get-tuple-element.29), channel_id=1, source_target_pairs={{1,0},{2,1},{3,2},{4,3},{5,4},{6,5},{7,6},{8,7},{9,8},{10,9},{11,1... | collective-permute-start | bytes 73736 | tf_op jit(solution)/shard_map/ppermute | solution.py:491
  123.9 2.7 %collective-permute-done.7 = f32[6,1,4,256]{3,2,1,0:T(4,128)S(1)} collective-permute-done((f32[6,1,4,256]{3,2,1,0:T(4,128)S(1)}, f32[6,1,4,256]{3,2,1,0:T(4,128)S(1)}, u32[]{:S(2)}, u32[]{:S(2)}) %collective-permute-start.7) | collective-permute-done | bytes 24608 | tf_op jit(solution)/shard_map/ppermute | solution.py:491
  126.7 1.2 copy-done.3
  127.9 0.9 copy-done.15
  128.8 22.4 %near.3.n_ref = f32[32,4,256]{2,1,0:T(4,128)S(1)} custom-call(s32[288]{0:T(512)S(1)} %reshape.84.mask_ref, f32[60,4,256]{2,1,0:T(4,128)S(1)} %bitcast.29, bf16[60,256,32]{2,1,0:T(8,128)(2,1)S(1)} %copy-done.1, bf16[60,32,256]{2,1,0:T(8,128)(2,1)S(1)} %copy-done.3, bf16[9,32,256]{2,1,0:T(8,128)(2,1)S(1)} %copy-done.15), custom_call_target="tpu_custom_call" | custom-call | tf_op jit(solution)/shard_map/near/pallas_call | solution.py:186
  151.9 1.8 energy.1
  153.6 0.7 broadcast_in_dim.33
  154.4 13.2 %all_to_all.20 = f32[16,1,512]{2,1,0:T(1,128)S(1)} all-to-all(f32[16,1,512]{2,1,0:T(1,128)S(1)} %reshape.97), channel_id=1, replica_groups=mesh['gx'=16,'gy'=16] {'gy'}, dimensions={0} | all-to-all | bytes 65536 | tf_op jit(solution)/shard_map/all_to_all | solution.py:499
  169.0 0.9 broadcast_in_dim.34
  169.9 1.5 reshape.99
  171.3 28.4 %all_to_all.21 = f32[16,1,8192]{2,1,0:T(1,128)S(1)} all-to-all(f32[16,1,8192]{2,1,0:T(1,128)} %reshape.99), channel_id=1, replica_groups=mesh['gx'=16,'gy'=16] {'gx'}, dimensions={0} | all-to-all | bytes 1048576 | tf_op jit(solution)/shard_map/all_to_all | solution.py:499
  199.7 2.7 %reduce.3 = f32[16,8192]{1,0:T(8,128)} reduce(f32[16,1,8192]{2,1,0:T(1,128)S(1)} %all_to_all.21, f32[]{:T(128)} %broadcast.50), dimensions={1}, to_apply=%all_to_all.15.reduce_sub_computation | reduce | bytes 1048580 | tf_op jit(solution)/shard_map/all_to_all | solution.py:499
  202.4 1.5 reshape.100
  203.9 0.9 copy-done.11
  204.8 0.8 copy-done.13
  205.7 0.9 copy-done.18
  206.6 9.8 %final.1 = (f32[32,4,256]{2,1,0:T(4,128)}, f32[32,4,256]{2,1,0:T(4,128)}) custom-call(s32[1]{0:T(128)} %bitcast.place_ref, s32[32]{0:T(128)S(1)} %reshape.79.count_ref, f32[256,8,64]{2,1,0:T(8,128)S(1)} %bitcast.22, f32[2,64,64]{2,1,0:T(8,128)S(1)} %bitcast.32, f32[7,64,64]{2,1,0:T(8,128)S(1)} %copy-done.11, f32[7,64,64]{2,1,0:T(8,128)S(1)} %copy-done.18, ...), custom_call_target="tpu_custom_call" | custom-call | tf_op jit(solution)/shard_map/final/pallas_call | solution.py:474
  (75 shorter events, 5.9 us)
Async XLA Ops:
  0.6 39.2 %copy-start.23 = (f32[4,8,3,256]{3,1,2,0:T(8,128)S(1)}, f32[4,8,3,256]{3,1,2,0:T(8,128)}, u32[]{:S(2)}) copy-start(f32[4,8,3,256]{3,1,2,0:T(8,128)} %param.11) | copy-start | bytes 294916
  2.4 1.6 copy-start.6
  4.0 1.2 copy-start.9
  5.2 49.4 %copy-start.25 = (s32[4,8]{1,0:T(4,128)S(1)}, s32[4,8]{1,0:T(4,128)}, u32[]{:S(2)}) copy-start(s32[4,8]{1,0:T(4,128)} %param.13) | copy-start | bytes 388
  5.2 49.6 %copy-start.26 = (f32[3,64]{1,0:T(4,128)S(1)}, f32[3,64]{1,0:T(4,128)}, u32[]{:S(2)}) copy-start(f32[3,64]{1,0:T(4,128)} %row_ref.1) | copy-start | bytes 2308
  9.8 44.9 %copy-start.24 = (s32[4,8,9]{2,1,0:T(8,128)S(1)}, s32[4,8,9]{2,1,0:T(8,128)}, u32[]{:S(2)}) copy-start(s32[4,8,9]{2,1,0:T(8,128)} %param.14) | copy-start | bytes 3460
  9.8 45.8 %copy-start.22 = (f32[2,64,64]{2,1,0:T(8,128)S(1)}, f32[2,64,64]{2,1,0:T(8,128)}, u32[]{:S(2)}) copy-start(f32[2,64,64]{2,1,0:T(8,128)} %upper_ref.1) | copy-start | bytes 98308
  9.8 48.6 %copy-start.19 = (bf16[32,24]{1,0:T(8,128)(2,1)S(1)}, bf16[32,24]{1,0:T(8,128)(2,1)}, u32[]{:S(2)}) copy-start(bf16[32,24]{1,0:T(8,128)(2,1)} %constant.26.clone.target_ref) | copy-start | bytes 4612
  9.8 48.6 %copy-start.20 = (bf16[32,24]{1,0:T(8,128)(2,1)S(1)}, bf16[32,24]{1,0:T(8,128)(2,1)}, u32[]{:S(2)}) copy-start(bf16[32,24]{1,0:T(8,128)(2,1)} %constant.27.clone.source_ref) | copy-start | bytes 4612
  10.6 17.4 %all-to-all-start = ((f32[16,1,512]{2,1,0:T(1,128)}), f32[16,1,512]{2,1,0:T(1,128)S(1)}, u32[]{:S(2)}, u32[]{:S(2)}) async-start(f32[16,1,512]{2,1,0:T(1,128)} %reshape.93), calls=%async_computation | async-start | bytes 65536 | tf_op jit(solution)/shard_map/all_to_all | solution.py:499
  33.0 55.9 %all-to-all-start.1 = ((f32[16,1,8192]{2,1,0:T(1,128)}), f32[16,1,8192]{2,1,0:T(1,128)}, u32[]{:S(2)}, u32[]{:S(2)}) async-start(f32[16,1,8192]{2,1,0:T(1,128)} %reshape.95), calls=%async_computation.1 | async-start | bytes 1048576 | tf_op jit(solution)/shard_map/all_to_all | solution.py:499
  40.0 6.6 %collective-permute-start = (f32[1,8,8,256]{3,2,1,0:T(8,128)S(1)}, f32[1,8,8,256]{3,2,1,0:T(8,128)S(1)}, u32[]{:S(2)}, u32[]{:S(2)}) collective-permute-start(f32[1,8,8,256]{3,2,1,0:T(8,128)S(1)} %get-tuple-element.26), channel_id=1, source_target_pairs={{0,16},{16,32},{32,48},{48,64},{64,80},{80,96},{96,112},{112,128},... | collective-permute-start | bytes 196616 | tf_op jit(solution)/shard_map/ppermute | solution.py:490
  43.2 5.8 %collective-permute-start.1 = (f32[1,8,8,256]{3,2,1,0:T(8,128)S(1)}, f32[1,8,8,256]{3,2,1,0:T(8,128)S(1)}, u32[]{:S(2)}, u32[]{:S(2)}) collective-permute-start(f32[1,8,8,256]{3,2,1,0:T(8,128)S(1)} %get-tuple-element.27), channel_id=1, source_target_pairs={{16,0},{32,16},{48,32},{64,48},{80,64},{96,80},{112,96},{128,112},... | collective-permute-start | bytes 196616 | tf_op jit(solution)/shard_map/ppermute | solution.py:491
  49.0 9.2 %collective-permute-start.2 = (f32[6,1,8,256]{3,2,1,0:T(8,128)S(1)}, f32[6,1,8,256]{3,2,1,0:T(8,128)S(1)}, u32[]{:S(2)}, u32[]{:S(2)}) collective-permute-start(f32[6,1,8,256]{3,2,1,0:T(8,128)S(1)} %get-tuple-element.24), channel_id=1, source_target_pairs={{0,1},{1,2},{2,3},{3,4},{4,5},{5,6},{6,7},{7,8},{8,9},{9,10},{10,1... | collective-permute-start | bytes 147464 | tf_op jit(solution)/shard_map/ppermute | solution.py:490
  52.7 5.6 %collective-permute-start.3 = (f32[6,1,8,256]{3,2,1,0:T(8,128)S(1)}, f32[6,1,8,256]{3,2,1,0:T(8,128)S(1)}, u32[]{:S(2)}, u32[]{:S(2)}) collective-permute-start(f32[6,1,8,256]{3,2,1,0:T(8,128)S(1)} %get-tuple-element.25), channel_id=1, source_target_pairs={{1,0},{2,1},{3,2},{4,3},{5,4},{6,5},{7,6},{8,7},{9,8},{10,9},{11,1... | collective-permute-start | bytes 147464 | tf_op jit(solution)/shard_map/ppermute | solution.py:491
  55.6 38.4 %copy-start.12 = (f32[2,64,64]{1,2,0:T(8,128)}, f32[2,64,64]{1,2,0:T(8,128)S(1)}, u32[]{:S(2)}) copy-start(f32[2,64,64]{1,2,0:T(8,128)S(1)} %copy.16) | copy-start | bytes 98308
  62.9 26.0 %copy-start.2 = (bf16[60,32,256]{2,1,0:T(8,128)(2,1)}, bf16[60,32,256]{2,1,0:T(8,128)(2,1)S(1)}, u32[]{:S(2)}) copy-start(bf16[60,32,256]{2,1,0:T(8,128)(2,1)S(1)} %get-tuple-element.18.t_ref) | copy-start | bytes 2949124
  62.9 1.1 copy-start.14
  86.4 1.9 copy-start
  88.2 0.7 copy-start.16
  94.0 32.6 %copy-start.1 = (bf16[60,256,32]{2,1,0:T(8,128)(2,1)S(1)}, bf16[60,256,32]{2,1,0:T(8,128)(2,1)}, u32[]{:S(2)}) copy-start(bf16[60,256,32]{2,1,0:T(8,128)(2,1)} %copy-done) | copy-start | bytes 2949124
  94.1 1.1 copy-start.10
  95.2 1.1 copy-start.17
  105.4 45.8 %copy-start.21 = (f32[8,64]{1,0:T(8,128)}, f32[8,64]{1,0:T(8,128)S(1)}, u32[]{:S(2)}) copy-start(f32[8,64]{1,0:T(8,128)S(1)} %get-tuple-element.20.c_ref) | copy-start | bytes 6148
  105.4 46.4 %copy-start.4 = (f32[32,4,256]{2,1,0:T(4,128)}, f32[32,4,256]{2,1,0:T(4,128)S(1)}, u32[]{:S(2)}) copy-start(f32[32,4,256]{2,1,0:T(4,128)S(1)} %get-tuple-element.19.e_ref) | copy-start | bytes 393220
  105.5 7.9 %collective-permute-start.4 = (f32[1,8,4,256]{3,2,1,0:T(4,128)S(1)}, f32[1,8,4,256]{3,2,1,0:T(4,128)S(1)}, u32[]{:S(2)}, u32[]{:S(2)}) collective-permute-start(f32[1,8,4,256]{3,2,1,0:T(4,128)S(1)} %get-tuple-element.30), channel_id=1, source_target_pairs={{0,16},{16,32},{32,48},{48,64},{64,80},{80,96},{96,112},{112,128},... | collective-permute-start | bytes 98312 | tf_op jit(solution)/shard_map/ppermute | solution.py:490
  112.0 7.5 %collective-permute-start.5 = (f32[1,8,4,256]{3,2,1,0:T(4,128)S(1)}, f32[1,8,4,256]{3,2,1,0:T(4,128)S(1)}, u32[]{:S(2)}, u32[]{:S(2)}) collective-permute-start(f32[1,8,4,256]{3,2,1,0:T(4,128)S(1)} %get-tuple-element.31), channel_id=1, source_target_pairs={{16,0},{32,16},{48,32},{64,48},{80,64},{96,80},{112,96},{128,112},... | collective-permute-start | bytes 98312 | tf_op jit(solution)/shard_map/ppermute | solution.py:491
  119.6 4.3 %collective-permute-start.6 = (f32[6,1,4,256]{3,2,1,0:T(4,128)S(1)}, f32[6,1,4,256]{3,2,1,0:T(4,128)S(1)}, u32[]{:S(2)}, u32[]{:S(2)}) collective-permute-start(f32[6,1,4,256]{3,2,1,0:T(4,128)S(1)} %get-tuple-element.28), channel_id=1, source_target_pairs={{0,1},{1,2},{2,3},{3,4},{4,5},{5,6},{6,7},{7,8},{8,9},{9,10},{10,1... | collective-permute-start | bytes 73736 | tf_op jit(solution)/shard_map/ppermute | solution.py:490
  121.5 5.1 %collective-permute-start.7 = (f32[6,1,4,256]{3,2,1,0:T(4,128)S(1)}, f32[6,1,4,256]{3,2,1,0:T(4,128)S(1)}, u32[]{:S(2)}, u32[]{:S(2)}) collective-permute-start(f32[6,1,4,256]{3,2,1,0:T(4,128)S(1)} %get-tuple-element.29), channel_id=1, source_target_pairs={{1,0},{2,1},{3,2},{4,3},{5,4},{6,5},{7,6},{8,7},{9,8},{10,9},{11,1... | collective-permute-start | bytes 73736 | tf_op jit(solution)/shard_map/ppermute | solution.py:491
  126.7 1.2 copy-start.3
  127.9 0.9 copy-start.15
  151.2 0.7 copy-start.7
  151.9 52.0 %copy-start.8 = (f32[32,4,256]{2,1,0:T(4,128)S(1)}, f32[32,4,256]{2,1,0:T(4,128)}, u32[]{:S(2)}) copy-start(f32[32,4,256]{2,1,0:T(4,128)} %copy-done.7) | copy-start | bytes 393220
  153.6 50.3 %copy-start.5 = (f32[32,4,256]{2,1,0:T(4,128)S(1)}, f32[32,4,256]{2,1,0:T(4,128)}, u32[]{:S(2)}) copy-start(f32[32,4,256]{2,1,0:T(4,128)} %copy-done.4) | copy-start | bytes 393220
  203.9 0.9 copy-start.11
  204.8 0.8 copy-start.13
  205.7 0.9 copy-start.18

commit v2 on v1

v2 whole, which is shorter than its diff:
```python
import functools

import jax
import jax.numpy as jnp
import numpy as np
from jax import lax
from jax.experimental import pallas as pl
from jax.experimental.pallas import tpu as pltpu
from jax.sharding import PartitionSpec as P

F32 = jnp.float32
BF = jnp.bfloat16
NEAR_LENGTH = 0.5
FAR_LENGTH = 16.0
NEAR_RATE = 3.0**0.5 / NEAR_LENGTH
FAR_RATE = 3.0**0.5 / FAR_LENGTH
LOG2E = 1.4426950408889634
COUPLING_SCALE = 1.0 / 128.0
GROUP = 8
CHUNK = 64
BUILD_SLOTS = 2
READ_SLOTS = 4
VMEM_LIMIT = 20 * 2**20
VM = pl.BlockSpec(memory_space=pltpu.VMEM)
ANY = pl.BlockSpec(memory_space=pl.ANY)
SM = pl.BlockSpec(memory_space=pltpu.SMEM)


def rounded(x):
    return x.astype(BF).astype(F32)


def split2(x):
    high = x.astype(BF)
    return high, (x - high.astype(F32)).astype(BF)


def rows16(x):
    first = rounded(x)
    second = rounded(x - first)
    third = rounded(x - first - second)
    return jnp.concatenate([first, second, third, jnp.zeros_like(x)], axis=0).astype(BF)


def join16(y):
    return y[0:4] + y[4:8] + y[8:12]


def dot(a, b):
    return jnp.dot(a, b, preferred_element_type=F32)


def dot_nt(a, b):
    return lax.dot_general(a, b, (((1,), (1,)), ((), ())), preferred_element_type=F32)


def split3(x):
    first = x.astype(BF)
    rest = x - first.astype(F32)
    second = rest.astype(BF)
    return first, second, (rest - second.astype(F32)).astype(BF)


def exact_dot(a, b):
    return jnp.dot(a, b, precision=lax.Precision.HIGHEST, preferred_element_type=F32)


def feature_tables():
    target = np.zeros((32, 24), np.float32)
    source = np.zeros((32, 24), np.float32)
    factor = np.ones((9, 32), np.float32)
    one = 19
    for c in range(3):
        target[2 * c, c] = target[2 * c + 1, c] = -2
        source[2 * c, c] = source[2 * c + 1, 8 + c] = 1
        target[6 + 2 * c, 8 + c] = target[7 + 2 * c, 8 + c] = -2
        source[6 + 2 * c, c] = source[7 + 2 * c, 8 + c] = 1
    for k in range(3):
        target[12 + k, one] = source[12 + k, 16 + k] = 1
        target[15 + k, 16 + k] = source[15 + k, one] = 1
    for c in range(2):
        target[18 + 2 * c, c] = target[19 + 2 * c, 8 + c] = 1
        source[18 + 2 * c, one] = source[19 + 2 * c, one] = 1
        target[22 + 2 * c, one] = target[23 + 2 * c, one] = 1
        source[22 + 2 * c, c] = source[23 + 2 * c, 8 + c] = 1
    target[26, one] = source[26, one] = 1
    for code in range(9):
        off = (code // 3 - 1, code % 3 - 1)
        for c in range(2):
            factor[code, 18 + 2 * c : 20 + 2 * c] = -2 * off[c]
            factor[code, 22 + 2 * c : 24 + 2 * c] = 2 * off[c]
        factor[code, 26] = off[0] ** 2 + off[1] ** 2
    return target, source, factor


def params():
    return pltpu.CompilerParams(vmem_limit_bytes=VMEM_LIMIT)


def around(nx, ny):
    wide = ny + 2
    return (
        (nx * ny, lambda i: (i // ny + 1) * wide + i % ny + 1),
        (ny, lambda i: i + 1),
        (ny, lambda i: (nx + 1) * wide + i + 1),
        (nx + 2, lambda i: i * wide),
        (nx + 2, lambda i: i * wide + wide - 1),
    )


def each_leaf(nx, ny, refs, body, unroll=4):
    for ref, (count, place) in zip(refs, around(nx, ny)):

        def step(i, carry, ref=ref, place=place):
            body(place(i), ref, i)
            return carry

        lax.fori_loop(0, count, step, 0, unroll=unroll if count % unroll == 0 else 2)


def pack_kernel(nx, ny, count_ref, points_ref, sides_ref, packed_ref, top_ref, bottom_ref, r_ref, valid_ref):
    size = points_ref.shape[2]
    row = lax.broadcasted_iota(jnp.int32, (3, size), 0)
    lane = lax.broadcasted_iota(jnp.int32, (1, size), 1)

    def body(a, carry):
        first = (lax.axis_index("gx") * nx + a // ny).astype(F32) + 0.5
        second = (lax.axis_index("gy") * ny + a % ny).astype(F32) + 0.5
        packed_ref[a, 0:3] = points_ref[a] - jnp.where(row == 0, first, jnp.where(row == 1, second, 0.5))
        count = count_ref[a // ny, a % ny]
        packed_ref[a, 3:4] = jnp.full((1, size), count.astype(F32))
        valid = jnp.where(lane < count, 1.0, 0.0)
        r = jnp.where(valid > 0.0, sides_ref[a], 0.0)
        packed_ref[a, 4:8] = r
        part = pl.ds(pl.multiple_of(a * size, size), size)
        r_ref[:, part] = r
        valid_ref[:, part] = valid
        return carry

    lax.fori_loop(0, nx * ny, body, 0, unroll=4)
    top_ref[...] = packed_ref[0:ny]
    bottom_ref[...] = packed_ref[(nx - 1) * ny : nx * ny]


def pack(nx, ny, counts, points, sides):
    leaves, _, size = points.shape
    return pl.pallas_call(
        functools.partial(pack_kernel, nx, ny),
        out_shape=[
            jax.ShapeDtypeStruct((leaves, 8, size), F32),
            jax.ShapeDtypeStruct((ny, 8, size), F32),
            jax.ShapeDtypeStruct((ny, 8, size), F32),
            jax.ShapeDtypeStruct((4, leaves * size), F32),
            jax.ShapeDtypeStruct((1, leaves * size), F32),
        ],
        in_specs=[SM, VM, VM],
        out_specs=[VM] * 5,
        compiler_params=params(),
        name="pack",
    )(counts, points, sides)


def sides_kernel(nx, ny, own_ref, up_ref, down_ref, left_ref, right_ref):
    for col, ref in ((0, left_ref), (ny - 1, right_ref)):
        ref[0] = up_ref[col]
        ref[nx + 1] = down_ref[col]
        for i in range(nx):
            ref[i + 1] = own_ref[i * ny + col]


def side_columns(nx, ny, own, up, down):
    out = jax.ShapeDtypeStruct((nx + 2,) + own.shape[1:], F32)
    return pl.pallas_call(
        functools.partial(sides_kernel, nx, ny),
        out_shape=[out, out],
        in_specs=[VM] * 3,
        out_specs=[VM] * 2,
        compiler_params=params(),
        name="side_columns",
    )(own, up, down)


def geometry_kernel(nx, ny, own_ref, up_ref, down_ref, left_ref, right_ref, target_ref, source_ref, s_ref, t_ref):
    row = lax.broadcasted_iota(jnp.int32, (8, own_ref.shape[2]), 0)

    def body(e, ref, i):
        x = jnp.where(row < 3, ref[i], 0.0)
        first = rounded(x)
        second = rounded(x - first)
        held = first + second
        norm = jnp.sum(held * held, axis=0, keepdims=True)
        n1 = rounded(norm)
        n2 = rounded(norm - n1)
        n3 = rounded(norm - n1 - n2)
        last = jnp.where(row == 0, n1, jnp.where(row == 1, n2, jnp.where(row == 2, n3, jnp.where(row == 3, 1.0, 0.0))))
        f = jnp.concatenate([first, second, last], axis=0).astype(BF)
        t_ref[e] = dot(target_ref[...], f).astype(BF)
        s_ref[e] = lax.dot_general(
            f, source_ref[...], (((0,), (1,)), ((), ())), preferred_element_type=F32
        ).astype(BF)

    each_leaf(nx, ny, (own_ref, up_ref, down_ref, left_ref, right_ref), body, 8)


def geometry(nx, ny, parts, target_table, source_table):
    leaves, size = (nx + 2) * (ny + 2), parts[0].shape[2]
    return pl.pallas_call(
        functools.partial(geometry_kernel, nx, ny),
        out_shape=[
            jax.ShapeDtypeStruct((leaves, size, 32), BF),
            jax.ShapeDtypeStruct((leaves, 32, size), BF),
        ],
        in_specs=[VM] * 7,
        out_specs=[VM] * 2,
        compiler_params=params(),
        name="geometry",
    )(*parts, jnp.asarray(target_table, BF), jnp.asarray(source_table, BF))


def build_kernel(
    nx, ny, mask_ref, own_ref, up_ref, down_ref, left_ref, right_ref, s_ref, t_ref, factor_ref, c_ref, g_ref, b_ref,
    o_ref, list_ref, cache_ref, out_ref, v16, acc, spare, count_ref, buffer, sems,
):
    wide = ny + 2
    leaves = (nx + 2) * wide
    size = own_ref.shape[2]
    short = size - CHUNK

    def split_leaf(e, ref, i):
        v16[e] = rows16(ref[i, 4:8])
        count_ref[e] = ref[i, 3, 0].astype(jnp.int32)

    each_leaf(nx, ny, (own_ref, up_ref, down_ref, left_ref, right_ref), split_leaf)
    v16[leaves] = jnp.zeros((16, size), BF)
    acc[...] = jnp.zeros_like(acc)
    for slot in range(BUILD_SLOTS):
        for j in range(GROUP):
            buffer[slot, j, :, short:size] = jnp.zeros((2, CHUNK, size), BF)
    dummy = leaves * 1024

    def note(a, carry):
        full, less = carry
        corner = (a // ny) * wide + a % ny
        for code in range(9):
            source = corner + code // 3 * wide + code % 3
            entry = (source * 16 + code) * 64 + a
            on = jnp.where(mask_ref[a // ny, a % ny, code] != 0, 1, 0)
            long = jnp.where(count_ref[source] > short, on, 0)
            list_ref[full] = entry
            spare[less] = entry
            full = full + long
            less = less + (on - long)
        return full, less

    full, less = lax.fori_loop(0, nx * ny, note, (0, 0), unroll=2)
    for j in range(GROUP):
        list_ref[full + j] = dummy
        spare[less + j] = dummy
    full_groups = (full + GROUP - 1) // GROUP
    less_groups = (less + GROUP - 1) // GROUP
    groups = full_groups + less_groups

    def move(k, carry):
        list_ref[full_groups * GROUP + k] = spare[k]
        return carry

    lax.fori_loop(0, less_groups * GROUP, move, 0)
    list_ref[list_ref.shape[0] - 1] = groups

    def copy_out(g):
        slot = g % BUILD_SLOTS
        return pltpu.make_async_copy(buffer.at[slot], cache_ref.at[g], sems.at[slot])

    def run(first, last, rows):
        def group(g, carry):
            slot = g % BUILD_SLOTS

            @pl.when(g >= BUILD_SLOTS)
            def _():
                copy_out(g - BUILD_SLOTS).wait()

            done = []
            for j in range(GROUP):
                entry = list_ref[g * GROUP + j]
                a = entry & 63
                code = (entry >> 6) & 15
                source = entry >> 10
                t = t_ref[(a // ny + 1) * wide + a % ny + 1] * factor_ref[code]
                s = s_ref[jnp.minimum(source, leaves - 1)]
                v = v16[source]
                total = jnp.zeros((16, size), F32)
                for k in range(rows // CHUNK):
                    part = slice(k * CHUNK, (k + 1) * CHUNK)
                    squared = jnp.maximum(dot(s[part], t), 1e-30)
                    distance = squared * lax.rsqrt(squared)
                    value = (1.0 + NEAR_RATE * distance) * jnp.exp2((-NEAR_RATE * LOG2E) * distance)
                    high, low = split2(value)
                    buffer[slot, j, 0, part] = high
                    buffer[slot, j, 1, part] = low
                    total += dot(v[:, part], high) + dot(v[:, part], low)
                done.append((a, total))
            for a, total in done:
                acc[a] += total
            copy_out(g).start()
            return carry

        lax.fori_loop(first, last, group, 0)

    run(0, full_groups, size)
    run(full_groups, groups, short)
    for back in range(BUILD_SLOTS):
        copy_out(groups - 1 - back).wait()

    def finish(a, carry):
        o_ref[:, pl.ds(pl.multiple_of(a * size, size), size)] = join16(acc[a]) * (1.0 / size**0.5)
        return carry

    lax.fori_loop(0, nx * ny, finish, 0, unroll=4)
    for i in range(out_ref.shape[0]):
        out_ref[i] = c_ref[...]


def near_build(nx, ny, mask, parts, s, t, factor, c, g, b, copies):
    size = parts[0].shape[2]
    leaves = (nx + 2) * (ny + 2)
    most = nx * ny * 9 + 2 * GROUP
    return pl.pallas_call(
        functools.partial(build_kernel, nx, ny),
        out_shape=[
            jax.ShapeDtypeStruct((4, nx * ny * size), F32),
            jax.ShapeDtypeStruct((most + 8,), jnp.int32),
            jax.ShapeDtypeStruct((most // GROUP, GROUP, 2, size, size), BF),
            jax.ShapeDtypeStruct((copies, 8, 128), F32),
        ],
        in_specs=[SM] + [VM] * 9 + [ANY] * 2,
        out_specs=[VM, SM, ANY, VM],
        scratch_shapes=[
            pltpu.VMEM((leaves + 1, 16, size), BF),
            pltpu.VMEM((nx * ny, 16, size), F32),
            pltpu.SMEM((most,), jnp.int32),
            pltpu.SMEM((leaves,), jnp.int32),
            pltpu.VMEM((BUILD_SLOTS, GROUP, 2, size, size), BF),
            pltpu.SemaphoreType.DMA((BUILD_SLOTS,)),
        ],
        compiler_params=params(),
        name="near_build",
    )(mask, *parts, s, t, factor, c, g, b)


def reuse_kernel(
    nx, ny, list_ref, own_ref, up_ref, down_ref, left_ref, right_ref, c_ref, cache_ref,
    o_ref, out_ref, v16, acc, buffer, sems,
):
    wide = ny + 2
    leaves = (nx + 2) * wide
    size = own_ref.shape[2]
    groups = list_ref[list_ref.shape[0] - 1]

    def copy_in(g):
        slot = g % READ_SLOTS
        return pltpu.make_async_copy(cache_ref.at[g], buffer.at[slot], sems.at[slot])

    for g in range(READ_SLOTS - 1):
        copy_in(g).start()

    def split_leaf(e, ref, i):
        v16[e] = rows16(ref[i])

    each_leaf(nx, ny, (own_ref, up_ref, down_ref, left_ref, right_ref), split_leaf)
    v16[leaves] = jnp.zeros((16, size), BF)
    acc[...] = jnp.zeros_like(acc)

    def group(g, carry):
        slot = g % READ_SLOTS
        copy_in(g).wait()

        @pl.when(g + READ_SLOTS - 1 < groups)
        def _():
            copy_in(g + READ_SLOTS - 1).start()

        done = []
        for j in range(GROUP):
            entry = list_ref[g * GROUP + j]
            v = v16[entry >> 10]
            done.append((entry & 63, dot(v, buffer[slot, j, 0]) + dot(v, buffer[slot, j, 1])))
        for a, total in done:
            acc[a] += total
        return carry

    lax.fori_loop(0, groups, group, 0)

    def finish(a, sums):
        near = join16(acc[a]) * (1.0 / size**0.5)
        o_ref[:, pl.ds(pl.multiple_of(a * size, size), size)] = near
        v = own_ref[a]
        return tuple(sums[s] + v * near[s : s + 1] for s in range(4))

    sums = lax.fori_loop(0, nx * ny, finish, tuple(jnp.zeros((4, size), F32) for _ in range(4)), unroll=4)
    columns = [jnp.sum(x, axis=1, keepdims=True) for x in sums]
    block = jnp.concatenate([jnp.zeros((4, 12), F32)] + columns + [jnp.zeros((4, 112), F32)], axis=1)
    total = c_ref[...] + jnp.concatenate([jnp.zeros((4, 128), F32), block], axis=0)
    for i in range(out_ref.shape[0]):
        out_ref[i] = total


def near_reuse(nx, ny, todo, parts, c, cache, copies):
    size = parts[0].shape[2]
    leaves = (nx + 2) * (ny + 2)
    return pl.pallas_call(
        functools.partial(reuse_kernel, nx, ny),
        out_shape=[jax.ShapeDtypeStruct((4, nx * ny * size), F32), jax.ShapeDtypeStruct((copies, 8, 128), F32)],
        in_specs=[SM] + [VM] * 6 + [ANY],
        out_specs=[VM] * 2,
        scratch_shapes=[
            pltpu.VMEM((leaves + 1, 16, size), BF),
            pltpu.VMEM((nx * ny, 16, size), F32),
            pltpu.VMEM((READ_SLOTS,) + cache.shape[1:], BF),
            pltpu.SemaphoreType.DMA((READ_SLOTS,)),
        ],
        compiler_params=params(),
        name="near_reuse",
    )(todo, *parts, c, cache)


def upward_kernel(r_ref, basis_ref, transfer_ref, joint_ref, c_ref):
    leaves, terms, size = basis_ref.shape

    def body(a, total):
        part = pl.ds(pl.multiple_of(a * size, size), size)
        joint = exact_dot(transfer_ref[a], basis_ref[a])
        terms3 = split3(joint)
        v = rows16(r_ref[:, part])
        for k, term in enumerate(terms3):
            joint_ref[k, :, part] = term
            total = total + dot_nt(v, term)
        return total

    total = join16(lax.fori_loop(0, leaves, body, jnp.zeros((16, terms), F32), unroll=8))
    total = jnp.concatenate([total, jnp.zeros((4, 128 - terms), F32)], axis=1)
    total = jnp.concatenate([total, jnp.zeros((4, 128), F32)], axis=0)
    c_ref[...] = total


def upward(r, basis, transfer):
    leaves, terms, size = basis.shape
    return pl.pallas_call(
        upward_kernel,
        out_shape=[
            jax.ShapeDtypeStruct((3, terms, leaves * size), BF),
            jax.ShapeDtypeStruct((8, 128), F32),
        ],
        in_specs=[VM] * 3,
        out_specs=[VM] * 2,
        compiler_params=params(),
        name="upward",
    )(r, basis, transfer)


def own_place(cols):
    return lax.axis_index("gx") * cols + lax.axis_index("gy")


def coupling_kernel(levels, cols, tile, upper_ref, row_ref, b_ref, g_ref, turned_ref):
    place = own_place(cols)
    col_values = jnp.concatenate([row_ref[...], jnp.zeros((5, 64), F32)], axis=0).T
    for k in range(2):
        turned_ref[k] = upper_ref[k].T
    down = None
    for level in range(levels):
        span = 2**level
        extent = (1, span) if span <= cols else (span // cols, cols)
        half = (0.5 * tile[0] * extent[0], 0.5 * tile[1] * extent[1], 0.5)
        apart = (0.0, 2.0 * span * tile[1]) if 2 * span < cols else (2.0 * span / cols * tile[0], 0.0)

        def matrix(sign):
            squared = jnp.zeros((64, 64), F32)
            for c in range(3):
                step = half[c] * (col_values[:, c : c + 1] - row_ref[c : c + 1, :])
                if c < 2:
                    step = step + sign * apart[c]
                squared = squared + step * step
            squared = jnp.maximum(squared, 1e-30)
            scaled = FAR_RATE * (squared * lax.rsqrt(squared))
            return COUPLING_SCALE * ((1.0 + scaled) * jnp.exp(-scaled))

        b_ref[level] = matrix(-1.0)
        upper = (place // (2 * span)) % 2
        own = matrix(jnp.where(upper == 1, -1.0, 1.0))
        g_ref[level] = own if down is None else exact_dot(own, down)
        if level + 1 < levels:
            bit = (place // span) % 2
            step_down = upper_ref[bit]
            down = step_down if down is None else exact_dot(step_down, down)


def couplings(levels, cols, tile, upper, nodes):
    out = jax.ShapeDtypeStruct((levels, 64, 64), F32)
    return pl.pallas_call(
        functools.partial(coupling_kernel, levels, cols, tile),
        out_shape=[out, out, jax.ShapeDtypeStruct(upper.shape, F32)],
        in_specs=[VM] * 2,
        out_specs=[VM] * 3,
        compiler_params=params(),
        name="couplings",
    )(upper, nodes)


def pair_energy(c, b, sums):
    count = c.shape[0]
    quads = c.reshape(count // 4, 4, 8, 64)
    low = quads[:, 0:2].reshape(count // 2 * 8, 64)
    high = quads[:, 2:4].reshape(count // 2, 8, 64)
    carried = exact_dot(low, b).reshape(count // 2, 8, 64)
    return [sums[s] + jnp.sum(carried * high[:, s : s + 1, :], axis=0) for s in range(4)]


def lift(c, upper_t):
    count = c.shape[0]
    paired = c.reshape(count // 2, 2, 8, 64)
    even = paired[:, 0].reshape(count // 2 * 8, 64)
    odd = paired[:, 1].reshape(count // 2 * 8, 64)
    return (exact_dot(even, upper_t[0]) + exact_dot(odd, upper_t[1])).reshape(count // 2, 8, 64)


def no_sums():
    return [jnp.zeros((8, 64), F32) for _ in range(4)]


def columns_of(sums):
    return jnp.concatenate([jnp.sum(x, axis=1, keepdims=True) for x in sums], axis=1)


def row_kernel(with_energy, c_ref, upper_ref, g_ref, b_ref, y_ref, out_ref, scratch):
    x = c_ref[...]
    c = x[:, :, 0:64]
    place = lax.axis_index("gy")
    y = jnp.zeros((8, 64), F32)
    sums = no_sums()
    level = 0
    while c.shape[0] > 2:
        scratch[0 : c.shape[0]] = c
        y = y + exact_dot(scratch[(place // 2**level) ^ 2], g_ref[level])
        if with_energy:
            sums = pair_energy(c, b_ref[level], sums)
        c = lift(c, upper_ref)
        level += 1
    y_ref[...] = y
    lower = jnp.zeros((4, 128), F32)
    if with_energy:
        lower = jnp.sum(x, axis=0)[4:8]
        lower = jnp.concatenate([lower[:, 0:16], columns_of(sums)[0:4], jnp.zeros((4, 108), F32)], axis=1)
    total = jnp.concatenate([jnp.concatenate([c[0, 0:4], c[1, 0:4]], axis=1), lower], axis=0)
    for i in range(out_ref.shape[0]):
        out_ref[i] = total


def row_tree(with_energy, c, upper_t, g, b):
    return pl.pallas_call(
        functools.partial(row_kernel, with_energy),
        out_shape=[jax.ShapeDtypeStruct((8, 64), F32), jax.ShapeDtypeStruct(c.shape, F32)],
        in_specs=[VM] * 4,
        out_specs=[VM] * 2,
        scratch_shapes=[pltpu.VMEM((c.shape[0], 8, 64), F32)],
        compiler_params=params(),
        name="row_tree",
    )(c, upper_t, g, b)


def upper_levels(cols, levels, x, y, upper_ref, g_ref, b_ref, scratch, with_energy):
    place = own_place(cols)
    level = cols.bit_length() - 2
    c = jnp.stack([x[:, :, 0:64], x[:, :, 64:128]], axis=1).reshape(2 * x.shape[0], 8, 64)
    sums = no_sums()
    while level < levels:
        scratch[0 : c.shape[0]] = c
        y = y + exact_dot(scratch[(place // 2**level) ^ 2], g_ref[level])
        if with_energy:
            sums = pair_energy(c, b_ref[level], sums)
        if level + 1 < levels:
            c = lift(c, upper_ref)
        level += 1
    return y[0:4], sums


SPLITS = 8


def far_of(y, joint_ref, part):
    return join16(dot(y, joint_ref[0, :, part]) + (dot(y, joint_ref[1, :, part]) + dot(y, joint_ref[2, :, part])))


def middle_kernel(
    cols, levels, x_ref, y_ref, upper_ref, g_ref, joint_ref, r_ref, n_ref, valid_ref,
    e_ref, leaf_ref, top_ref, bottom_ref, out_ref, scratch, both,
):
    leaves, _, size = leaf_ref.shape
    own, _ = upper_levels(cols, levels, x_ref[...], y_ref[...], upper_ref, g_ref, None, scratch, False)
    y = rows16(own)
    width = leaves * size // SPLITS
    for k in range(SPLITS):
        part = slice(k * width, (k + 1) * width)
        far = far_of(y, joint_ref, part)
        e = valid_ref[:, part] * (n_ref[:, part] + far)
        e_ref[:, part] = e
        both[0:16, part] = rows16(r_ref[:, part])
        both[16:32, part] = rows16(e)
        for i in range(leaves // SPLITS):
            leaf_ref[k * (leaves // SPLITS) + i] = e[:, i * size : (i + 1) * size]
    edge = top_ref.shape[0]
    top_ref[...] = leaf_ref[0:edge]
    bottom_ref[...] = leaf_ref[leaves - edge : leaves]
    e16 = both[16:32, :]
    c = join16(dot_nt(e16, joint_ref[0]) + (dot_nt(e16, joint_ref[1]) + dot_nt(e16, joint_ref[2])))
    square = dot_nt(both[...], both[...])

    def block(i, j):
        part = join16(square[16 * i : 16 * i + 16, 16 * j : 16 * j + 16])
        return part[:, 0:4] + part[:, 4:8] + part[:, 8:12]

    moments = jnp.concatenate([block(0, 0), block(0, 1), block(1, 1), jnp.zeros((4, 116), F32)], axis=1)
    out_ref[...] = jnp.concatenate([jnp.concatenate([c, jnp.zeros((4, 64), F32)], axis=1), moments], axis=0)


def middle(cols, levels, leaves, edge, x, y, upper_t, g, joint, r, n, valid):
    size = r.shape[1] // leaves
    return pl.pallas_call(
        functools.partial(middle_kernel, cols, levels),
        out_shape=[
            jax.ShapeDtypeStruct(r.shape, F32),
            jax.ShapeDtypeStruct((leaves, 4, size), F32),
            jax.ShapeDtypeStruct((edge, 4, size), F32),
            jax.ShapeDtypeStruct((edge, 4, size), F32),
            jax.ShapeDtypeStruct((8, 128), F32),
        ],
        in_specs=[VM] * 8,
        out_specs=[VM] * 5,
        scratch_shapes=[pltpu.VMEM((2 * x.shape[0], 8, 64), F32), pltpu.VMEM((32, r.shape[1]), BF)],
        compiler_params=params(),
        name="middle",
    )(x, y, upper_t, g, joint, r, n, valid)


def mat_mul(a, b):
    return [[sum(a[i][k] * b[k][j] for k in range(4)) for j in range(4)] for i in range(4)]


def mat_add(a, b):
    return [[a[i][j] + b[i][j] for j in range(4)] for i in range(4)]


def mat_sub(a, b):
    return [[a[i][j] - b[i][j] for j in range(4)] for i in range(4)]


def mat_t(a):
    return [[a[j][i] for j in range(4)] for i in range(4)]


def mat_solve(a, b):
    a = [list(row) for row in a]
    b = [list(row) for row in b]
    width = len(b[0])
    inverse = []
    for col in range(4):
        inverse.append(1.0 / a[col][col])
        for row in range(col + 1, 4):
            factor = a[row][col] * inverse[col]
            for k in range(col + 1, 4):
                a[row][k] = a[row][k] - factor * a[col][k]
            for k in range(width):
                b[row][k] = b[row][k] - factor * b[col][k]
    result = [None] * 4
    for col in reversed(range(4)):
        row = list(b[col])
        for later in range(col + 1, 4):
            row = [row[k] - a[col][later] * result[later][k] for k in range(width)]
        result[col] = [value * inverse[col] for value in row]
    return result


def weights(gram, cross, square, cubic):
    curvature = mat_add(gram, cross)
    both = mat_solve(curvature, [gram[i] + cross[i] for i in range(4)])
    step = [row[0:4] for row in both]
    rest = [row[4:8] for row in both]
    mixed = mat_mul(mat_t(rest), mat_mul(cross, step))
    gram_next = mat_sub(
        mat_add(mat_mul(mat_t(rest), mat_mul(gram, rest)), mat_mul(mat_t(step), mat_mul(square, step))),
        mat_add(mixed, mat_t(mixed)),
    )
    mix = mat_solve(gram, gram_next)
    lead = mat_add(rest, mix)
    second = mat_sub(lead, step)
    with_r = mat_sub(mat_add(mat_mul(gram, lead), mat_mul(cross, second)), mat_mul(square, step))
    with_e = mat_sub(mat_add(mat_mul(mat_t(cross), lead), mat_mul(square, second)), mat_mul(cubic, step))
    curvature_next = mat_sub(mat_mul(mat_t(lead), with_r), mat_mul(mat_t(step), with_e))
    step_next = mat_solve(curvature_next, gram_next)
    lead_step = mat_mul(lead, step_next)
    step_step = mat_mul(step, step_next)
    second_step = mat_sub(lead_step, step_step)
    solution = (mat_add(step, lead_step), [[-v for v in row] for row in step_step], None)
    residual = (mat_sub(rest, lead_step), [[-(step[i][j] + second_step[i][j]) for j in range(4)] for i in range(4)], step_step)
    return solution, residual


def final_kernel(
    cols, levels, c_ref, y_ref, upper_ref, g_ref, b_ref, joint_ref, r_ref, e_ref, n_ref, valid_ref,
    x_ref, out_ref, scratch,
):
    leaves, _, size = x_ref.shape
    c = c_ref[...]
    own, sums = upper_levels(cols, levels, c, y_ref[...], upper_ref, g_ref, b_ref, scratch, True)
    y = rows16(own)
    moments = jnp.sum(c, axis=0)[4:8]
    half = columns_of(sums)

    def matrix(x, at):
        return [[jnp.broadcast_to(x[i : i + 1, at + j : at + j + 1], (1, 128)) for j in range(4)] for i in range(4)]

    half = mat_add(matrix(moments, 16), matrix(half, 0))
    cubic = mat_add(matrix(moments, 12), mat_add(half, mat_t(half)))
    solution, residual = weights(matrix(moments, 0), matrix(moments, 4), matrix(moments, 8), cubic)
    row = lax.broadcasted_iota(jnp.int32, (8, 128), 0)
    col = lax.broadcasted_iota(jnp.int32, (8, 128), 1)
    table = jnp.zeros((8, 128), F32)
    for first, parts in ((0, solution), (4, residual)):
        for k, part in enumerate(parts):
            if part is None:
                continue
            for i in range(4):
                line = jnp.zeros((8, 128), F32)
                for j in range(4):
                    line = jnp.where(row == first + j, part[i][j], line)
                table = jnp.where(col == 4 * k + i, line + table, table)
    table = table[:, 0:16]
    width = leaves * size // SPLITS
    for k in range(SPLITS):
        part = slice(k * width, (k + 1) * width)
        far = far_of(y, joint_ref, part)
        f = valid_ref[:, part] * (n_ref[:, part] + far)
        stacked = jnp.concatenate([r_ref[:, part], e_ref[:, part], f, jnp.zeros_like(f)], axis=0)
        both = jnp.dot(table, stacked, precision=lax.Precision.HIGHEST, preferred_element_type=F32)
        for i in range(leaves // SPLITS):
            x_ref[k * (leaves // SPLITS) + i] = both[0:4, i * size : (i + 1) * size]
            out_ref[k * (leaves // SPLITS) + i] = both[4:8, i * size : (i + 1) * size]


def final(cols, levels, leaves, c, y, upper_t, g, b, joint, r, e, n, valid):
    out = jax.ShapeDtypeStruct((leaves, 4, r.shape[1] // leaves), F32)
    return pl.pallas_call(
        functools.partial(final_kernel, cols, levels),
        out_shape=[out, out],
        in_specs=[VM] * 10,
        out_specs=[VM] * 2,
        scratch_shapes=[pltpu.VMEM((2 * c.shape[0], 8, 64), F32)],
        compiler_params=params(),
        name="final",
    )(c, y, upper_t, g, b, joint, r, e, n, valid)


def swap(axis, first, last):
    count = lax.axis_size(axis)
    up = [(i, i + 1) for i in range(count - 1)]
    down = [(j, i) for i, j in up]
    return lax.ppermute(last, axis, up), lax.ppermute(first, axis, down)


def edges(nx, ny, own, top, bottom):
    up, down = swap("gx", top, bottom)
    left, right = swap("gy", *side_columns(nx, ny, own, up, down))
    return own, up, down, left, right


def exchange(x, axis):
    return lax.all_to_all(x, axis, 0, 0, tiled=True)


def on_device(points, right_sides, leaf_counts, near_mask, leaf_basis, leaf_transfer, upper_transfer, proxy_nodes):
    nx, ny, _, size = points.shape
    leaves = nx * ny
    rows, cols = lax.axis_size("gx"), lax.axis_size("gy")
    levels = (rows * cols).bit_length() - 2
    target_table, source_table, factor = feature_tables()
    factor = jnp.asarray(np.broadcast_to(factor[:, :, None], (9, 32, size)), BF)

    def flat(x):
        return x.reshape((leaves,) + x.shape[2:])

    packed, top, bottom, r, valid = pack(nx, ny, leaf_counts, flat(points), flat(right_sides))
    parts = edges(nx, ny, packed, top, bottom)
    joint, c = upward(r, flat(leaf_basis), flat(leaf_transfer))
    b, g, upper_t = couplings(levels, cols, (nx, ny), upper_transfer, proxy_nodes)
    s, t = geometry(nx, ny, parts, target_table, source_table)
    n, todo, cache, c = near_build(nx, ny, near_mask, parts, s, t, factor, c, g, b, cols)
    y, c = row_tree(False, exchange(c, "gy"), upper_t, g, b)
    e, e_leaves, top, bottom, c = middle(
        cols, levels, leaves, ny, exchange(c, "gx"), y, upper_t, g, joint, r, n, valid
    )
    n, c = near_reuse(nx, ny, todo, edges(nx, ny, e_leaves, top, bottom), c, cache, cols)
    y, c = row_tree(True, exchange(c, "gy"), upper_t, g, b)
    x, out = final(cols, levels, leaves, exchange(c, "gx"), y, upper_t, g, b, joint, r, e, n, valid)
    shape = (nx, ny, 4, size)
    return x.reshape(shape), out.reshape(shape)


def solution(mesh):
    return jax.shard_map(
        on_device,
        mesh=mesh,
        in_specs=(
            P("gx", "gy", None, None),
            P("gx", "gy", None, None),
            P("gx", "gy"),
            P("gx", "gy", None),
            P("gx", "gy", None, None),
            P("gx", "gy", None, None),
            P(),
            P(),
        ),
        out_specs=(P("gx", "gy", None, None), P("gx", "gy", None, None)),
        check_vma=False,
    )
```

time: 215 us -> 166 us (0.77)
  blocking collectives: 41.5 us -> 66.8 us
  local copies, waits for them, and re-layouts: 27.3 us -> 6.93 us
  Pallas kernels: 77 us -> 57.9 us
  starting transfers between devices: 39 us -> 23.2 us
  waiting for transfers between devices: 20.5 us -> 10.3 us
  other arithmetic: 9.86 us -> 0 us
    all_to_all x2 -> x4, blocking collectives: 41.5 us -> 66.8 us  [exchange(): return lax.all_to_all(x, axis, 0, 0, tiled=True)]
    pallas_call x7 -> x11, Pallas kernels: 74.4 us -> 56.4 us  [the longest x1 25.5 us: near_build(): pl.pallas_call(functools.partial(build_kernel, nx, ny), out_shape=[jax.Sh...]
    all_to_all x2 -> x0, starting transfers between devices: 16.8 us -> none  [from_all(): lax.all_to_all(jnp.broadcast_to(x[None], (count,) + x.shape), axis, 0, 0,...]
    unnamed x64 -> x21, local copies, waits for them, and re-layouts: 23.6 us -> 6.93 us
    all_to_all x4 -> x0, other arithmetic: 7.69 us -> none  [from_all(): lax.all_to_all(jnp.broadcast_to(x[None], (count,) + x.shape), axis, 0, 0,...]
    all_to_all x2 -> x0, waiting for transfers between devices: 7.05 us -> none  [from_all(): lax.all_to_all(jnp.broadcast_to(x[None], (count,) + x.shape), axis, 0, 0,...]
    ppermute x8, waiting for transfers between devices: 13.4 us -> 10.3 us  [swap(): return (lax.ppermute(last, axis, up), lax.ppermute(first, axis, down))]
    broadcast_in_dim x7 -> x0, local copies, waits for them, and re-layouts: 2.82 us -> none  [the longest x4 2.73 us: from_all(): jnp.broadcast_to(x[None], (count,) + x.shape)]
  transfers between devices with their start and end apart: 10 -> 8, of which waited for: 5 -> 3; matrix products, arithmetic and copies ran while one was open for 1% -> 0% of each run, Pallas kernels for 14% -> 4%
where the time goes in v2:
time: 166 us
  blocking collectives  66.8 us (40%)
  Pallas kernels  57.9 us (35%)
  starting transfers between devices  23.2 us (14%)
  waiting for transfers between devices  10.3 us (6%)
  local copies, waits for them, and re-layouts  6.93 us (4%)
    all_to_all x4, blocking collectives, exchange(): return lax.all_to_all(x, axis, 0, 0, tiled=True)  66.8 us
    pallas_call x1, Pallas kernels, near_build(): pl.pallas_call(functools.partial(build_kernel, nx, ny), out_shape=[jax.Sh...  25.5 us
    ppermute x8, starting transfers between devices, swap(): return (lax.ppermute(last, axis, up), lax.ppermute(first, axis, down))  23.2 us
    pallas_call x1, Pallas kernels, near_reuse(): pl.pallas_call(functools.partial(reuse_kernel, nx, ny), out_shape=[jax.Sh...  12.9 us
    ppermute x8, waiting for transfers between devices, swap(): return (lax.ppermute(last, axis, up), lax.ppermute(first, axis, down))  10.3 us
    unnamed x21, local copies, waits for them, and re-layouts  6.93 us
    pallas_call x1, Pallas kernels, upward(): pl.pallas_call(upward_kernel, out_shape=[jax.ShapeDtypeStruct((3, terms,...  4.82 us
    pallas_call x1, Pallas kernels, final(): pl.pallas_call(functools.partial(final_kernel, cols, levels), out_shape=[...  4.26 us
  transfers between devices with their start and end apart: 8, of which 3 were waited for; matrix products, arithmetic and copies ran while one was open for 0% of the time, Pallas kernels for 4%

profile of v2, /device:TPU:1, one launch (start us, length us, event | category | flops | bytes accessed | tf_op | source)
XLA Modules:
  0.0 165.9 jit_solution(11794297300444002635)
XLA Ops:
  0.6 0.0 copy-start.6
  0.6 0.0 copy-start.7
  0.7 0.0 copy-start.2
  0.7 0.0 copy-start.5
  0.7 1.0 copy.13
  1.7 0.0 copy-start.3
  1.7 0.9 copy-done.3
  2.6 0.0 copy-start.8
  2.6 0.7 copy-done.8
  3.3 1.0 pack.1
  4.3 3.9 %collective-permute-start = (f32[8,8,256]{2,1,0:T(8,128)S(1)}, f32[8,8,256]{2,1,0:T(8,128)S(1)}, u32[]{:S(2)}, u32[]{:S(2)}) collective-permute-start(f32[8,8,256]{2,1,0:T(8,128)S(1)} %get-tuple-element.36), channel_id=1, source_target_pairs={{0,16},{16,32},{32,48},{48,64},{64,80},{80,96},{96,112},{112,128},... | collective-permute-start | bytes 196616 | tf_op jit(solution)/shard_map/ppermute | solution.py:765
  8.3 1.3 collective-permute-start.1
  9.6 0.0 collective-permute-done.up_ref
  9.6 3.7 %collective-permute-done.1.down_ref = f32[8,8,256]{2,1,0:T(8,128)S(1)} collective-permute-done((f32[8,8,256]{2,1,0:T(8,128)S(1)}, f32[8,8,256]{2,1,0:T(8,128)S(1)}, u32[]{:S(2)}, u32[]{:S(2)}) %collective-permute-start.1) | collective-permute-done | bytes 65568 | tf_op jit(solution)/shard_map/ppermute | solution.py:765
  13.3 5.5 %collective-permute-start.2 = (f32[6,8,256]{2,1,0:T(8,128)S(1)}, f32[6,8,256]{2,1,0:T(8,128)S(1)}, u32[]{:S(2)}, u32[]{:S(2)}) collective-permute-start(f32[6,8,256]{2,1,0:T(8,128)S(1)} %get-tuple-element.38), channel_id=1, source_target_pairs={{0,1},{1,2},{2,3},{3,4},{4,5},{5,6},{6,7},{7,8},{8,9},{9,10},{10,1... | collective-permute-start | bytes 147464 | tf_op jit(solution)/shard_map/ppermute | solution.py:765
  18.8 1.9 %collective-permute-start.3 = (f32[6,8,256]{2,1,0:T(8,128)S(1)}, f32[6,8,256]{2,1,0:T(8,128)S(1)}, u32[]{:S(2)}, u32[]{:S(2)}) collective-permute-start(f32[6,8,256]{2,1,0:T(8,128)S(1)} %get-tuple-element.39), channel_id=1, source_target_pairs={{1,0},{2,1},{3,2},{4,3},{5,4},{6,5},{7,6},{8,7},{9,8},{10,9},{11,1... | collective-permute-start | bytes 147464 | tf_op jit(solution)/shard_map/ppermute | solution.py:765
  20.8 0.0 copy-start.4
  20.8 0.8 copy-done.4
  21.6 0.7 copy-done.9
  22.3 1.4 couplings.1
  23.7 1.6 copy-done
  25.3 1.2 copy-done.1
  26.5 4.8 %upward.1 = (bf16[3,64,8192]{2,1,0:T(8,128)(2,1)S(1)}, f32[8,128]{1,0:T(8,128)S(1)}) custom-call(f32[4,8192]{1,0:T(4,128)S(1)} %get-tuple-element.42.r_ref, f32[32,64,256]{2,1,0:T(8,128)S(1)} %bitcast.6, f32[32,64,64]{2,1,0:T(8,128)S(1)} %bitcast.7), custom_call_target="tpu_custom_call" | custom-call | tf_op jit(solution)/shard_map/upward/pallas_call | solution.py:446
  31.4 0.0 collective-permute-done.2.left_ref
  31.4 0.0 collective-permute-done.3.right_ref
  31.4 0.0 copy-done.6
  31.4 0.0 copy-done.7
  31.4 3.6 %geometry.1 = (bf16[60,256,32]{2,1,0:T(8,128)(2,1)S(1)}, bf16[60,32,256]{2,1,0:T(8,128)(2,1)S(1)}) custom-call(f32[32,8,256]{2,1,0:T(8,128)S(1)} %get-tuple-element.35.own_ref, f32[8,8,256]{2,1,0:T(8,128)S(1)} %collective-permute-done.up_ref, f32[8,8,256]{2,1,0:T(8,128)S(1)} %collective-permute-done.1.down_ref, ...), custom_call_target="tpu_custom_call" | custom-call | tf_op jit(solution)/shard_map/geometry/pallas_call | solution.py:207
  35.0 0.0 copy-done.2
  35.0 0.0 copy-done.5
  35.0 25.5 %near_build.1 = (f32[4,8192]{1,0:T(4,128)S(1)}, s32[312]{0:T(512)S(1)}, bf16[38,8,2,256,256]{4,3,2,1,0:T(8,128)(2,1)}, f32[16,8,128]{2,1,0:T(8,128)S(1)}) custom-call(s32[4,8,9]{2,1,0:T(8,128)S(1)} %copy-done.5, f32[32,8,256]{2,1,0:T(8,128)S(1)} %get-tuple-element.35.own_ref, f32[8,8,256]{2,1,0:T(8,128)S(1)} %collective-permute-done.up_ref, ...), custom_call_target="tpu_custom_call" | custom-call | tf_op jit(solution)/shard_map/near_build/pallas_call | solution.py:327
  60.5 20.0 %all_to_all.20.c_ref = f32[16,8,128]{2,1,0:T(8,128)S(1)} all-to-all(f32[16,8,128]{2,1,0:T(8,128)S(1)} %get-tuple-element.47), channel_id=1, replica_groups=mesh['gx'=16,'gy'=16] {'gy'}, dimensions={0} | all-to-all | bytes 131072 | tf_op jit(solution)/shard_map/all_to_all | solution.py:775
  80.5 0.8 row_tree.2
  81.3 18.2 %all_to_all.21.x_ref = f32[16,8,128]{2,1,0:T(8,128)S(1)} all-to-all(f32[16,8,128]{2,1,0:T(8,128)S(1)} %get-tuple-element.49), channel_id=1, replica_groups=mesh['gx'=16,'gy'=16] {'gx'}, dimensions={0} | all-to-all | bytes 131072 | tf_op jit(solution)/shard_map/all_to_all | solution.py:775
  99.5 2.7 %middle.1 = (f32[4,8192]{1,0:T(4,128)S(1)}, f32[32,4,256]{2,1,0:T(4,128)S(1)}, f32[8,4,256]{2,1,0:T(4,128)S(1)}, f32[8,4,256]{2,1,0:T(4,128)S(1)}, f32[8,128]{1,0:T(8,128)S(1)}) custom-call(f32[16,8,128]{2,1,0:T(8,128)S(1)} %all_to_all.21.x_ref, f32[8,64]{1,0:T(8,128)S(1)} %get-tuple-element.50.y_ref, f32[2,64,64]{2,1,0:T(8,128)S(1)} %get-tuple-element.48.upper_ref, ...), custom_call_target="tpu_custom_call" | custom-call | tf_op jit(solution)/shard_map/middle/pallas_call | solution.py:626
  102.2 2.3 %collective-permute-start.4 = (f32[8,4,256]{2,1,0:T(4,128)S(1)}, f32[8,4,256]{2,1,0:T(4,128)S(1)}, u32[]{:S(2)}, u32[]{:S(2)}) collective-permute-start(f32[8,4,256]{2,1,0:T(4,128)S(1)} %get-tuple-element.55), channel_id=1, source_target_pairs={{0,16},{16,32},{32,48},{48,64},{64,80},{80,96},{96,112},{112,128},... | collective-permute-start | bytes 98312 | tf_op jit(solution)/shard_map/ppermute | solution.py:765
  104.5 1.3 collective-permute-start.5
  105.8 0.0 collective-permute-done.4.up_ref
  105.8 3.3 %collective-permute-done.5.down_ref = f32[8,4,256]{2,1,0:T(4,128)S(1)} collective-permute-done((f32[8,4,256]{2,1,0:T(4,128)S(1)}, f32[8,4,256]{2,1,0:T(4,128)S(1)}, u32[]{:S(2)}, u32[]{:S(2)}) %collective-permute-start.5) | collective-permute-done | bytes 32800 | tf_op jit(solution)/shard_map/ppermute | solution.py:765
  109.1 5.0 %collective-permute-start.6 = (f32[6,4,256]{2,1,0:T(4,128)S(1)}, f32[6,4,256]{2,1,0:T(4,128)S(1)}, u32[]{:S(2)}, u32[]{:S(2)}) collective-permute-start(f32[6,4,256]{2,1,0:T(4,128)S(1)} %get-tuple-element.57), channel_id=1, source_target_pairs={{0,1},{1,2},{2,3},{3,4},{4,5},{5,6},{6,7},{7,8},{8,9},{9,10},{10,1... | collective-permute-start | bytes 73736 | tf_op jit(solution)/shard_map/ppermute | solution.py:765
  114.2 1.9 %collective-permute-start.7 = (f32[6,4,256]{2,1,0:T(4,128)S(1)}, f32[6,4,256]{2,1,0:T(4,128)S(1)}, u32[]{:S(2)}, u32[]{:S(2)}) collective-permute-start(f32[6,4,256]{2,1,0:T(4,128)S(1)} %get-tuple-element.58), channel_id=1, source_target_pairs={{1,0},{2,1},{3,2},{4,3},{5,4},{6,5},{7,6},{8,7},{9,8},{10,9},{11,1... | collective-permute-start | bytes 73736 | tf_op jit(solution)/shard_map/ppermute | solution.py:765
  116.1 0.0 collective-permute-done.6.left_ref
  116.1 3.2 %collective-permute-done.7.right_ref = f32[6,4,256]{2,1,0:T(4,128)S(1)} collective-permute-done((f32[6,4,256]{2,1,0:T(4,128)S(1)}, f32[6,4,256]{2,1,0:T(4,128)S(1)}, u32[]{:S(2)}, u32[]{:S(2)}) %collective-permute-start.7) | collective-permute-done | bytes 24608 | tf_op jit(solution)/shard_map/ppermute | solution.py:765
  119.3 12.9 %near_reuse.1 = (f32[4,8192]{1,0:T(4,128)S(1)}, f32[16,8,128]{2,1,0:T(8,128)S(1)}) custom-call(s32[312]{0:T(512)S(1)} %get-tuple-element.46.list_ref, f32[32,4,256]{2,1,0:T(4,128)S(1)} %get-tuple-element.54.own_ref, f32[8,4,256]{2,1,0:T(4,128)S(1)} %collective-permute-done.4.up_ref, f32[8,4,256]{2,1,0:T(4,128)S(1)} %collective-permute-done.5.down_ref, ...), custom_call_target="tpu_custom_call" | custom-call | tf_op jit(solution)/shard_map/near_reuse/pallas_call | solution.py:409
  132.2 12.8 %all_to_all.22.c_ref = f32[16,8,128]{2,1,0:T(8,128)S(1)} all-to-all(f32[16,8,128]{2,1,0:T(8,128)S(1)} %get-tuple-element.61), channel_id=1, replica_groups=mesh['gx'=16,'gy'=16] {'gy'}, dimensions={0} | all-to-all | bytes 131072 | tf_op jit(solution)/shard_map/all_to_all | solution.py:775
  145.0 0.9 row_tree.3
  145.9 15.8 %all_to_all.23.c_ref = f32[16,8,128]{2,1,0:T(8,128)S(1)} all-to-all(f32[16,8,128]{2,1,0:T(8,128)S(1)} %get-tuple-element.62), channel_id=1, replica_groups=mesh['gx'=16,'gy'=16] {'gx'}, dimensions={0} | all-to-all | bytes 131072 | tf_op jit(solution)/shard_map/all_to_all | solution.py:775
  161.7 4.3 %final.1 = (f32[32,4,256]{2,1,0:T(4,128)}, f32[32,4,256]{2,1,0:T(4,128)}) custom-call(f32[16,8,128]{2,1,0:T(8,128)S(1)} %all_to_all.23.c_ref, f32[8,64]{1,0:T(8,128)S(1)} %get-tuple-element.63.y_ref, f32[2,64,64]{2,1,0:T(8,128)S(1)} %get-tuple-element.48.upper_ref, f32[7,64,64]{2,1,0:T(8,128)S(1)} %get-tuple-element.44.g_ref, ...), custom_call_target="tpu_custom_call" | custom-call | tf_op jit(solution)/shard_map/final/pallas_call | solution.py:750
  (5 shorter events, 0.0 us)
Async XLA Ops:
  0.6 30.8 %copy-start.6 = (bf16[32,24]{1,0:T(8,128)(2,1)S(1)}, bf16[32,24]{1,0:T(8,128)(2,1)}, u32[]{:S(2)}) copy-start(bf16[32,24]{1,0:T(8,128)(2,1)} %constant.8.clone.source_ref) | copy-start | bytes 4612
  0.6 30.8 %copy-start.7 = (bf16[32,24]{1,0:T(8,128)(2,1)S(1)}, bf16[32,24]{1,0:T(8,128)(2,1)}, u32[]{:S(2)}) copy-start(bf16[32,24]{1,0:T(8,128)(2,1)} %constant.7.clone.target_ref) | copy-start | bytes 4612
  0.7 34.4 %copy-start.2 = (bf16[9,32,256]{2,1,0:T(8,128)(2,1)S(1)}, bf16[9,32,256]{2,1,0:T(8,128)(2,1)}, u32[]{:S(2)}) copy-start(bf16[9,32,256]{2,1,0:T(8,128)(2,1)} %constant.6.clone.factor_ref) | copy-start | bytes 442372
  0.7 34.4 %copy-start.5 = (s32[4,8,9]{2,1,0:T(8,128)S(1)}, s32[4,8,9]{2,1,0:T(8,128)}, u32[]{:S(2)}) copy-start(s32[4,8,9]{2,1,0:T(8,128)} %mask_ref.1) | copy-start | bytes 3460
  1.7 0.9 copy-start.3
  2.6 0.7 copy-start.8
  4.3 5.3 %collective-permute-start = (f32[8,8,256]{2,1,0:T(8,128)S(1)}, f32[8,8,256]{2,1,0:T(8,128)S(1)}, u32[]{:S(2)}, u32[]{:S(2)}) collective-permute-start(f32[8,8,256]{2,1,0:T(8,128)S(1)} %get-tuple-element.36), channel_id=1, source_target_pairs={{0,16},{16,32},{32,48},{48,64},{64,80},{80,96},{96,112},{112,128},... | collective-permute-start | bytes 196616 | tf_op jit(solution)/shard_map/ppermute | solution.py:765
  8.3 5.0 %collective-permute-start.1 = (f32[8,8,256]{2,1,0:T(8,128)S(1)}, f32[8,8,256]{2,1,0:T(8,128)S(1)}, u32[]{:S(2)}, u32[]{:S(2)}) collective-permute-start(f32[8,8,256]{2,1,0:T(8,128)S(1)} %get-tuple-element.37), channel_id=1, source_target_pairs={{16,0},{32,16},{48,32},{64,48},{80,64},{96,80},{112,96},{128,112},... | collective-permute-start | bytes 196616 | tf_op jit(solution)/shard_map/ppermute | solution.py:765
  13.3 18.1 %collective-permute-start.2 = (f32[6,8,256]{2,1,0:T(8,128)S(1)}, f32[6,8,256]{2,1,0:T(8,128)S(1)}, u32[]{:S(2)}, u32[]{:S(2)}) collective-permute-start(f32[6,8,256]{2,1,0:T(8,128)S(1)} %get-tuple-element.38), channel_id=1, source_target_pairs={{0,1},{1,2},{2,3},{3,4},{4,5},{5,6},{6,7},{7,8},{8,9},{9,10},{10,1... | collective-permute-start | bytes 147464 | tf_op jit(solution)/shard_map/ppermute | solution.py:765
  18.8 12.5 %collective-permute-start.3 = (f32[6,8,256]{2,1,0:T(8,128)S(1)}, f32[6,8,256]{2,1,0:T(8,128)S(1)}, u32[]{:S(2)}, u32[]{:S(2)}) collective-permute-start(f32[6,8,256]{2,1,0:T(8,128)S(1)} %get-tuple-element.39), channel_id=1, source_target_pairs={{1,0},{2,1},{3,2},{4,3},{5,4},{6,5},{7,6},{8,7},{9,8},{10,9},{11,1... | collective-permute-start | bytes 147464 | tf_op jit(solution)/shard_map/ppermute | solution.py:765
  20.8 0.8 copy-start.4
  21.6 0.7 copy-start.9
  23.7 1.6 copy-start
  25.3 1.2 copy-start.1
  102.2 3.6 %collective-permute-start.4 = (f32[8,4,256]{2,1,0:T(4,128)S(1)}, f32[8,4,256]{2,1,0:T(4,128)S(1)}, u32[]{:S(2)}, u32[]{:S(2)}) collective-permute-start(f32[8,4,256]{2,1,0:T(4,128)S(1)} %get-tuple-element.55), channel_id=1, source_target_pairs={{0,16},{16,32},{32,48},{48,64},{64,80},{80,96},{96,112},{112,128},... | collective-permute-start | bytes 98312 | tf_op jit(solution)/shard_map/ppermute | solution.py:765
  104.5 4.7 %collective-permute-start.5 = (f32[8,4,256]{2,1,0:T(4,128)S(1)}, f32[8,4,256]{2,1,0:T(4,128)S(1)}, u32[]{:S(2)}, u32[]{:S(2)}) collective-permute-start(f32[8,4,256]{2,1,0:T(4,128)S(1)} %get-tuple-element.56), channel_id=1, source_target_pairs={{16,0},{32,16},{48,32},{64,48},{80,64},{96,80},{112,96},{128,112},... | collective-permute-start | bytes 98312 | tf_op jit(solution)/shard_map/ppermute | solution.py:765
  109.1 7.0 %collective-permute-start.6 = (f32[6,4,256]{2,1,0:T(4,128)S(1)}, f32[6,4,256]{2,1,0:T(4,128)S(1)}, u32[]{:S(2)}, u32[]{:S(2)}) collective-permute-start(f32[6,4,256]{2,1,0:T(4,128)S(1)} %get-tuple-element.57), channel_id=1, source_target_pairs={{0,1},{1,2},{2,3},{3,4},{4,5},{5,6},{6,7},{7,8},{8,9},{9,10},{10,1... | collective-permute-start | bytes 73736 | tf_op jit(solution)/shard_map/ppermute | solution.py:765
  114.2 5.1 %collective-permute-start.7 = (f32[6,4,256]{2,1,0:T(4,128)S(1)}, f32[6,4,256]{2,1,0:T(4,128)S(1)}, u32[]{:S(2)}, u32[]{:S(2)}) collective-permute-start(f32[6,4,256]{2,1,0:T(4,128)S(1)} %get-tuple-element.58), channel_id=1, source_target_pairs={{1,0},{2,1},{3,2},{4,3},{5,4},{6,5},{7,6},{8,7},{9,8},{10,9},{11,1... | collective-permute-start | bytes 73736 | tf_op jit(solution)/shard_map/ppermute | solution.py:765

commit v3 on v2

--- a/solution.py
+++ b/solution.py
@@ -19,7 +19,7 @@
 GROUP = 8
 CHUNK = 64
 BUILD_SLOTS = 2
-READ_SLOTS = 4
+READ_SLOTS = 6
 VMEM_LIMIT = 20 * 2**20
 VM = pl.BlockSpec(memory_space=pltpu.VMEM)
 ANY = pl.BlockSpec(memory_space=pl.ANY)
@@ -119,14 +119,14 @@
 
 
 def pack_kernel(nx, ny, count_ref, points_ref, sides_ref, packed_ref, top_ref, bottom_ref, r_ref, valid_ref):
-    size = points_ref.shape[2]
-    row = lax.broadcasted_iota(jnp.int32, (3, size), 0)
+    size = points_ref.shape[3]
     lane = lax.broadcasted_iota(jnp.int32, (1, size), 1)
 
     def body(a, carry):
         first = (lax.axis_index("gx") * nx + a // ny).astype(F32) + 0.5
         second = (lax.axis_index("gy") * ny + a % ny).astype(F32) + 0.5
-        packed_ref[a, 0:3] = points_ref[a] - jnp.where(row == 0, first, jnp.where(row == 1, second, 0.5))
+        for c, centre in enumerate((first, second, 0.5)):
+            packed_ref[a, c : c + 1] = points_ref[a // ny, c, pl.ds(a % ny, 1)] - centre
         count = count_ref[a // ny, a % ny]
         packed_ref[a, 3:4] = jnp.full((1, size), count.astype(F32))
         valid = jnp.where(lane < count, 1.0, 0.0)
@@ -143,7 +143,7 @@
 
 
 def pack(nx, ny, counts, points, sides):
-    leaves, _, size = points.shape
+    leaves, _, size = sides.shape
     return pl.pallas_call(
         functools.partial(pack_kernel, nx, ny),
         out_shape=[
@@ -160,7 +160,7 @@
     )(counts, points, sides)
 
 
-def sides_kernel(nx, ny, own_ref, up_ref, down_ref, left_ref, right_ref):
+def sides_kernel(nx, ny, own_ref, up_ref, down_ref, after_ref, left_ref, right_ref):
     for col, ref in ((0, left_ref), (ny - 1, right_ref)):
         ref[0] = up_ref[col]
         ref[nx + 1] = down_ref[col]
@@ -168,23 +168,36 @@
             ref[i + 1] = own_ref[i * ny + col]
 
 
-def side_columns(nx, ny, own, up, down):
+def side_columns(nx, ny, own, up, down, after):
     out = jax.ShapeDtypeStruct((nx + 2,) + own.shape[1:], F32)
     return pl.pallas_call(
         functools.partial(sides_kernel, nx, ny),
         out_shape=[out, out],
-        in_specs=[VM] * 3,
+        in_specs=[VM] * 3 + [ANY],
         out_specs=[VM] * 2,
         compiler_params=params(),
         name="side_columns",
-    )(own, up, down)
-
-
-def geometry_kernel(nx, ny, own_ref, up_ref, down_ref, left_ref, right_ref, target_ref, source_ref, s_ref, t_ref):
-    row = lax.broadcasted_iota(jnp.int32, (8, own_ref.shape[2]), 0)
-
-    def body(e, ref, i):
-        x = jnp.where(row < 3, ref[i], 0.0)
+    )(own, up, down, after)
+
+
+def geometry_kernel(
+    nx, ny, mask_ref, own_ref, up_ref, down_ref, left_ref, right_ref, target_ref, source_ref, c_ref, after_ref,
+    s_ref, t_ref, v_ref, long_ref, short_ref, groups_ref, out_ref, count_ref,
+):
+    wide = ny + 2
+    leaves = (nx + 2) * wide
+    size = own_ref.shape[2]
+    row = lax.broadcasted_iota(jnp.int32, (8, size), 0)
+    refs = (own_ref, up_ref, down_ref, left_ref, right_ref)
+
+    def read_count(e, ref, i):
+        count_ref[e] = ref[i, 3, 0].astype(jnp.int32)
+
+    each_leaf(nx, ny, refs, read_count)
+
+    def features(e, ref, i):
+        packed = ref[i]
+        x = jnp.where(row < 3, packed, 0.0)
         first = rounded(x)
         second = rounded(x - first)
         held = first + second
@@ -198,96 +211,116 @@
         s_ref[e] = lax.dot_general(
             f, source_ref[...], (((0,), (1,)), ((), ())), preferred_element_type=F32
         ).astype(BF)
-
-    each_leaf(nx, ny, (own_ref, up_ref, down_ref, left_ref, right_ref), body, 8)
-
-
-def geometry(nx, ny, parts, target_table, source_table):
-    leaves, size = (nx + 2) * (ny + 2), parts[0].shape[2]
-    return pl.pallas_call(
-        functools.partial(geometry_kernel, nx, ny),
-        out_shape=[
-            jax.ShapeDtypeStruct((leaves, size, 32), BF),
-            jax.ShapeDtypeStruct((leaves, 32, size), BF),
-        ],
-        in_specs=[VM] * 7,
-        out_specs=[VM] * 2,
-        compiler_params=params(),
-        name="geometry",
-    )(*parts, jnp.asarray(target_table, BF), jnp.asarray(source_table, BF))
-
-
-def build_kernel(
-    nx, ny, mask_ref, own_ref, up_ref, down_ref, left_ref, right_ref, s_ref, t_ref, factor_ref, c_ref, g_ref, b_ref,
-    o_ref, list_ref, cache_ref, out_ref, v16, acc, spare, count_ref, buffer, sems,
-):
-    wide = ny + 2
-    leaves = (nx + 2) * wide
-    size = own_ref.shape[2]
-    short = size - CHUNK
-
-    def split_leaf(e, ref, i):
-        v16[e] = rows16(ref[i, 4:8])
-        count_ref[e] = ref[i, 3, 0].astype(jnp.int32)
-
-    each_leaf(nx, ny, (own_ref, up_ref, down_ref, left_ref, right_ref), split_leaf)
-    v16[leaves] = jnp.zeros((16, size), BF)
-    acc[...] = jnp.zeros_like(acc)
-    for slot in range(BUILD_SLOTS):
-        for j in range(GROUP):
-            buffer[slot, j, :, short:size] = jnp.zeros((2, CHUNK, size), BF)
-    dummy = leaves * 1024
+        v_ref[e] = rows16(packed[4:8])
 
     def note(a, carry):
-        full, less = carry
+        features((a // ny + 1) * wide + a % ny + 1, own_ref, a)
+        long_count, short_count = carry
         corner = (a // ny) * wide + a % ny
         for code in range(9):
             source = corner + code // 3 * wide + code % 3
             entry = (source * 16 + code) * 64 + a
             on = jnp.where(mask_ref[a // ny, a % ny, code] != 0, 1, 0)
-            long = jnp.where(count_ref[source] > short, on, 0)
-            list_ref[full] = entry
-            spare[less] = entry
-            full = full + long
-            less = less + (on - long)
-        return full, less
-
-    full, less = lax.fori_loop(0, nx * ny, note, (0, 0), unroll=2)
+            is_long = jnp.where(count_ref[source] > size - CHUNK, on, 0)
+            long_ref[long_count] = entry
+            short_ref[short_count] = entry
+            long_count = long_count + is_long
+            short_count = short_count + (on - is_long)
+        return long_count, short_count
+
+    long_count, short_count = lax.fori_loop(0, nx * ny, note, (0, 0), unroll=4)
     for j in range(GROUP):
-        list_ref[full + j] = dummy
-        spare[less + j] = dummy
-    full_groups = (full + GROUP - 1) // GROUP
-    less_groups = (less + GROUP - 1) // GROUP
-    groups = full_groups + less_groups
-
-    def move(k, carry):
-        list_ref[full_groups * GROUP + k] = spare[k]
-        return carry
-
-    lax.fori_loop(0, less_groups * GROUP, move, 0)
-    list_ref[list_ref.shape[0] - 1] = groups
-
-    def copy_out(g):
-        slot = g % BUILD_SLOTS
-        return pltpu.make_async_copy(buffer.at[slot], cache_ref.at[g], sems.at[slot])
-
-    def run(first, last, rows):
+        long_ref[long_count + j] = leaves * 1024
+        short_ref[short_count + j] = leaves * 1024
+    groups_ref[0] = (long_count + GROUP - 1) // GROUP
+    groups_ref[1] = (short_count + GROUP - 1) // GROUP
+    for ref, (count, place) in list(zip(refs, around(nx, ny)))[1:]:
+
+        def step(i, carry, ref=ref, place=place):
+            features(place(i), ref, i)
+            return carry
+
+        lax.fori_loop(0, count, step, 0, unroll=True)
+    v_ref[leaves] = jnp.zeros((16, size), BF)
+    for i in range(out_ref.shape[0]):
+        out_ref[i] = c_ref[...]
+
+
+def geometry(nx, ny, mask, parts, target_table, source_table, c, after, copies):
+    leaves, size = (nx + 2) * (ny + 2), parts[0].shape[2]
+    most = nx * ny * 9 + GROUP
+    return pl.pallas_call(
+        functools.partial(geometry_kernel, nx, ny),
+        out_shape=[
+            jax.ShapeDtypeStruct((leaves, size, 32), BF),
+            jax.ShapeDtypeStruct((leaves, 32, size), BF),
+            jax.ShapeDtypeStruct((leaves + 1, 16, size), BF),
+            jax.ShapeDtypeStruct((most,), jnp.int32),
+            jax.ShapeDtypeStruct((most,), jnp.int32),
+            jax.ShapeDtypeStruct((2,), jnp.int32),
+            jax.ShapeDtypeStruct((copies, 8, 128), F32),
+        ],
+        in_specs=[SM] + [VM] * 8 + [ANY],
+        out_specs=[VM] * 3 + [SM] * 3 + [VM],
+        scratch_shapes=[pltpu.SMEM((leaves,), jnp.int32)],
+        compiler_params=params(),
+        name="geometry",
+    )(mask, *parts, jnp.asarray(target_table, BF), jnp.asarray(source_table, BF), c, after)
+
+
+def block_copy(buffer, cache_ref, sems, slots, rows, inward):
+    def copy(g):
+        slot = g % slots
+        here, there = buffer.at[slot], cache_ref.at[g]
+        if rows < cache_ref.shape[3]:
+            here, there = here.at[:, :, 0:rows], there.at[:, :, 0:rows]
+        if inward:
+            return pltpu.make_async_copy(there, here, sems.at[slot])
+        return pltpu.make_async_copy(here, there, sems.at[slot])
+
+    return copy
+
+
+def build_kernel(
+    nx, ny, long_ref, short_ref, groups_ref, v_ref, s_ref, t_ref, factor_ref, after_ref,
+    o_ref, cache_ref, acc, buffer, sems,
+):
+    wide = ny + 2
+    leaves = (nx + 2) * wide
+    size = o_ref.shape[1] // (nx * ny)
+    short = size - CHUNK
+    acc[...] = jnp.zeros_like(acc)
+    long_groups = groups_ref[0]
+    groups = long_groups + groups_ref[1]
+    out_long = block_copy(buffer, cache_ref, sems, BUILD_SLOTS, size, False)
+    out_short = block_copy(buffer, cache_ref, sems, BUILD_SLOTS, short, False)
+
+    def wait(g):
+        @pl.when(g < long_groups)
+        def _():
+            out_long(g).wait()
+
+        @pl.when(g >= long_groups)
+        def _():
+            out_short(g).wait()
+
+    def run(first, last, rows, list_ref, start):
         def group(g, carry):
             slot = g % BUILD_SLOTS
 
             @pl.when(g >= BUILD_SLOTS)
             def _():
-                copy_out(g - BUILD_SLOTS).wait()
+                wait(g - BUILD_SLOTS)
 
             done = []
             for j in range(GROUP):
-                entry = list_ref[g * GROUP + j]
+                entry = list_ref[(g - first) * GROUP + j]
                 a = entry & 63
                 code = (entry >> 6) & 15
                 source = entry >> 10
                 t = t_ref[(a // ny + 1) * wide + a % ny + 1] * factor_ref[code]
                 s = s_ref[jnp.minimum(source, leaves - 1)]
-                v = v16[source]
+                v = v_ref[source]
                 total = jnp.zeros((16, size), F32)
                 for k in range(rows // CHUNK):
                     part = slice(k * CHUNK, (k + 1) * CHUNK)
@@ -301,67 +334,68 @@
                 done.append((a, total))
             for a, total in done:
                 acc[a] += total
-            copy_out(g).start()
+            start(g).start()
             return carry
 
         lax.fori_loop(first, last, group, 0)
 
-    run(0, full_groups, size)
-    run(full_groups, groups, short)
+    run(0, long_groups, size, long_ref, out_long)
+    run(long_groups, groups, short, short_ref, out_short)
     for back in range(BUILD_SLOTS):
-        copy_out(groups - 1 - back).wait()
+        wait(groups - 1 - back)
 
     def finish(a, carry):
         o_ref[:, pl.ds(pl.multiple_of(a * size, size), size)] = join16(acc[a]) * (1.0 / size**0.5)
         return carry
 
     lax.fori_loop(0, nx * ny, finish, 0, unroll=4)
-    for i in range(out_ref.shape[0]):
-        out_ref[i] = c_ref[...]
-
-
-def near_build(nx, ny, mask, parts, s, t, factor, c, g, b, copies):
-    size = parts[0].shape[2]
-    leaves = (nx + 2) * (ny + 2)
-    most = nx * ny * 9 + 2 * GROUP
+
+
+def near_build(nx, ny, lists, v, s, t, factor, after):
+    size = v.shape[2]
+    most = lists[0].shape[0] // GROUP + 1
     return pl.pallas_call(
         functools.partial(build_kernel, nx, ny),
         out_shape=[
             jax.ShapeDtypeStruct((4, nx * ny * size), F32),
-            jax.ShapeDtypeStruct((most + 8,), jnp.int32),
-            jax.ShapeDtypeStruct((most // GROUP, GROUP, 2, size, size), BF),
-            jax.ShapeDtypeStruct((copies, 8, 128), F32),
+            jax.ShapeDtypeStruct((most, GROUP, 2, size, size), BF),
         ],
-        in_specs=[SM] + [VM] * 9 + [ANY] * 2,
-        out_specs=[VM, SM, ANY, VM],
+        in_specs=[SM] * 3 + [VM] * 4 + [ANY],
+        out_specs=[VM, ANY],
         scratch_shapes=[
-            pltpu.VMEM((leaves + 1, 16, size), BF),
             pltpu.VMEM((nx * ny, 16, size), F32),
-            pltpu.SMEM((most,), jnp.int32),
-            pltpu.SMEM((leaves,), jnp.int32),
             pltpu.VMEM((BUILD_SLOTS, GROUP, 2, size, size), BF),
             pltpu.SemaphoreType.DMA((BUILD_SLOTS,)),
         ],
         compiler_params=params(),
         name="near_build",
-    )(mask, *parts, s, t, factor, c, g, b)
+    )(*lists, v, s, t, factor, after)
 
 
 def reuse_kernel(
-    nx, ny, list_ref, own_ref, up_ref, down_ref, left_ref, right_ref, c_ref, cache_ref,
+    nx, ny, long_ref, short_ref, groups_ref, own_ref, up_ref, down_ref, left_ref, right_ref, c_ref, cache_ref,
     o_ref, out_ref, v16, acc, buffer, sems,
 ):
     wide = ny + 2
     leaves = (nx + 2) * wide
     size = own_ref.shape[2]
-    groups = list_ref[list_ref.shape[0] - 1]
-
-    def copy_in(g):
-        slot = g % READ_SLOTS
-        return pltpu.make_async_copy(cache_ref.at[g], buffer.at[slot], sems.at[slot])
+    short = size - CHUNK
+    long_groups = groups_ref[0]
+    groups = long_groups + groups_ref[1]
+    in_long = block_copy(buffer, cache_ref, sems, READ_SLOTS, size, True)
+    in_short = block_copy(buffer, cache_ref, sems, READ_SLOTS, short, True)
+
+    def fetch(g):
+        @pl.when(g < long_groups)
+        def _():
+            in_long(g).start()
+
+        @pl.when(jnp.logical_and(g >= long_groups, g < groups))
+        def _():
+            in_short(g).start()
 
     for g in range(READ_SLOTS - 1):
-        copy_in(g).start()
+        fetch(g)
 
     def split_leaf(e, ref, i):
         v16[e] = rows16(ref[i])
@@ -370,24 +404,24 @@
     v16[leaves] = jnp.zeros((16, size), BF)
     acc[...] = jnp.zeros_like(acc)
 
-    def group(g, carry):
-        slot = g % READ_SLOTS
-        copy_in(g).wait()
-
-        @pl.when(g + READ_SLOTS - 1 < groups)
-        def _():
-            copy_in(g + READ_SLOTS - 1).start()
-
-        done = []
-        for j in range(GROUP):
-            entry = list_ref[g * GROUP + j]
-            v = v16[entry >> 10]
-            done.append((entry & 63, dot(v, buffer[slot, j, 0]) + dot(v, buffer[slot, j, 1])))
-        for a, total in done:
-            acc[a] += total
-        return carry
-
-    lax.fori_loop(0, groups, group, 0)
+    def run(first, last, rows, list_ref, copy):
+        def group(g, carry):
+            slot = g % READ_SLOTS
+            copy(g).wait()
+            fetch(g + READ_SLOTS - 1)
+            done = []
+            for j in range(GROUP):
+                entry = list_ref[(g - first) * GROUP + j]
+                v = v16[entry >> 10][:, 0:rows]
+                done.append((entry & 63, dot(v, buffer[slot, j, 0, 0:rows]) + dot(v, buffer[slot, j, 1, 0:rows])))
+            for a, total in done:
+                acc[a] += total
+            return carry
+
+        lax.fori_loop(first, last, group, 0)
+
+    run(0, long_groups, size, long_ref, in_long)
+    run(long_groups, groups, short, short_ref, in_short)
 
     def finish(a, sums):
         near = join16(acc[a]) * (1.0 / size**0.5)
@@ -403,13 +437,13 @@
         out_ref[i] = total
 
 
-def near_reuse(nx, ny, todo, parts, c, cache, copies):
+def near_reuse(nx, ny, lists, parts, c, cache, copies):
     size = parts[0].shape[2]
     leaves = (nx + 2) * (ny + 2)
     return pl.pallas_call(
         functools.partial(reuse_kernel, nx, ny),
         out_shape=[jax.ShapeDtypeStruct((4, nx * ny * size), F32), jax.ShapeDtypeStruct((copies, 8, 128), F32)],
-        in_specs=[SM] + [VM] * 6 + [ANY],
+        in_specs=[SM] * 3 + [VM] * 6 + [ANY],
         out_specs=[VM] * 2,
         scratch_shapes=[
             pltpu.VMEM((leaves + 1, 16, size), BF),
@@ -419,7 +453,7 @@
         ],
         compiler_params=params(),
         name="near_reuse",
-    )(todo, *parts, c, cache)
+    )(*lists, *parts, c, cache)
 
 
 def upward_kernel(r_ref, basis_ref, transfer_ref, joint_ref, c_ref):
@@ -427,18 +461,15 @@
 
     def body(a, total):
         part = pl.ds(pl.multiple_of(a * size, size), size)
-        joint = exact_dot(transfer_ref[a], basis_ref[a])
-        terms3 = split3(joint)
         v = rows16(r_ref[:, part])
-        for k, term in enumerate(terms3):
-            joint_ref[k, :, part] = term
-            total = total + dot_nt(v, term)
+        for term, piece in enumerate(split3(exact_dot(transfer_ref[a], basis_ref[a]))):
+            joint_ref[term, :, part] = piece
+            total = total + dot_nt(v, piece)
         return total
 
-    total = join16(lax.fori_loop(0, leaves, body, jnp.zeros((16, terms), F32), unroll=8))
-    total = jnp.concatenate([total, jnp.zeros((4, 128 - terms), F32)], axis=1)
-    total = jnp.concatenate([total, jnp.zeros((4, 128), F32)], axis=0)
-    c_ref[...] = total
+    total = lax.fori_loop(0, leaves, body, jnp.zeros((16, terms), F32), unroll=8)
+    total = jnp.concatenate([join16(total), jnp.zeros((4, 128 - terms), F32)], axis=1)
+    c_ref[...] = jnp.concatenate([total, jnp.zeros((4, 128), F32)], axis=0)
 
 
 def upward(r, basis, transfer):
@@ -582,7 +613,7 @@
     return y[0:4], sums
 
 
-SPLITS = 8
+SPLITS = 4
 
 
 def far_of(y, joint_ref, part):
@@ -765,9 +796,9 @@
     return lax.ppermute(last, axis, up), lax.ppermute(first, axis, down)
 
 
-def edges(nx, ny, own, top, bottom):
+def edges(nx, ny, own, top, bottom, after):
     up, down = swap("gx", top, bottom)
-    left, right = swap("gy", *side_columns(nx, ny, own, up, down))
+    left, right = swap("gy", *side_columns(nx, ny, own, up, down, after))
     return own, up, down, left, right
 
 
@@ -786,17 +817,16 @@
     def flat(x):
         return x.reshape((leaves,) + x.shape[2:])
 
-    packed, top, bottom, r, valid = pack(nx, ny, leaf_counts, flat(points), flat(right_sides))
-    parts = edges(nx, ny, packed, top, bottom)
+    packed, top, bottom, r, valid = pack(nx, ny, leaf_counts, jnp.swapaxes(points, 1, 2), flat(right_sides))
     joint, c = upward(r, flat(leaf_basis), flat(leaf_transfer))
+    parts = edges(nx, ny, packed, top, bottom, c)
     b, g, upper_t = couplings(levels, cols, (nx, ny), upper_transfer, proxy_nodes)
-    s, t = geometry(nx, ny, parts, target_table, source_table)
-    n, todo, cache, c = near_build(nx, ny, near_mask, parts, s, t, factor, c, g, b, cols)
+    s, t, v, *lists, c = geometry(nx, ny, near_mask, parts, target_table, source_table, c, b, cols)
     y, c = row_tree(False, exchange(c, "gy"), upper_t, g, b)
-    e, e_leaves, top, bottom, c = middle(
-        cols, levels, leaves, ny, exchange(c, "gx"), y, upper_t, g, joint, r, n, valid
-    )
-    n, c = near_reuse(nx, ny, todo, edges(nx, ny, e_leaves, top, bottom), c, cache, cols)
+    c = exchange(c, "gx")
+    n, cache = near_build(nx, ny, lists, v, s, t, factor, c)
+    e, e_leaves, top, bottom, c = middle(cols, levels, leaves, ny, c, y, upper_t, g, joint, r, n, valid)
+    n, c = near_reuse(nx, ny, lists, edges(nx, ny, e_leaves, top, bottom, c), c, cache, cols)
     y, c = row_tree(True, exchange(c, "gy"), upper_t, g, b)
     x, out = final(cols, levels, leaves, exchange(c, "gx"), y, upper_t, g, b, joint, r, e, n, valid)
     shape = (nx, ny, 4, size)

time: 166 us -> 156 us (0.940); the launches traced: 166 us -> 154 us
  blocking collectives: 66.8 us -> 57.2 us
  waiting for transfers between devices: 10.3 us -> 7.45 us
    all_to_all x4, blocking collectives: 66.8 us -> 57.2 us  [exchange(): return lax.all_to_all(x, axis, 0, 0, tiled=True)]
    ppermute x8, waiting for transfers between devices: 10.3 us -> 7.45 us  [swap(): return (lax.ppermute(last, axis, up), lax.ppermute(first, axis, down))]
    pallas_call x1, Pallas kernels: 25.5 us -> 23.5 us  [near_build(): pl.pallas_call(functools.partial(build_kernel, nx, ny), out_shape=[jax.Sh...]
    pallas_call x1, Pallas kernels: 3.59 us -> 5.53 us  [geometry(): pl.pallas_call(functools.partial(geometry_kernel, nx, ny), out_shape=[jax...]
    unnamed x21 -> x22, local copies, waits for them, and re-layouts: 6.93 us -> 6.71 us
where the time goes in v3:
time: 156 us; the launch traced here: 154 us
  blocking collectives  57.2 us (37%)
  Pallas kernels  57 us (37%)
  starting transfers between devices  24.6 us (16%)
  waiting for transfers between devices  7.45 us (5%)
  local copies, waits for them, and re-layouts  6.71 us (4%)
    all_to_all x4, blocking collectives, exchange(): return lax.all_to_all(x, axis, 0, 0, tiled=True)  57.2 us
    ppermute x8, starting transfers between devices, swap(): return (lax.ppermute(last, axis, up), lax.ppermute(first, axis, down))  24.6 us
    pallas_call x1, Pallas kernels, near_build(): pl.pallas_call(functools.partial(build_kernel, nx, ny), out_shape=[jax.Sh...  23.5 us
    pallas_call x1, Pallas kernels, near_reuse(): pl.pallas_call(functools.partial(reuse_kernel, nx, ny), out_shape=[jax.Sh...  12.5 us
    ppermute x8, waiting for transfers between devices, swap(): return (lax.ppermute(last, axis, up), lax.ppermute(first, axis, down))  7.45 us
    unnamed x22, local copies, waits for them, and re-layouts  6.71 us
    pallas_call x1, Pallas kernels, geometry(): pl.pallas_call(functools.partial(geometry_kernel, nx, ny), out_shape=[jax...  5.53 us
    pallas_call x1, Pallas kernels, upward(): pl.pallas_call(upward_kernel, out_shape=[jax.ShapeDtypeStruct((3, terms,...  4.82 us
  transfers between devices with their start and end apart: 8, of which 3 were waited for; matrix products, arithmetic and copies ran while one was open for 0% of the time, Pallas kernels for 4%

profile of v3, /device:TPU:1, one launch (start us, length us, event | category | flops | bytes accessed | tf_op | source)
XLA Modules:
  0.0 153.7 jit_solution(2472356987139438789)
XLA Ops:
  0.6 0.0 copy-start.2
  0.6 0.0 copy-start.3
  0.7 0.9 copy-done.3
  1.6 0.0 copy-start.4
  1.6 0.9 copy-done.4
  2.5 0.0 copy-start.9
  2.5 0.7 copy-done.9
  3.2 0.0 copy-start.5
  3.2 1.1 pack.1
  4.3 3.9 %collective-permute-start = (f32[8,8,256]{2,1,0:T(8,128)S(1)}, f32[8,8,256]{2,1,0:T(8,128)S(1)}, u32[]{:S(2)}, u32[]{:S(2)}) collective-permute-start(f32[8,8,256]{2,1,0:T(8,128)S(1)} %get-tuple-element.39), channel_id=1, source_target_pairs={{0,16},{16,32},{32,48},{48,64},{64,80},{80,96},{96,112},{112,128},... | collective-permute-start | bytes 196616 | tf_op jit(solution)/shard_map/ppermute | solution.py:796
  8.2 1.3 collective-permute-start.1
  9.5 0.0 copy-start
  9.5 1.6 %copy-done = f32[4,8,64,256]{3,2,1,0:T(8,128)S(1)} copy-done((f32[4,8,64,256]{3,2,1,0:T(8,128)S(1)}, f32[4,8,64,256]{3,2,1,0:T(8,128)}, u32[]{:S(2)}) %copy-start) | copy-done | bytes 2097176
  11.1 1.2 copy-done.1
  12.3 4.8 %upward.1 = (bf16[3,64,8192]{2,1,0:T(8,128)(2,1)S(1)}, f32[8,128]{1,0:T(8,128)S(1)}) custom-call(f32[4,8192]{1,0:T(4,128)S(1)} %get-tuple-element.41.r_ref, f32[32,64,256]{2,1,0:T(8,128)S(1)} %bitcast.6, f32[32,64,64]{2,1,0:T(8,128)S(1)} %bitcast.7), custom_call_target="tpu_custom_call" | custom-call | tf_op jit(solution)/shard_map/upward/pallas_call | solution.py:477
  17.2 0.0 collective-permute-done.up_ref
  17.2 0.0 collective-permute-done.1.down_ref
  17.2 4.4 %collective-permute-start.2 = (f32[6,8,256]{2,1,0:T(8,128)S(1)}, f32[6,8,256]{2,1,0:T(8,128)S(1)}, u32[]{:S(2)}, u32[]{:S(2)}) collective-permute-start(f32[6,8,256]{2,1,0:T(8,128)S(1)} %get-tuple-element.43), channel_id=1, source_target_pairs={{0,1},{1,2},{2,3},{3,4},{4,5},{5,6},{6,7},{7,8},{8,9},{9,10},{10,1... | collective-permute-start | bytes 147464 | tf_op jit(solution)/shard_map/ppermute | solution.py:796
  21.6 1.9 %collective-permute-start.3 = (f32[6,8,256]{2,1,0:T(8,128)S(1)}, f32[6,8,256]{2,1,0:T(8,128)S(1)}, u32[]{:S(2)}, u32[]{:S(2)}) collective-permute-start(f32[6,8,256]{2,1,0:T(8,128)S(1)} %get-tuple-element.44), channel_id=1, source_target_pairs={{1,0},{2,1},{3,2},{4,3},{5,4},{6,5},{7,6},{8,7},{9,8},{10,9},{11,1... | collective-permute-start | bytes 147464 | tf_op jit(solution)/shard_map/ppermute | solution.py:796
  23.5 0.0 copy-done.5
  23.6 0.0 copy-start.10
  23.6 0.7 copy-done.10
  24.2 1.4 couplings.1
  25.7 0.0 collective-permute-done.2.left_ref
  25.7 1.4 collective-permute-done.3.right_ref
  27.0 0.0 copy-done.6
  27.0 0.0 copy-done.7
  27.0 0.7 copy-done.8
  27.7 5.5 %geometry.1 = (bf16[60,256,32]{2,1,0:T(8,128)(2,1)S(1)}, bf16[60,32,256]{2,1,0:T(8,128)(2,1)S(1)}, bf16[61,16,256]{2,1,0:T(8,128)(2,1)S(1)}, s32[296]{0:T(512)S(...) custom-call(s32[4,8,9]{2,1,0:T(8,128)S(1)} %copy-done.6, ...), custom_call_target="tpu_custom_call" | custom-call | tf_op jit(solution)/shard_map/geometry/pallas_call | solution.py:252
  33.3 16.2 %all_to_all.20.c_ref = f32[16,8,128]{2,1,0:T(8,128)S(1)} all-to-all(f32[16,8,128]{2,1,0:T(8,128)S(1)} %get-tuple-element.49), channel_id=1, replica_groups=mesh['gx'=16,'gy'=16] {'gy'}, dimensions={0} | all-to-all | bytes 131072 | tf_op jit(solution)/shard_map/all_to_all | solution.py:806
  49.4 0.8 row_tree.2
  50.2 14.2 %all_to_all.21.after_ref.x_ref = f32[16,8,128]{2,1,0:T(8,128)S(1)} all-to-all(f32[16,8,128]{2,1,0:T(8,128)S(1)} %get-tuple-element.52), channel_id=1, replica_groups=mesh['gx'=16,'gy'=16] {'gx'}, dimensions={0} | all-to-all | bytes 131072 | tf_op jit(solution)/shard_map/all_to_all | solution.py:806
  64.4 0.0 copy-done.2
  64.4 23.5 %near_build.1 = (f32[4,8192]{1,0:T(4,128)S(1)}, bf16[38,8,2,256,256]{4,3,2,1,0:T(8,128)(2,1)}) custom-call(s32[296]{0:T(512)S(1)} %get-tuple-element.46.long_ref, s32[296]{0:T(512)S(1)} %get-tuple-element.47.short_ref, s32[2]{0:T(128)S(1)} %get-tuple-element.48.groups_ref, bf16[61,16,256]{2,1,0:T(8,128)(2,1)S(1)} %get-tuple-element.55.v_ref, ...), custom_call_target="tpu_custom_call" | custom-call | tf_op jit(solution)/shard_map/near_build/pallas_call | solution.py:357
  87.9 2.7 %middle.1 = (f32[4,8192]{1,0:T(4,128)S(1)}, f32[32,4,256]{2,1,0:T(4,128)S(1)}, f32[8,4,256]{2,1,0:T(4,128)S(1)}, f32[8,4,256]{2,1,0:T(4,128)S(1)}, f32[8,128]{1,0:T(8,128)S(1)}) custom-call(f32[16,8,128]{2,1,0:T(8,128)S(1)} %all_to_all.21.after_ref.x_ref, f32[8,64]{1,0:T(8,128)S(1)} %get-tuple-element.53.y_ref, ...), custom_call_target="tpu_custom_call" | custom-call | tf_op jit(solution)/shard_map/middle/pallas_call | solution.py:657
  90.6 5.4 %collective-permute-start.4 = (f32[8,4,256]{2,1,0:T(4,128)S(1)}, f32[8,4,256]{2,1,0:T(4,128)S(1)}, u32[]{:S(2)}, u32[]{:S(2)}) collective-permute-start(f32[8,4,256]{2,1,0:T(4,128)S(1)} %get-tuple-element.61), channel_id=1, source_target_pairs={{0,16},{16,32},{32,48},{48,64},{64,80},{80,96},{96,112},{112,128},... | collective-permute-start | bytes 98312 | tf_op jit(solution)/shard_map/ppermute | solution.py:796
  96.1 1.3 collective-permute-start.5
  97.4 0.0 collective-permute-done.4.up_ref
  97.4 3.3 %collective-permute-done.5.down_ref = f32[8,4,256]{2,1,0:T(4,128)S(1)} collective-permute-done((f32[8,4,256]{2,1,0:T(4,128)S(1)}, f32[8,4,256]{2,1,0:T(4,128)S(1)}, u32[]{:S(2)}, u32[]{:S(2)}) %collective-permute-start.5) | collective-permute-done | bytes 32800 | tf_op jit(solution)/shard_map/ppermute | solution.py:796
  100.8 3.9 %collective-permute-start.6 = (f32[6,4,256]{2,1,0:T(4,128)S(1)}, f32[6,4,256]{2,1,0:T(4,128)S(1)}, u32[]{:S(2)}, u32[]{:S(2)}) collective-permute-start(f32[6,4,256]{2,1,0:T(4,128)S(1)} %get-tuple-element.64), channel_id=1, source_target_pairs={{0,1},{1,2},{2,3},{3,4},{4,5},{5,6},{6,7},{7,8},{8,9},{9,10},{10,1... | collective-permute-start | bytes 73736 | tf_op jit(solution)/shard_map/ppermute | solution.py:796
  104.7 2.4 %collective-permute-start.7 = (f32[6,4,256]{2,1,0:T(4,128)S(1)}, f32[6,4,256]{2,1,0:T(4,128)S(1)}, u32[]{:S(2)}, u32[]{:S(2)}) collective-permute-start(f32[6,4,256]{2,1,0:T(4,128)S(1)} %get-tuple-element.65), channel_id=1, source_target_pairs={{1,0},{2,1},{3,2},{4,3},{5,4},{6,5},{7,6},{8,7},{9,8},{10,9},{11,1... | collective-permute-start | bytes 73736 | tf_op jit(solution)/shard_map/ppermute | solution.py:796
  107.1 0.0 collective-permute-done.6.left_ref
  107.1 2.7 %collective-permute-done.7.right_ref = f32[6,4,256]{2,1,0:T(4,128)S(1)} collective-permute-done((f32[6,4,256]{2,1,0:T(4,128)S(1)}, f32[6,4,256]{2,1,0:T(4,128)S(1)}, u32[]{:S(2)}, u32[]{:S(2)}) %collective-permute-start.7) | collective-permute-done | bytes 24608 | tf_op jit(solution)/shard_map/ppermute | solution.py:796
  109.8 12.5 %near_reuse.1 = (f32[4,8192]{1,0:T(4,128)S(1)}, f32[16,8,128]{2,1,0:T(8,128)S(1)}) custom-call(s32[296]{0:T(512)S(1)} %get-tuple-element.46.long_ref, s32[296]{0:T(512)S(1)} %get-tuple-element.47.short_ref, s32[2]{0:T(128)S(1)} %get-tuple-element.48.groups_ref, f32[32,4,256]{2,1,0:T(4,128)S(1)} %get-tuple-element.60.own_ref, ...), custom_call_target="tpu_custom_call" | custom-call | tf_op jit(solution)/shard_map/near_reuse/pallas_call | solution.py:443
  122.3 14.9 %all_to_all.22.c_ref = f32[16,8,128]{2,1,0:T(8,128)S(1)} all-to-all(f32[16,8,128]{2,1,0:T(8,128)S(1)} %get-tuple-element.67), channel_id=1, replica_groups=mesh['gx'=16,'gy'=16] {'gy'}, dimensions={0} | all-to-all | bytes 131072 | tf_op jit(solution)/shard_map/all_to_all | solution.py:806
  137.2 0.9 row_tree.3
  138.1 11.9 %all_to_all.23.c_ref = f32[16,8,128]{2,1,0:T(8,128)S(1)} all-to-all(f32[16,8,128]{2,1,0:T(8,128)S(1)} %get-tuple-element.68), channel_id=1, replica_groups=mesh['gx'=16,'gy'=16] {'gx'}, dimensions={0} | all-to-all | bytes 131072 | tf_op jit(solution)/shard_map/all_to_all | solution.py:806
  150.0 3.8 %final.1 = (f32[32,4,256]{2,1,0:T(4,128)}, f32[32,4,256]{2,1,0:T(4,128)}) custom-call(f32[16,8,128]{2,1,0:T(8,128)S(1)} %all_to_all.23.c_ref, f32[8,64]{1,0:T(8,128)S(1)} %get-tuple-element.69.y_ref, f32[2,64,64]{2,1,0:T(8,128)S(1)} %get-tuple-element.50.upper_ref, f32[7,64,64]{2,1,0:T(8,128)S(1)} %get-tuple-element.51.g_ref, ...), custom_call_target="tpu_custom_call" | custom-call | tf_op jit(solution)/shard_map/final/pallas_call | solution.py:781
  (6 shorter events, 0.0 us)
Async XLA Ops:
  0.6 63.8 %copy-start.2 = (bf16[9,32,256]{2,1,0:T(8,128)(2,1)S(1)}, bf16[9,32,256]{2,1,0:T(8,128)(2,1)}, u32[]{:S(2)}) copy-start(bf16[9,32,256]{2,1,0:T(8,128)(2,1)} %constant.6.clone.factor_ref) | copy-start | bytes 442372
  0.6 0.9 copy-start.3
  1.6 0.9 copy-start.4
  2.5 0.7 copy-start.9
  3.2 20.4 %copy-start.5 = (f32[2,64,64]{2,1,0:T(8,128)S(1)}, f32[2,64,64]{2,1,0:T(8,128)}, u32[]{:S(2)}) copy-start(f32[2,64,64]{2,1,0:T(8,128)} %upper_ref.1) | copy-start | bytes 98308
  3.2 23.9 %copy-start.6 = (s32[4,8,9]{2,1,0:T(8,128)S(1)}, s32[4,8,9]{2,1,0:T(8,128)}, u32[]{:S(2)}) copy-start(s32[4,8,9]{2,1,0:T(8,128)} %mask_ref.1) | copy-start | bytes 3460
  3.2 23.9 %copy-start.7 = (bf16[32,24]{1,0:T(8,128)(2,1)S(1)}, bf16[32,24]{1,0:T(8,128)(2,1)}, u32[]{:S(2)}) copy-start(bf16[32,24]{1,0:T(8,128)(2,1)} %constant.8.clone.source_ref) | copy-start | bytes 4612
  4.3 12.9 %collective-permute-start = (f32[8,8,256]{2,1,0:T(8,128)S(1)}, f32[8,8,256]{2,1,0:T(8,128)S(1)}, u32[]{:S(2)}, u32[]{:S(2)}) collective-permute-start(f32[8,8,256]{2,1,0:T(8,128)S(1)} %get-tuple-element.39), channel_id=1, source_target_pairs={{0,16},{16,32},{32,48},{48,64},{64,80},{80,96},{96,112},{112,128},... | collective-permute-start | bytes 196616 | tf_op jit(solution)/shard_map/ppermute | solution.py:796
  8.2 9.0 %collective-permute-start.1 = (f32[8,8,256]{2,1,0:T(8,128)S(1)}, f32[8,8,256]{2,1,0:T(8,128)S(1)}, u32[]{:S(2)}, u32[]{:S(2)}) collective-permute-start(f32[8,8,256]{2,1,0:T(8,128)S(1)} %get-tuple-element.40), channel_id=1, source_target_pairs={{16,0},{32,16},{48,32},{64,48},{80,64},{96,80},{112,96},{128,112},... | collective-permute-start | bytes 196616 | tf_op jit(solution)/shard_map/ppermute | solution.py:796
  9.5 1.6 %copy-start = (f32[4,8,64,256]{3,2,1,0:T(8,128)S(1)}, f32[4,8,64,256]{3,2,1,0:T(8,128)}, u32[]{:S(2)}) copy-start(f32[4,8,64,256]{3,2,1,0:T(8,128)} %param.15) | copy-start | bytes 6291460
  11.1 1.2 copy-start.1
  17.2 8.4 %collective-permute-start.2 = (f32[6,8,256]{2,1,0:T(8,128)S(1)}, f32[6,8,256]{2,1,0:T(8,128)S(1)}, u32[]{:S(2)}, u32[]{:S(2)}) collective-permute-start(f32[6,8,256]{2,1,0:T(8,128)S(1)} %get-tuple-element.43), channel_id=1, source_target_pairs={{0,1},{1,2},{2,3},{3,4},{4,5},{5,6},{6,7},{7,8},{8,9},{9,10},{10,1... | collective-permute-start | bytes 147464 | tf_op jit(solution)/shard_map/ppermute | solution.py:796
  21.6 5.4 %collective-permute-start.3 = (f32[6,8,256]{2,1,0:T(8,128)S(1)}, f32[6,8,256]{2,1,0:T(8,128)S(1)}, u32[]{:S(2)}, u32[]{:S(2)}) collective-permute-start(f32[6,8,256]{2,1,0:T(8,128)S(1)} %get-tuple-element.44), channel_id=1, source_target_pairs={{1,0},{2,1},{3,2},{4,3},{5,4},{6,5},{7,6},{8,7},{9,8},{10,9},{11,1... | collective-permute-start | bytes 147464 | tf_op jit(solution)/shard_map/ppermute | solution.py:796
  23.6 0.7 copy-start.10
  27.0 0.7 copy-start.8
  90.6 6.8 %collective-permute-start.4 = (f32[8,4,256]{2,1,0:T(4,128)S(1)}, f32[8,4,256]{2,1,0:T(4,128)S(1)}, u32[]{:S(2)}, u32[]{:S(2)}) collective-permute-start(f32[8,4,256]{2,1,0:T(4,128)S(1)} %get-tuple-element.61), channel_id=1, source_target_pairs={{0,16},{16,32},{32,48},{48,64},{64,80},{80,96},{96,112},{112,128},... | collective-permute-start | bytes 98312 | tf_op jit(solution)/shard_map/ppermute | solution.py:796
  96.1 4.7 %collective-permute-start.5 = (f32[8,4,256]{2,1,0:T(4,128)S(1)}, f32[8,4,256]{2,1,0:T(4,128)S(1)}, u32[]{:S(2)}, u32[]{:S(2)}) collective-permute-start(f32[8,4,256]{2,1,0:T(4,128)S(1)} %get-tuple-element.62), channel_id=1, source_target_pairs={{16,0},{32,16},{48,32},{64,48},{80,64},{96,80},{112,96},{128,112},... | collective-permute-start | bytes 98312 | tf_op jit(solution)/shard_map/ppermute | solution.py:796
  100.8 6.3 %collective-permute-start.6 = (f32[6,4,256]{2,1,0:T(4,128)S(1)}, f32[6,4,256]{2,1,0:T(4,128)S(1)}, u32[]{:S(2)}, u32[]{:S(2)}) collective-permute-start(f32[6,4,256]{2,1,0:T(4,128)S(1)} %get-tuple-element.64), channel_id=1, source_target_pairs={{0,1},{1,2},{2,3},{3,4},{4,5},{5,6},{6,7},{7,8},{8,9},{9,10},{10,1... | collective-permute-start | bytes 73736 | tf_op jit(solution)/shard_map/ppermute | solution.py:796
  104.7 5.1 %collective-permute-start.7 = (f32[6,4,256]{2,1,0:T(4,128)S(1)}, f32[6,4,256]{2,1,0:T(4,128)S(1)}, u32[]{:S(2)}, u32[]{:S(2)}) collective-permute-start(f32[6,4,256]{2,1,0:T(4,128)S(1)} %get-tuple-element.65), channel_id=1, source_target_pairs={{1,0},{2,1},{3,2},{4,3},{5,4},{6,5},{7,6},{8,7},{9,8},{10,9},{11,1... | collective-permute-start | bytes 73736 | tf_op jit(solution)/shard_map/ppermute | solution.py:796

commit v4 on v3

--- a/solution.py
+++ b/solution.py
@@ -791,7 +791,7 @@
 
 def swap(axis, first, last):
     count = lax.axis_size(axis)
-    up = [(i, i + 1) for i in range(count - 1)]
+    up = [(i, (i + 1) % count) for i in range(count)]
     down = [(j, i) for i, j in up]
     return lax.ppermute(last, axis, up), lax.ppermute(first, axis, down)
 

time: 156 us -> 141 us (0.904); the launches traced: 154 us -> 141 us
  starting transfers between devices: 24.6 us -> 14.4 us
  blocking collectives: 57.2 us -> 51.7 us
  Pallas kernels: 57 us -> 61.5 us
  waiting for transfers between devices: 7.45 us -> 5.74 us
    ppermute x8, starting transfers between devices: 24.6 us -> 14.4 us  [swap(): return (lax.ppermute(last, axis, up), lax.ppermute(first, axis, down))]
    all_to_all x4, blocking collectives: 57.2 us -> 51.7 us  [exchange(): return lax.all_to_all(x, axis, 0, 0, tiled=True)]
    pallas_call x1, Pallas kernels: 23.5 us -> 26.5 us  [near_build(): pl.pallas_call(functools.partial(build_kernel, nx, ny), out_shape=[jax.Sh...]
    ppermute x8, waiting for transfers between devices: 7.45 us -> 5.74 us  [swap(): return (lax.ppermute(last, axis, up), lax.ppermute(first, axis, down))]
  transfers between devices with their start and end apart: 8 -> 8, of which waited for: 3 -> 4; matrix products, arithmetic and copies ran while one was open for 0% -> 0% of each run, Pallas kernels for 4% -> 4%
where the time goes in v4:
time: 141 us
  Pallas kernels  61.5 us (44%)
  blocking collectives  51.7 us (37%)
  starting transfers between devices  14.4 us (10%)
  local copies, waits for them, and re-layouts  6.72 us (5%)
  waiting for transfers between devices  5.74 us (4%)
    all_to_all x4, blocking collectives, exchange(): return lax.all_to_all(x, axis, 0, 0, tiled=True)  51.7 us
    pallas_call x1, Pallas kernels, near_build(): pl.pallas_call(functools.partial(build_kernel, nx, ny), out_shape=[jax.Sh...  26.5 us
    ppermute x8, starting transfers between devices, swap(): return (lax.ppermute(last, axis, up), lax.ppermute(first, axis, down))  14.4 us
    pallas_call x1, Pallas kernels, near_reuse(): pl.pallas_call(functools.partial(reuse_kernel, nx, ny), out_shape=[jax.Sh...  14 us
    unnamed x22, local copies, waits for them, and re-layouts  6.72 us
    ppermute x8, waiting for transfers between devices, swap(): return (lax.ppermute(last, axis, up), lax.ppermute(first, axis, down))  5.74 us
    pallas_call x1, Pallas kernels, geometry(): pl.pallas_call(functools.partial(geometry_kernel, nx, ny), out_shape=[jax...  5.53 us
    pallas_call x1, Pallas kernels, upward(): pl.pallas_call(upward_kernel, out_shape=[jax.ShapeDtypeStruct((3, terms,...  4.82 us
  transfers between devices with their start and end apart: 8, of which 4 were waited for; matrix products, arithmetic and copies ran while one was open for 0% of the time, Pallas kernels for 4%

profile of v4, /device:TPU:1, one launch (start us, length us, event | category | flops | bytes accessed | tf_op | source)
XLA Modules:
  0.0 140.8 jit_solution(6288444876659349426)
XLA Ops:
  0.6 0.0 copy-start.2
  0.6 0.0 copy-start.3
  0.7 0.9 copy-done.3
  1.6 0.0 copy-start.4
  1.6 0.9 copy-done.4
  2.5 0.0 copy-start.9
  2.5 0.7 copy-done.9
  3.2 0.0 copy-start.5
  3.2 0.0 copy-start.6
  3.2 0.0 copy-start.7
  3.2 1.1 pack.1
  4.3 2.1 %collective-permute-start = (f32[8,8,256]{2,1,0:T(8,128)S(1)}, f32[8,8,256]{2,1,0:T(8,128)S(1)}, u32[]{:S(2)}, u32[]{:S(2)}) collective-permute-start(f32[8,8,256]{2,1,0:T(8,128)S(1)} %get-tuple-element.39), channel_id=1, source_target_pairs={{0,16},{16,32},{32,48},{48,64},{64,80},{80,96},{96,112},{112,128},... | collective-permute-start | bytes 196616 | tf_op jit(solution)/shard_map/ppermute | solution.py:796
  6.4 3.8 %collective-permute-start.1 = (f32[8,8,256]{2,1,0:T(8,128)S(1)}, f32[8,8,256]{2,1,0:T(8,128)S(1)}, u32[]{:S(2)}, u32[]{:S(2)}) collective-permute-start(f32[8,8,256]{2,1,0:T(8,128)S(1)} %get-tuple-element.40), channel_id=1, source_target_pairs={{16,0},{32,16},{48,32},{64,48},{80,64},{96,80},{112,96},{128,112},... | collective-permute-start | bytes 196616 | tf_op jit(solution)/shard_map/ppermute | solution.py:796
  10.2 1.6 %copy-done = f32[4,8,64,256]{3,2,1,0:T(8,128)S(1)} copy-done((f32[4,8,64,256]{3,2,1,0:T(8,128)S(1)}, f32[4,8,64,256]{3,2,1,0:T(8,128)}, u32[]{:S(2)}) %copy-start) | copy-done | bytes 2097176
  11.8 1.2 copy-done.1
  13.0 4.8 %upward.1 = (bf16[3,64,8192]{2,1,0:T(8,128)(2,1)S(1)}, f32[8,128]{1,0:T(8,128)S(1)}) custom-call(f32[4,8192]{1,0:T(4,128)S(1)} %get-tuple-element.41.r_ref, f32[32,64,256]{2,1,0:T(8,128)S(1)} %bitcast.6, f32[32,64,64]{2,1,0:T(8,128)S(1)} %bitcast.7), custom_call_target="tpu_custom_call" | custom-call | tf_op jit(solution)/shard_map/upward/pallas_call | solution.py:477
  17.8 0.0 collective-permute-done.up_ref
  17.8 0.0 collective-permute-done.1.down_ref
  17.9 2.5 %collective-permute-start.2 = (f32[6,8,256]{2,1,0:T(8,128)S(1)}, f32[6,8,256]{2,1,0:T(8,128)S(1)}, u32[]{:S(2)}, u32[]{:S(2)}) collective-permute-start(f32[6,8,256]{2,1,0:T(8,128)S(1)} %get-tuple-element.43), channel_id=1, source_target_pairs={{0,1},{1,2},{2,3},{3,4},{4,5},{5,6},{6,7},{7,8},{8,9},{9,10},{10,1... | collective-permute-start | bytes 147464 | tf_op jit(solution)/shard_map/ppermute | solution.py:796
  20.4 0.2 collective-permute-start.3
  20.7 0.0 copy-done.5
  20.7 0.7 copy-done.10
  21.4 1.4 %couplings.1 = (f32[7,64,64]{2,1,0:T(8,128)S(1)}, f32[7,64,64]{2,1,0:T(8,128)S(1)}, f32[2,64,64]{2,1,0:T(8,128)S(1)}) custom-call(f32[2,64,64]{2,1,0:T(8,128)S(1)} %copy-done.5, f32[3,64]{1,0:T(4,128)S(1)} %copy-done.10), custom_call_target="tpu_custom_call" | custom-call | tf_op jit(solution)/shard_map/couplings/pallas_call | solution.py:529
  22.8 0.0 collective-permute-done.2.left_ref
  22.8 1.2 collective-permute-done.3.right_ref
  23.9 0.0 copy-done.6
  23.9 0.0 copy-done.7
  24.0 0.7 copy-done.8
  24.6 5.5 %geometry.1 = (bf16[60,256,32]{2,1,0:T(8,128)(2,1)S(1)}, bf16[60,32,256]{2,1,0:T(8,128)(2,1)S(1)}, bf16[61,16,256]{2,1,0:T(8,128)(2,1)S(1)}, s32[296]{0:T(512)S(...) custom-call(s32[4,8,9]{2,1,0:T(8,128)S(1)} %copy-done.6, ...), custom_call_target="tpu_custom_call" | custom-call | tf_op jit(solution)/shard_map/geometry/pallas_call | solution.py:252
  30.2 16.1 %all_to_all.20.c_ref = f32[16,8,128]{2,1,0:T(8,128)S(1)} all-to-all(f32[16,8,128]{2,1,0:T(8,128)S(1)} %get-tuple-element.49), channel_id=1, replica_groups=mesh['gx'=16,'gy'=16] {'gy'}, dimensions={0} | all-to-all | bytes 131072 | tf_op jit(solution)/shard_map/all_to_all | solution.py:806
  46.3 0.8 row_tree.2
  47.1 9.8 %all_to_all.21.after_ref.x_ref = f32[16,8,128]{2,1,0:T(8,128)S(1)} all-to-all(f32[16,8,128]{2,1,0:T(8,128)S(1)} %get-tuple-element.52), channel_id=1, replica_groups=mesh['gx'=16,'gy'=16] {'gx'}, dimensions={0} | all-to-all | bytes 131072 | tf_op jit(solution)/shard_map/all_to_all | solution.py:806
  56.8 0.0 copy-done.2
  56.9 26.5 %near_build.1 = (f32[4,8192]{1,0:T(4,128)S(1)}, bf16[38,8,2,256,256]{4,3,2,1,0:T(8,128)(2,1)}) custom-call(s32[296]{0:T(512)S(1)} %get-tuple-element.46.long_ref, s32[296]{0:T(512)S(1)} %get-tuple-element.47.short_ref, s32[2]{0:T(128)S(1)} %get-tuple-element.48.groups_ref, bf16[61,16,256]{2,1,0:T(8,128)(2,1)S(1)} %get-tuple-element.55.v_ref, ...), custom_call_target="tpu_custom_call" | custom-call | tf_op jit(solution)/shard_map/near_build/pallas_call | solution.py:357
  83.3 2.7 %middle.1 = (f32[4,8192]{1,0:T(4,128)S(1)}, f32[32,4,256]{2,1,0:T(4,128)S(1)}, f32[8,4,256]{2,1,0:T(4,128)S(1)}, f32[8,4,256]{2,1,0:T(4,128)S(1)}, f32[8,128]{1,0:T(8,128)S(1)}) custom-call(f32[16,8,128]{2,1,0:T(8,128)S(1)} %all_to_all.21.after_ref.x_ref, f32[8,64]{1,0:T(8,128)S(1)} %get-tuple-element.53.y_ref, ...), custom_call_target="tpu_custom_call" | custom-call | tf_op jit(solution)/shard_map/middle/pallas_call | solution.py:657
  86.0 0.0 collective-permute-start.4
  86.1 4.8 %collective-permute-start.5 = (f32[8,4,256]{2,1,0:T(4,128)S(1)}, f32[8,4,256]{2,1,0:T(4,128)S(1)}, u32[]{:S(2)}, u32[]{:S(2)}) collective-permute-start(f32[8,4,256]{2,1,0:T(4,128)S(1)} %get-tuple-element.62), channel_id=1, source_target_pairs={{16,0},{32,16},{48,32},{64,48},{80,64},{96,80},{112,96},{128,112},... | collective-permute-start | bytes 98312 | tf_op jit(solution)/shard_map/ppermute | solution.py:796
  90.8 1.3 collective-permute-done.4.up_ref
  92.1 0.0 collective-permute-done.5.down_ref
  92.2 0.9 collective-permute-start.6
  93.1 0.0 collective-permute-start.7
  93.1 0.9 collective-permute-done.6.left_ref
  94.0 2.3 %collective-permute-done.7.right_ref = f32[6,4,256]{2,1,0:T(4,128)S(1)} collective-permute-done((f32[6,4,256]{2,1,0:T(4,128)S(1)}, f32[6,4,256]{2,1,0:T(4,128)S(1)}, u32[]{:S(2)}, u32[]{:S(2)}) %collective-permute-start.7) | collective-permute-done | bytes 24608 | tf_op jit(solution)/shard_map/ppermute | solution.py:796
  96.3 14.0 %near_reuse.1 = (f32[4,8192]{1,0:T(4,128)S(1)}, f32[16,8,128]{2,1,0:T(8,128)S(1)}) custom-call(s32[296]{0:T(512)S(1)} %get-tuple-element.46.long_ref, s32[296]{0:T(512)S(1)} %get-tuple-element.47.short_ref, s32[2]{0:T(128)S(1)} %get-tuple-element.48.groups_ref, f32[32,4,256]{2,1,0:T(4,128)S(1)} %get-tuple-element.60.own_ref, ...), custom_call_target="tpu_custom_call" | custom-call | tf_op jit(solution)/shard_map/near_reuse/pallas_call | solution.py:443
  110.3 11.9 %all_to_all.22.c_ref = f32[16,8,128]{2,1,0:T(8,128)S(1)} all-to-all(f32[16,8,128]{2,1,0:T(8,128)S(1)} %get-tuple-element.67), channel_id=1, replica_groups=mesh['gx'=16,'gy'=16] {'gy'}, dimensions={0} | all-to-all | bytes 131072 | tf_op jit(solution)/shard_map/all_to_all | solution.py:806
  122.2 0.9 row_tree.3
  123.1 14.0 %all_to_all.23.c_ref = f32[16,8,128]{2,1,0:T(8,128)S(1)} all-to-all(f32[16,8,128]{2,1,0:T(8,128)S(1)} %get-tuple-element.68), channel_id=1, replica_groups=mesh['gx'=16,'gy'=16] {'gx'}, dimensions={0} | all-to-all | bytes 131072 | tf_op jit(solution)/shard_map/all_to_all | solution.py:806
  137.1 3.8 %final.1 = (f32[32,4,256]{2,1,0:T(4,128)}, f32[32,4,256]{2,1,0:T(4,128)}) custom-call(f32[16,8,128]{2,1,0:T(8,128)S(1)} %all_to_all.23.c_ref, f32[8,64]{1,0:T(8,128)S(1)} %get-tuple-element.69.y_ref, f32[2,64,64]{2,1,0:T(8,128)S(1)} %get-tuple-element.50.upper_ref, f32[7,64,64]{2,1,0:T(8,128)S(1)} %get-tuple-element.51.g_ref, ...), custom_call_target="tpu_custom_call" | custom-call | tf_op jit(solution)/shard_map/final/pallas_call | solution.py:781
  (6 shorter events, 0.0 us)
Async XLA Ops:
  0.6 56.2 %copy-start.2 = (bf16[9,32,256]{2,1,0:T(8,128)(2,1)S(1)}, bf16[9,32,256]{2,1,0:T(8,128)(2,1)}, u32[]{:S(2)}) copy-start(bf16[9,32,256]{2,1,0:T(8,128)(2,1)} %constant.6.clone.factor_ref) | copy-start | bytes 442372
  0.6 0.9 copy-start.3
  1.6 0.9 copy-start.4
  2.5 0.7 copy-start.9
  3.2 17.5 %copy-start.5 = (f32[2,64,64]{2,1,0:T(8,128)S(1)}, f32[2,64,64]{2,1,0:T(8,128)}, u32[]{:S(2)}) copy-start(f32[2,64,64]{2,1,0:T(8,128)} %upper_ref.1) | copy-start | bytes 98308
  3.2 20.8 %copy-start.6 = (s32[4,8,9]{2,1,0:T(8,128)S(1)}, s32[4,8,9]{2,1,0:T(8,128)}, u32[]{:S(2)}) copy-start(s32[4,8,9]{2,1,0:T(8,128)} %mask_ref.1) | copy-start | bytes 3460
  3.2 20.8 %copy-start.7 = (bf16[32,24]{1,0:T(8,128)(2,1)S(1)}, bf16[32,24]{1,0:T(8,128)(2,1)}, u32[]{:S(2)}) copy-start(bf16[32,24]{1,0:T(8,128)(2,1)} %constant.8.clone.source_ref) | copy-start | bytes 4612
  4.3 13.6 %collective-permute-start = (f32[8,8,256]{2,1,0:T(8,128)S(1)}, f32[8,8,256]{2,1,0:T(8,128)S(1)}, u32[]{:S(2)}, u32[]{:S(2)}) collective-permute-start(f32[8,8,256]{2,1,0:T(8,128)S(1)} %get-tuple-element.39), channel_id=1, source_target_pairs={{0,16},{16,32},{32,48},{48,64},{64,80},{80,96},{96,112},{112,128},... | collective-permute-start | bytes 196616 | tf_op jit(solution)/shard_map/ppermute | solution.py:796
  6.4 11.5 %collective-permute-start.1 = (f32[8,8,256]{2,1,0:T(8,128)S(1)}, f32[8,8,256]{2,1,0:T(8,128)S(1)}, u32[]{:S(2)}, u32[]{:S(2)}) collective-permute-start(f32[8,8,256]{2,1,0:T(8,128)S(1)} %get-tuple-element.40), channel_id=1, source_target_pairs={{16,0},{32,16},{48,32},{64,48},{80,64},{96,80},{112,96},{128,112},... | collective-permute-start | bytes 196616 | tf_op jit(solution)/shard_map/ppermute | solution.py:796
  10.2 1.6 %copy-start = (f32[4,8,64,256]{3,2,1,0:T(8,128)S(1)}, f32[4,8,64,256]{3,2,1,0:T(8,128)}, u32[]{:S(2)}) copy-start(f32[4,8,64,256]{3,2,1,0:T(8,128)} %param.15) | copy-start | bytes 6291460
  11.8 1.2 copy-start.1
  17.9 4.9 %collective-permute-start.2 = (f32[6,8,256]{2,1,0:T(8,128)S(1)}, f32[6,8,256]{2,1,0:T(8,128)S(1)}, u32[]{:S(2)}, u32[]{:S(2)}) collective-permute-start(f32[6,8,256]{2,1,0:T(8,128)S(1)} %get-tuple-element.43), channel_id=1, source_target_pairs={{0,1},{1,2},{2,3},{3,4},{4,5},{5,6},{6,7},{7,8},{8,9},{9,10},{10,1... | collective-permute-start | bytes 147464 | tf_op jit(solution)/shard_map/ppermute | solution.py:796
  20.4 3.5 %collective-permute-start.3 = (f32[6,8,256]{2,1,0:T(8,128)S(1)}, f32[6,8,256]{2,1,0:T(8,128)S(1)}, u32[]{:S(2)}, u32[]{:S(2)}) collective-permute-start(f32[6,8,256]{2,1,0:T(8,128)S(1)} %get-tuple-element.44), channel_id=1, source_target_pairs={{1,0},{2,1},{3,2},{4,3},{5,4},{6,5},{7,6},{8,7},{9,8},{10,9},{11,1... | collective-permute-start | bytes 147464 | tf_op jit(solution)/shard_map/ppermute | solution.py:796
  20.7 0.7 copy-start.10
  24.0 0.7 copy-start.8
  86.0 6.1 %collective-permute-start.4 = (f32[8,4,256]{2,1,0:T(4,128)S(1)}, f32[8,4,256]{2,1,0:T(4,128)S(1)}, u32[]{:S(2)}, u32[]{:S(2)}) collective-permute-start(f32[8,4,256]{2,1,0:T(4,128)S(1)} %get-tuple-element.61), channel_id=1, source_target_pairs={{0,16},{16,32},{32,48},{48,64},{64,80},{80,96},{96,112},{112,128},... | collective-permute-start | bytes 98312 | tf_op jit(solution)/shard_map/ppermute | solution.py:796
  86.1 6.1 %collective-permute-start.5 = (f32[8,4,256]{2,1,0:T(4,128)S(1)}, f32[8,4,256]{2,1,0:T(4,128)S(1)}, u32[]{:S(2)}, u32[]{:S(2)}) collective-permute-start(f32[8,4,256]{2,1,0:T(4,128)S(1)} %get-tuple-element.62), channel_id=1, source_target_pairs={{16,0},{32,16},{48,32},{64,48},{80,64},{96,80},{112,96},{128,112},... | collective-permute-start | bytes 98312 | tf_op jit(solution)/shard_map/ppermute | solution.py:796
  92.2 1.9 %collective-permute-start.6 = (f32[6,4,256]{2,1,0:T(4,128)S(1)}, f32[6,4,256]{2,1,0:T(4,128)S(1)}, u32[]{:S(2)}, u32[]{:S(2)}) collective-permute-start(f32[6,4,256]{2,1,0:T(4,128)S(1)} %get-tuple-element.64), channel_id=1, source_target_pairs={{0,1},{1,2},{2,3},{3,4},{4,5},{5,6},{6,7},{7,8},{8,9},{9,10},{10,1... | collective-permute-start | bytes 73736 | tf_op jit(solution)/shard_map/ppermute | solution.py:796
  93.1 3.3 %collective-permute-start.7 = (f32[6,4,256]{2,1,0:T(4,128)S(1)}, f32[6,4,256]{2,1,0:T(4,128)S(1)}, u32[]{:S(2)}, u32[]{:S(2)}) collective-permute-start(f32[6,4,256]{2,1,0:T(4,128)S(1)} %get-tuple-element.65), channel_id=1, source_target_pairs={{1,0},{2,1},{3,2},{4,3},{5,4},{6,5},{7,6},{8,7},{9,8},{10,9},{11,1... | collective-permute-start | bytes 73736 | tf_op jit(solution)/shard_map/ppermute | solution.py:796

commit v5 on v4

--- a/solution.py
+++ b/solution.py
@@ -228,7 +228,7 @@
             short_count = short_count + (on - is_long)
         return long_count, short_count
 
-    long_count, short_count = lax.fori_loop(0, nx * ny, note, (0, 0), unroll=4)
+    long_count, short_count = lax.fori_loop(0, nx * ny, note, (0, 0), unroll=8)
     for j in range(GROUP):
         long_ref[long_count + j] = leaves * 1024
         short_ref[short_count + j] = leaves * 1024
@@ -467,7 +467,7 @@
             total = total + dot_nt(v, piece)
         return total
 
-    total = lax.fori_loop(0, leaves, body, jnp.zeros((16, terms), F32), unroll=8)
+    total = lax.fori_loop(0, leaves, body, jnp.zeros((16, terms), F32), unroll=16)
     total = jnp.concatenate([join16(total), jnp.zeros((4, 128 - terms), F32)], axis=1)
     c_ref[...] = jnp.concatenate([total, jnp.zeros((4, 128), F32)], axis=0)
 
@@ -576,8 +576,10 @@
         c = lift(c, upper_ref)
         level += 1
     y_ref[...] = y
-    lower = jnp.zeros((4, 128), F32)
-    if with_energy:
+    if not with_energy:
+        lower = jnp.max(jnp.max(jnp.abs(x), axis=0), axis=1, keepdims=True)
+        lower = jnp.broadcast_to(jnp.max(lower, axis=0, keepdims=True), (4, 128))
+    else:
         lower = jnp.sum(x, axis=0)[4:8]
         lower = jnp.concatenate([lower[:, 0:16], columns_of(sums)[0:4], jnp.zeros((4, 108), F32)], axis=1)
     total = jnp.concatenate([jnp.concatenate([c[0, 0:4], c[1, 0:4]], axis=1), lower], axis=0)
@@ -620,18 +622,43 @@
     return join16(dot(y, joint_ref[0, :, part]) + (dot(y, joint_ref[1, :, part]) + dot(y, joint_ref[2, :, part])))
 
 
+def scale_of(x, upper_ref, levels):
+    largest = jnp.max(jnp.max(x[:, 4:8], axis=0), axis=0, keepdims=True)
+    sizes = jnp.abs(upper_ref[...])
+    up = jnp.max(jnp.sum(sizes[0] + sizes[1], axis=0, keepdims=True), axis=1, keepdims=True)
+    down = jnp.max(jnp.max(jnp.sum(sizes, axis=2, keepdims=True), axis=0), axis=0, keepdims=True)
+    growth = jnp.ones((1, 1), F32)
+    for _ in range(levels - 1):
+        growth = 1.0 + growth * (up * down)
+    bound = 864.0 + 576.0 * (growth * largest)
+    power = jnp.ones_like(bound)
+    scale = jnp.full_like(bound, 2.0**48)
+    inverse = jnp.full_like(bound, 2.0**-48)
+    for k in (64, 32, 16, 8, 4, 2):
+        fits = bound >= power * 2.0**k
+        power = jnp.where(fits, power * 2.0**k, power)
+        scale = jnp.where(fits, scale * 2.0 ** (-1.5 * k), scale)
+        inverse = jnp.where(fits, inverse * 2.0 ** (1.5 * k), inverse)
+    return jnp.minimum(scale, 1.0), jnp.maximum(inverse, 1.0)
+
+
 def middle_kernel(
     cols, levels, x_ref, y_ref, upper_ref, g_ref, joint_ref, r_ref, n_ref, valid_ref,
-    e_ref, leaf_ref, top_ref, bottom_ref, out_ref, scratch, both,
+    e_ref, leaf_ref, top_ref, bottom_ref, out_ref, scale_ref, scratch, both,
 ):
     leaves, _, size = leaf_ref.shape
     own, _ = upper_levels(cols, levels, x_ref[...], y_ref[...], upper_ref, g_ref, None, scratch, False)
     y = rows16(own)
+    scale, inverse = scale_of(x_ref[...], upper_ref, levels)
+    scale_ref[0:1] = scale
+    scale_ref[1:2] = inverse
+    scale = jnp.concatenate([scale] * (size // 128), axis=1)
     width = leaves * size // SPLITS
+    scale = jnp.concatenate([scale] * (width // size), axis=1)
     for k in range(SPLITS):
         part = slice(k * width, (k + 1) * width)
         far = far_of(y, joint_ref, part)
-        e = valid_ref[:, part] * (n_ref[:, part] + far)
+        e = valid_ref[:, part] * (scale * (n_ref[:, part] + far))
         e_ref[:, part] = e
         both[0:16, part] = rows16(r_ref[:, part])
         both[16:32, part] = rows16(e)
@@ -662,9 +689,10 @@
             jax.ShapeDtypeStruct((edge, 4, size), F32),
             jax.ShapeDtypeStruct((edge, 4, size), F32),
             jax.ShapeDtypeStruct((8, 128), F32),
+            jax.ShapeDtypeStruct((2, 128), F32),
         ],
         in_specs=[VM] * 8,
-        out_specs=[VM] * 5,
+        out_specs=[VM] * 6,
         scratch_shapes=[pltpu.VMEM((2 * x.shape[0], 8, 64), F32), pltpu.VMEM((32, r.shape[1]), BF)],
         compiler_params=params(),
         name="middle",
@@ -709,8 +737,12 @@
     return result
 
 
-def weights(gram, cross, square, cubic):
-    curvature = mat_add(gram, cross)
+def mat_scale(a, factor):
+    return [[value * factor for value in row] for row in a]
+
+
+def weights(gram, cross, square, cubic, scale, inverse):
+    curvature = mat_add(mat_scale(gram, scale), cross)
     both = mat_solve(curvature, [gram[i] + cross[i] for i in range(4)])
     step = [row[0:4] for row in both]
     rest = [row[4:8] for row in both]
@@ -721,21 +753,23 @@
     )
     mix = mat_solve(gram, gram_next)
     lead = mat_add(rest, mix)
-    second = mat_sub(lead, step)
-    with_r = mat_sub(mat_add(mat_mul(gram, lead), mat_mul(cross, second)), mat_mul(square, step))
+    second = mat_sub(mat_scale(lead, inverse), step)
+    with_r = mat_sub(
+        mat_add(mat_mul(gram, lead), mat_mul(cross, second)), mat_scale(mat_mul(square, step), inverse)
+    )
     with_e = mat_sub(mat_add(mat_mul(mat_t(cross), lead), mat_mul(square, second)), mat_mul(cubic, step))
     curvature_next = mat_sub(mat_mul(mat_t(lead), with_r), mat_mul(mat_t(step), with_e))
     step_next = mat_solve(curvature_next, gram_next)
     lead_step = mat_mul(lead, step_next)
     step_step = mat_mul(step, step_next)
-    second_step = mat_sub(lead_step, step_step)
-    solution = (mat_add(step, lead_step), [[-v for v in row] for row in step_step], None)
-    residual = (mat_sub(rest, lead_step), [[-(step[i][j] + second_step[i][j]) for j in range(4)] for i in range(4)], step_step)
+    second_step = mat_mul(second, step_next)
+    solution = (mat_add(mat_scale(step, scale), lead_step), mat_scale(step_step, -1.0), None)
+    residual = (mat_sub(rest, lead_step), mat_scale(mat_add(step, second_step), -1.0), step_step)
     return solution, residual
 
 
 def final_kernel(
-    cols, levels, c_ref, y_ref, upper_ref, g_ref, b_ref, joint_ref, r_ref, e_ref, n_ref, valid_ref,
+    cols, levels, c_ref, y_ref, upper_ref, g_ref, b_ref, joint_ref, r_ref, e_ref, n_ref, valid_ref, scale_ref,
     x_ref, out_ref, scratch,
 ):
     leaves, _, size = x_ref.shape
@@ -750,7 +784,9 @@
 
     half = mat_add(matrix(moments, 16), matrix(half, 0))
     cubic = mat_add(matrix(moments, 12), mat_add(half, mat_t(half)))
-    solution, residual = weights(matrix(moments, 0), matrix(moments, 4), matrix(moments, 8), cubic)
+    solution, residual = weights(
+        matrix(moments, 0), matrix(moments, 4), matrix(moments, 8), cubic, scale_ref[0:1], scale_ref[1:2]
+    )
     row = lax.broadcasted_iota(jnp.int32, (8, 128), 0)
     col = lax.broadcasted_iota(jnp.int32, (8, 128), 1)
     table = jnp.zeros((8, 128), F32)
@@ -776,17 +812,17 @@
             out_ref[k * (leaves // SPLITS) + i] = both[4:8, i * size : (i + 1) * size]
 
 
-def final(cols, levels, leaves, c, y, upper_t, g, b, joint, r, e, n, valid):
+def final(cols, levels, leaves, c, y, upper_t, g, b, joint, r, e, n, valid, scale):
     out = jax.ShapeDtypeStruct((leaves, 4, r.shape[1] // leaves), F32)
     return pl.pallas_call(
         functools.partial(final_kernel, cols, levels),
         out_shape=[out, out],
-        in_specs=[VM] * 10,
+        in_specs=[VM] * 11,
         out_specs=[VM] * 2,
         scratch_shapes=[pltpu.VMEM((2 * c.shape[0], 8, 64), F32)],
         compiler_params=params(),
         name="final",
-    )(c, y, upper_t, g, b, joint, r, e, n, valid)
+    )(c, y, upper_t, g, b, joint, r, e, n, valid, scale)
 
 
 def swap(axis, first, last):
@@ -825,10 +861,10 @@
     y, c = row_tree(False, exchange(c, "gy"), upper_t, g, b)
     c = exchange(c, "gx")
     n, cache = near_build(nx, ny, lists, v, s, t, factor, c)
-    e, e_leaves, top, bottom, c = middle(cols, levels, leaves, ny, c, y, upper_t, g, joint, r, n, valid)
+    e, e_leaves, top, bottom, c, scale = middle(cols, levels, leaves, ny, c, y, upper_t, g, joint, r, n, valid)
     n, c = near_reuse(nx, ny, lists, edges(nx, ny, e_leaves, top, bottom, c), c, cache, cols)
     y, c = row_tree(True, exchange(c, "gy"), upper_t, g, b)
-    x, out = final(cols, levels, leaves, exchange(c, "gx"), y, upper_t, g, b, joint, r, e, n, valid)
+    x, out = final(cols, levels, leaves, exchange(c, "gx"), y, upper_t, g, b, joint, r, e, n, valid, scale)
     shape = (nx, ny, 4, size)
     return x.reshape(shape), out.reshape(shape)
 

time: 141 us -> 140 us (level)
  Pallas kernels: 61.5 us -> 56.4 us
  blocking collectives: 51.7 us -> 53.5 us
    pallas_call x1, Pallas kernels: 26.5 us -> 23.5 us  [near_build(): pl.pallas_call(functools.partial(build_kernel, nx, ny), out_shape=[jax.Sh...]
    all_to_all x4, blocking collectives: 51.7 us -> 53.5 us  [exchange(): return lax.all_to_all(x, axis, 0, 0, tiled=True)]
    pallas_call x1, Pallas kernels: 14 us -> 12.5 us  [near_reuse(): pl.pallas_call(functools.partial(reuse_kernel, nx, ny), out_shape=[jax.Sh...]
  transfers between devices with their start and end apart: 8 -> 8, of which waited for: 4 -> 5; matrix products, arithmetic and copies ran while one was open for 0% -> 0% of each run, Pallas kernels for 4% -> 4%
where the time goes in v5:
time: 140 us; the launch traced here: 139 us
  Pallas kernels  56.4 us (40%)
  blocking collectives  53.5 us (38%)
  starting transfers between devices  15.3 us (11%)
  local copies, waits for them, and re-layouts  6.72 us (5%)
  waiting for transfers between devices  6.41 us (5%)
    all_to_all x4, blocking collectives, exchange(): return lax.all_to_all(x, axis, 0, 0, tiled=True)  53.5 us
    pallas_call x1, Pallas kernels, near_build(): pl.pallas_call(functools.partial(build_kernel, nx, ny), out_shape=[jax.Sh...  23.5 us
    ppermute x8, starting transfers between devices, swap(): return (lax.ppermute(last, axis, up), lax.ppermute(first, axis, down))  15.3 us
    pallas_call x1, Pallas kernels, near_reuse(): pl.pallas_call(functools.partial(reuse_kernel, nx, ny), out_shape=[jax.Sh...  12.5 us
    unnamed x22, local copies, waits for them, and re-layouts  6.72 us
    ppermute x8, waiting for transfers between devices, swap(): return (lax.ppermute(last, axis, up), lax.ppermute(first, axis, down))  6.41 us
    pallas_call x1, Pallas kernels, geometry(): pl.pallas_call(functools.partial(geometry_kernel, nx, ny), out_shape=[jax...  5.38 us
    pallas_call x1, Pallas kernels, upward(): pl.pallas_call(upward_kernel, out_shape=[jax.ShapeDtypeStruct((3, terms,...  4.39 us
  transfers between devices with their start and end apart: 8, of which 5 were waited for; matrix products, arithmetic and copies ran while one was open for 0% of the time, Pallas kernels for 4%

profile of v5, /device:TPU:1, one launch (start us, length us, event | category | flops | bytes accessed | tf_op | source)
XLA Modules:
  0.0 139.1 jit_solution(12737923319901444261)
XLA Ops:
  0.6 0.0 copy-start.2
  0.6 0.0 copy-start.3
  0.7 0.9 copy-done.3
  1.6 0.0 copy-start.4
  1.6 0.9 copy-done.4
  2.5 0.0 copy-start.9
  2.5 0.7 copy-done.9
  3.2 0.0 copy-start.5
  3.2 0.0 copy-start.6
  3.2 0.0 copy-start.7
  3.2 1.1 pack.1
  4.3 2.1 %collective-permute-start = (f32[8,8,256]{2,1,0:T(8,128)S(1)}, f32[8,8,256]{2,1,0:T(8,128)S(1)}, u32[]{:S(2)}, u32[]{:S(2)}) collective-permute-start(f32[8,8,256]{2,1,0:T(8,128)S(1)} %get-tuple-element.40), channel_id=1, source_target_pairs={{0,16},{16,32},{32,48},{48,64},{64,80},{80,96},{96,112},{112,128},... | collective-permute-start | bytes 196616 | tf_op jit(solution)/shard_map/ppermute | solution.py:832
  6.4 3.8 %collective-permute-start.1 = (f32[8,8,256]{2,1,0:T(8,128)S(1)}, f32[8,8,256]{2,1,0:T(8,128)S(1)}, u32[]{:S(2)}, u32[]{:S(2)}) collective-permute-start(f32[8,8,256]{2,1,0:T(8,128)S(1)} %get-tuple-element.41), channel_id=1, source_target_pairs={{16,0},{32,16},{48,32},{64,48},{80,64},{96,80},{112,96},{128,112},... | collective-permute-start | bytes 196616 | tf_op jit(solution)/shard_map/ppermute | solution.py:832
  10.2 1.6 %copy-done = f32[4,8,64,256]{3,2,1,0:T(8,128)S(1)} copy-done((f32[4,8,64,256]{3,2,1,0:T(8,128)S(1)}, f32[4,8,64,256]{3,2,1,0:T(8,128)}, u32[]{:S(2)}) %copy-start) | copy-done | bytes 2097176
  11.8 1.2 copy-done.1
  13.0 4.4 %upward.1 = (bf16[3,64,8192]{2,1,0:T(8,128)(2,1)S(1)}, f32[8,128]{1,0:T(8,128)S(1)}) custom-call(f32[4,8192]{1,0:T(4,128)S(1)} %get-tuple-element.42.r_ref, f32[32,64,256]{2,1,0:T(8,128)S(1)} %bitcast.6, f32[32,64,64]{2,1,0:T(8,128)S(1)} %bitcast.7), custom_call_target="tpu_custom_call" | custom-call | tf_op jit(solution)/shard_map/upward/pallas_call | solution.py:477
  17.4 0.0 collective-permute-done.up_ref
  17.4 0.0 collective-permute-done.1.down_ref
  17.5 2.5 %collective-permute-start.2 = (f32[6,8,256]{2,1,0:T(8,128)S(1)}, f32[6,8,256]{2,1,0:T(8,128)S(1)}, u32[]{:S(2)}, u32[]{:S(2)}) collective-permute-start(f32[6,8,256]{2,1,0:T(8,128)S(1)} %get-tuple-element.44), channel_id=1, source_target_pairs={{0,1},{1,2},{2,3},{3,4},{4,5},{5,6},{6,7},{7,8},{8,9},{9,10},{10,1... | collective-permute-start | bytes 147464 | tf_op jit(solution)/shard_map/ppermute | solution.py:832
  20.0 0.2 collective-permute-start.3
  20.2 0.0 copy-done.5
  20.2 0.7 copy-done.10
  20.9 1.4 %couplings.1 = (f32[7,64,64]{2,1,0:T(8,128)S(1)}, f32[7,64,64]{2,1,0:T(8,128)S(1)}, f32[2,64,64]{2,1,0:T(8,128)S(1)}) custom-call(f32[2,64,64]{2,1,0:T(8,128)S(1)} %copy-done.5, f32[3,64]{1,0:T(4,128)S(1)} %copy-done.10), custom_call_target="tpu_custom_call" | custom-call | tf_op jit(solution)/shard_map/couplings/pallas_call | solution.py:529
  22.4 0.0 collective-permute-done.2.left_ref
  22.4 1.2 collective-permute-done.3.right_ref
  23.5 0.0 copy-done.6
  23.5 0.0 copy-done.7
  23.5 0.7 copy-done.8
  24.2 5.4 %geometry.1 = (bf16[60,256,32]{2,1,0:T(8,128)(2,1)S(1)}, bf16[60,32,256]{2,1,0:T(8,128)(2,1)S(1)}, bf16[61,16,256]{2,1,0:T(8,128)(2,1)S(1)}, s32[296]{0:T(512)S(...) custom-call(s32[4,8,9]{2,1,0:T(8,128)S(1)} %copy-done.6, ...), custom_call_target="tpu_custom_call" | custom-call | tf_op jit(solution)/shard_map/geometry/pallas_call | solution.py:252
  29.6 16.1 %all_to_all.20.c_ref = f32[16,8,128]{2,1,0:T(8,128)S(1)} all-to-all(f32[16,8,128]{2,1,0:T(8,128)S(1)} %get-tuple-element.50), channel_id=1, replica_groups=mesh['gx'=16,'gy'=16] {'gy'}, dimensions={0} | all-to-all | bytes 131072 | tf_op jit(solution)/shard_map/all_to_all | solution.py:842
  45.7 0.8 row_tree.2
  46.5 9.8 %all_to_all.21.after_ref.x_ref = f32[16,8,128]{2,1,0:T(8,128)S(1)} all-to-all(f32[16,8,128]{2,1,0:T(8,128)S(1)} %get-tuple-element.53), channel_id=1, replica_groups=mesh['gx'=16,'gy'=16] {'gx'}, dimensions={0} | all-to-all | bytes 131072 | tf_op jit(solution)/shard_map/all_to_all | solution.py:842
  56.3 0.0 copy-done.2
  56.3 23.5 %near_build.1 = (f32[4,8192]{1,0:T(4,128)S(1)}, bf16[38,8,2,256,256]{4,3,2,1,0:T(8,128)(2,1)}) custom-call(s32[296]{0:T(512)S(1)} %get-tuple-element.47.long_ref, s32[296]{0:T(512)S(1)} %get-tuple-element.48.short_ref, s32[2]{0:T(128)S(1)} %get-tuple-element.49.groups_ref, bf16[61,16,256]{2,1,0:T(8,128)(2,1)S(1)} %get-tuple-element.56.v_ref, ...), custom_call_target="tpu_custom_call" | custom-call | tf_op jit(solution)/shard_map/near_build/pallas_call | solution.py:357
  79.8 2.7 %middle.1 = (f32[4,8192]{1,0:T(4,128)S(1)}, f32[32,4,256]{2,1,0:T(4,128)S(1)}, f32[8,4,256]{2,1,0:T(4,128)S(1)}, f32[8,4,256]{2,1,0:T(4,128)S(1)}, f32[8,128]{1,0:T(8,128)S(1)}, /*index=5*/f32[2,128]{1,0:T(2,128)S(1)}) custom-call(f32[16,8,128]{2,1,0:T(8,128)S(1)} %all_to_all.21.after_ref.x_ref, f32[8,64]{1,0:T(8,128)S(1)} %get-tuple-element.54.y_ref, ...), custom_call_target="tpu_custom_call" | custom-call | tf_op jit(solution)/shard_map/middle/pallas_call | solution.py:684
  82.5 4.0 %collective-permute-start.4 = (f32[8,4,256]{2,1,0:T(4,128)S(1)}, f32[8,4,256]{2,1,0:T(4,128)S(1)}, u32[]{:S(2)}, u32[]{:S(2)}) collective-permute-start(f32[8,4,256]{2,1,0:T(4,128)S(1)} %get-tuple-element.62), channel_id=1, source_target_pairs={{0,16},{16,32},{32,48},{48,64},{64,80},{80,96},{96,112},{112,128},... | collective-permute-start | bytes 98312 | tf_op jit(solution)/shard_map/ppermute | solution.py:832
  86.5 0.8 collective-permute-start.5
  87.3 1.3 collective-permute-done.4.up_ref
  88.6 1.0 collective-permute-done.5.down_ref
  89.6 1.5 %collective-permute-start.6 = (f32[6,4,256]{2,1,0:T(4,128)S(1)}, f32[6,4,256]{2,1,0:T(4,128)S(1)}, u32[]{:S(2)}, u32[]{:S(2)}) collective-permute-start(f32[6,4,256]{2,1,0:T(4,128)S(1)} %get-tuple-element.65), channel_id=1, source_target_pairs={{0,1},{1,2},{2,3},{3,4},{4,5},{5,6},{6,7},{7,8},{8,9},{9,10},{10,1... | collective-permute-start | bytes 73736 | tf_op jit(solution)/shard_map/ppermute | solution.py:832
  91.0 0.3 collective-permute-start.7
  91.4 0.7 collective-permute-done.6.left_ref
  92.0 2.3 %collective-permute-done.7.right_ref = f32[6,4,256]{2,1,0:T(4,128)S(1)} collective-permute-done((f32[6,4,256]{2,1,0:T(4,128)S(1)}, f32[6,4,256]{2,1,0:T(4,128)S(1)}, u32[]{:S(2)}, u32[]{:S(2)}) %collective-permute-start.7) | collective-permute-done | bytes 24608 | tf_op jit(solution)/shard_map/ppermute | solution.py:832
  94.3 12.5 %near_reuse.1 = (f32[4,8192]{1,0:T(4,128)S(1)}, f32[16,8,128]{2,1,0:T(8,128)S(1)}) custom-call(s32[296]{0:T(512)S(1)} %get-tuple-element.47.long_ref, s32[296]{0:T(512)S(1)} %get-tuple-element.48.short_ref, s32[2]{0:T(128)S(1)} %get-tuple-element.49.groups_ref, f32[32,4,256]{2,1,0:T(4,128)S(1)} %get-tuple-element.61.own_ref, ...), custom_call_target="tpu_custom_call" | custom-call | tf_op jit(solution)/shard_map/near_reuse/pallas_call | solution.py:443
  106.8 15.1 %all_to_all.22.c_ref = f32[16,8,128]{2,1,0:T(8,128)S(1)} all-to-all(f32[16,8,128]{2,1,0:T(8,128)S(1)} %get-tuple-element.68), channel_id=1, replica_groups=mesh['gx'=16,'gy'=16] {'gy'}, dimensions={0} | all-to-all | bytes 131072 | tf_op jit(solution)/shard_map/all_to_all | solution.py:842
  121.9 0.9 row_tree.3
  122.8 12.5 %all_to_all.23.c_ref = f32[16,8,128]{2,1,0:T(8,128)S(1)} all-to-all(f32[16,8,128]{2,1,0:T(8,128)S(1)} %get-tuple-element.69), channel_id=1, replica_groups=mesh['gx'=16,'gy'=16] {'gx'}, dimensions={0} | all-to-all | bytes 131072 | tf_op jit(solution)/shard_map/all_to_all | solution.py:842
  135.3 3.8 %final.1 = (f32[32,4,256]{2,1,0:T(4,128)}, f32[32,4,256]{2,1,0:T(4,128)}) custom-call(f32[16,8,128]{2,1,0:T(8,128)S(1)} %all_to_all.23.c_ref, f32[8,64]{1,0:T(8,128)S(1)} %get-tuple-element.70.y_ref, f32[2,64,64]{2,1,0:T(8,128)S(1)} %get-tuple-element.51.upper_ref, f32[7,64,64]{2,1,0:T(8,128)S(1)} %get-tuple-element.52.g_ref, ...), custom_call_target="tpu_custom_call" | custom-call | tf_op jit(solution)/shard_map/final/pallas_call | solution.py:817
  (6 shorter events, 0.0 us)
Async XLA Ops:
  0.6 55.6 %copy-start.2 = (bf16[9,32,256]{2,1,0:T(8,128)(2,1)S(1)}, bf16[9,32,256]{2,1,0:T(8,128)(2,1)}, u32[]{:S(2)}) copy-start(bf16[9,32,256]{2,1,0:T(8,128)(2,1)} %constant.6.clone.factor_ref) | copy-start | bytes 442372
  0.6 0.9 copy-start.3
  1.6 0.9 copy-start.4
  2.5 0.7 copy-start.9
  3.2 17.1 %copy-start.5 = (f32[2,64,64]{2,1,0:T(8,128)S(1)}, f32[2,64,64]{2,1,0:T(8,128)}, u32[]{:S(2)}) copy-start(f32[2,64,64]{2,1,0:T(8,128)} %upper_ref.1) | copy-start | bytes 98308
  3.2 20.4 %copy-start.6 = (s32[4,8,9]{2,1,0:T(8,128)S(1)}, s32[4,8,9]{2,1,0:T(8,128)}, u32[]{:S(2)}) copy-start(s32[4,8,9]{2,1,0:T(8,128)} %mask_ref.1) | copy-start | bytes 3460
  3.2 20.4 %copy-start.7 = (bf16[32,24]{1,0:T(8,128)(2,1)S(1)}, bf16[32,24]{1,0:T(8,128)(2,1)}, u32[]{:S(2)}) copy-start(bf16[32,24]{1,0:T(8,128)(2,1)} %constant.8.clone.source_ref) | copy-start | bytes 4612
  4.3 13.1 %collective-permute-start = (f32[8,8,256]{2,1,0:T(8,128)S(1)}, f32[8,8,256]{2,1,0:T(8,128)S(1)}, u32[]{:S(2)}, u32[]{:S(2)}) collective-permute-start(f32[8,8,256]{2,1,0:T(8,128)S(1)} %get-tuple-element.40), channel_id=1, source_target_pairs={{0,16},{16,32},{32,48},{48,64},{64,80},{80,96},{96,112},{112,128},... | collective-permute-start | bytes 196616 | tf_op jit(solution)/shard_map/ppermute | solution.py:832
  6.4 11.1 %collective-permute-start.1 = (f32[8,8,256]{2,1,0:T(8,128)S(1)}, f32[8,8,256]{2,1,0:T(8,128)S(1)}, u32[]{:S(2)}, u32[]{:S(2)}) collective-permute-start(f32[8,8,256]{2,1,0:T(8,128)S(1)} %get-tuple-element.41), channel_id=1, source_target_pairs={{16,0},{32,16},{48,32},{64,48},{80,64},{96,80},{112,96},{128,112},... | collective-permute-start | bytes 196616 | tf_op jit(solution)/shard_map/ppermute | solution.py:832
  10.2 1.6 %copy-start = (f32[4,8,64,256]{3,2,1,0:T(8,128)S(1)}, f32[4,8,64,256]{3,2,1,0:T(8,128)}, u32[]{:S(2)}) copy-start(f32[4,8,64,256]{3,2,1,0:T(8,128)} %param.15) | copy-start | bytes 6291460
  11.8 1.2 copy-start.1
  17.5 4.9 %collective-permute-start.2 = (f32[6,8,256]{2,1,0:T(8,128)S(1)}, f32[6,8,256]{2,1,0:T(8,128)S(1)}, u32[]{:S(2)}, u32[]{:S(2)}) collective-permute-start(f32[6,8,256]{2,1,0:T(8,128)S(1)} %get-tuple-element.44), channel_id=1, source_target_pairs={{0,1},{1,2},{2,3},{3,4},{4,5},{5,6},{6,7},{7,8},{8,9},{9,10},{10,1... | collective-permute-start | bytes 147464 | tf_op jit(solution)/shard_map/ppermute | solution.py:832
  20.0 3.5 %collective-permute-start.3 = (f32[6,8,256]{2,1,0:T(8,128)S(1)}, f32[6,8,256]{2,1,0:T(8,128)S(1)}, u32[]{:S(2)}, u32[]{:S(2)}) collective-permute-start(f32[6,8,256]{2,1,0:T(8,128)S(1)} %get-tuple-element.45), channel_id=1, source_target_pairs={{1,0},{2,1},{3,2},{4,3},{5,4},{6,5},{7,6},{8,7},{9,8},{10,9},{11,1... | collective-permute-start | bytes 147464 | tf_op jit(solution)/shard_map/ppermute | solution.py:832
  20.2 0.7 copy-start.10
  23.5 0.7 copy-start.8
  82.5 6.1 %collective-permute-start.4 = (f32[8,4,256]{2,1,0:T(4,128)S(1)}, f32[8,4,256]{2,1,0:T(4,128)S(1)}, u32[]{:S(2)}, u32[]{:S(2)}) collective-permute-start(f32[8,4,256]{2,1,0:T(4,128)S(1)} %get-tuple-element.62), channel_id=1, source_target_pairs={{0,16},{16,32},{32,48},{48,64},{64,80},{80,96},{96,112},{112,128},... | collective-permute-start | bytes 98312 | tf_op jit(solution)/shard_map/ppermute | solution.py:832
  86.5 3.1 %collective-permute-start.5 = (f32[8,4,256]{2,1,0:T(4,128)S(1)}, f32[8,4,256]{2,1,0:T(4,128)S(1)}, u32[]{:S(2)}, u32[]{:S(2)}) collective-permute-start(f32[8,4,256]{2,1,0:T(4,128)S(1)} %get-tuple-element.63), channel_id=1, source_target_pairs={{16,0},{32,16},{48,32},{64,48},{80,64},{96,80},{112,96},{128,112},... | collective-permute-start | bytes 98312 | tf_op jit(solution)/shard_map/ppermute | solution.py:832
  89.6 2.5 %collective-permute-start.6 = (f32[6,4,256]{2,1,0:T(4,128)S(1)}, f32[6,4,256]{2,1,0:T(4,128)S(1)}, u32[]{:S(2)}, u32[]{:S(2)}) collective-permute-start(f32[6,4,256]{2,1,0:T(4,128)S(1)} %get-tuple-element.65), channel_id=1, source_target_pairs={{0,1},{1,2},{2,3},{3,4},{4,5},{5,6},{6,7},{7,8},{8,9},{9,10},{10,1... | collective-permute-start | bytes 73736 | tf_op jit(solution)/shard_map/ppermute | solution.py:832
  91.0 3.3 %collective-permute-start.7 = (f32[6,4,256]{2,1,0:T(4,128)S(1)}, f32[6,4,256]{2,1,0:T(4,128)S(1)}, u32[]{:S(2)}, u32[]{:S(2)}) collective-permute-start(f32[6,4,256]{2,1,0:T(4,128)S(1)} %get-tuple-element.66), channel_id=1, source_target_pairs={{1,0},{2,1},{3,2},{4,3},{5,4},{6,5},{7,6},{8,7},{9,8},{10,9},{11,1... | collective-permute-start | bytes 73736 | tf_op jit(solution)/shard_map/ppermute | solution.py:832

commit v6 on v5

--- a/solution.py
+++ b/solution.py
@@ -16,11 +16,11 @@
 FAR_RATE = 3.0**0.5 / FAR_LENGTH
 LOG2E = 1.4426950408889634
 COUPLING_SCALE = 1.0 / 128.0
-GROUP = 8
+GROUP = 16
 CHUNK = 64
 BUILD_SLOTS = 2
-READ_SLOTS = 6
-VMEM_LIMIT = 20 * 2**20
+READ_SLOTS = 5
+VMEM_LIMIT = 28 * 2**20
 VM = pl.BlockSpec(memory_space=pltpu.VMEM)
 ANY = pl.BlockSpec(memory_space=pl.ANY)
 SM = pl.BlockSpec(memory_space=pltpu.SMEM)

time: 140 us -> 141 us (level)
  Pallas kernels: 56.4 us -> 59.6 us
    pallas_call x1, Pallas kernels: 12.5 us -> 14.4 us  [near_reuse(): pl.pallas_call(functools.partial(reuse_kernel, nx, ny), out_shape=[jax.Sh...]
  transfers between devices with their start and end apart: 8 -> 8, of which waited for: 5 -> 4; matrix products, arithmetic and copies ran while one was open for 0% -> 0% of each run, Pallas kernels for 4% -> 4%
where the time goes in v6:
time: 141 us; the launch traced here: 140 us
  Pallas kernels  59.6 us (42%)
  blocking collectives  52.4 us (37%)
  starting transfers between devices  14.8 us (10%)
  local copies, waits for them, and re-layouts  6.72 us (5%)
  waiting for transfers between devices  5.92 us (4%)
    all_to_all x4, blocking collectives, exchange(): return lax.all_to_all(x, axis, 0, 0, tiled=True)  52.4 us
    pallas_call x1, Pallas kernels, near_build(): pl.pallas_call(functools.partial(build_kernel, nx, ny), out_shape=[jax.Sh...  24.8 us
    ppermute x8, starting transfers between devices, swap(): return (lax.ppermute(last, axis, up), lax.ppermute(first, axis, down))  14.8 us
    pallas_call x1, Pallas kernels, near_reuse(): pl.pallas_call(functools.partial(reuse_kernel, nx, ny), out_shape=[jax.Sh...  14.4 us
    unnamed x22, local copies, waits for them, and re-layouts  6.72 us
    ppermute x8, waiting for transfers between devices, swap(): return (lax.ppermute(last, axis, up), lax.ppermute(first, axis, down))  5.92 us
    pallas_call x1, Pallas kernels, geometry(): pl.pallas_call(functools.partial(geometry_kernel, nx, ny), out_shape=[jax...  5.38 us
    pallas_call x1, Pallas kernels, upward(): pl.pallas_call(upward_kernel, out_shape=[jax.ShapeDtypeStruct((3, terms,...  4.39 us
  transfers between devices with their start and end apart: 8, of which 4 were waited for; matrix products, arithmetic and copies ran while one was open for 0% of the time, Pallas kernels for 4%

profile of v6, /device:TPU:1, one launch (start us, length us, event | category | flops | bytes accessed | tf_op | source)
XLA Modules:
  0.0 140.2 jit_solution(214924649784008730)
XLA Ops:
  0.6 0.0 copy-start.2
  0.6 0.0 copy-start.3
  0.7 0.9 copy-done.3
  1.6 0.0 copy-start.4
  1.6 0.9 copy-done.4
  2.5 0.0 copy-start.9
  2.5 0.7 copy-done.9
  3.2 0.0 copy-start.5
  3.2 0.0 copy-start.6
  3.2 0.0 copy-start.7
  3.2 1.1 pack.1
  4.3 2.1 %collective-permute-start = (f32[8,8,256]{2,1,0:T(8,128)S(1)}, f32[8,8,256]{2,1,0:T(8,128)S(1)}, u32[]{:S(2)}, u32[]{:S(2)}) collective-permute-start(f32[8,8,256]{2,1,0:T(8,128)S(1)} %get-tuple-element.40), channel_id=1, source_target_pairs={{0,16},{16,32},{32,48},{48,64},{64,80},{80,96},{96,112},{112,128},... | collective-permute-start | bytes 196616 | tf_op jit(solution)/shard_map/ppermute | solution.py:832
  6.4 3.8 %collective-permute-start.1 = (f32[8,8,256]{2,1,0:T(8,128)S(1)}, f32[8,8,256]{2,1,0:T(8,128)S(1)}, u32[]{:S(2)}, u32[]{:S(2)}) collective-permute-start(f32[8,8,256]{2,1,0:T(8,128)S(1)} %get-tuple-element.41), channel_id=1, source_target_pairs={{16,0},{32,16},{48,32},{64,48},{80,64},{96,80},{112,96},{128,112},... | collective-permute-start | bytes 196616 | tf_op jit(solution)/shard_map/ppermute | solution.py:832
  10.2 1.6 %copy-done = f32[4,8,64,256]{3,2,1,0:T(8,128)S(1)} copy-done((f32[4,8,64,256]{3,2,1,0:T(8,128)S(1)}, f32[4,8,64,256]{3,2,1,0:T(8,128)}, u32[]{:S(2)}) %copy-start) | copy-done | bytes 2097176
  11.8 1.2 copy-done.1
  13.0 4.4 %upward.1 = (bf16[3,64,8192]{2,1,0:T(8,128)(2,1)S(1)}, f32[8,128]{1,0:T(8,128)S(1)}) custom-call(f32[4,8192]{1,0:T(4,128)S(1)} %get-tuple-element.42.r_ref, f32[32,64,256]{2,1,0:T(8,128)S(1)} %bitcast.6, f32[32,64,64]{2,1,0:T(8,128)S(1)} %bitcast.7), custom_call_target="tpu_custom_call" | custom-call | tf_op jit(solution)/shard_map/upward/pallas_call | solution.py:477
  17.4 0.0 collective-permute-done.up_ref
  17.4 0.0 collective-permute-done.1.down_ref
  17.5 2.5 %collective-permute-start.2 = (f32[6,8,256]{2,1,0:T(8,128)S(1)}, f32[6,8,256]{2,1,0:T(8,128)S(1)}, u32[]{:S(2)}, u32[]{:S(2)}) collective-permute-start(f32[6,8,256]{2,1,0:T(8,128)S(1)} %get-tuple-element.44), channel_id=1, source_target_pairs={{0,1},{1,2},{2,3},{3,4},{4,5},{5,6},{6,7},{7,8},{8,9},{9,10},{10,1... | collective-permute-start | bytes 147464 | tf_op jit(solution)/shard_map/ppermute | solution.py:832
  20.0 0.2 collective-permute-start.3
  20.2 0.0 copy-done.5
  20.2 0.7 copy-done.10
  20.9 1.4 %couplings.1 = (f32[7,64,64]{2,1,0:T(8,128)S(1)}, f32[7,64,64]{2,1,0:T(8,128)S(1)}, f32[2,64,64]{2,1,0:T(8,128)S(1)}) custom-call(f32[2,64,64]{2,1,0:T(8,128)S(1)} %copy-done.5, f32[3,64]{1,0:T(4,128)S(1)} %copy-done.10), custom_call_target="tpu_custom_call" | custom-call | tf_op jit(solution)/shard_map/couplings/pallas_call | solution.py:529
  22.4 0.0 collective-permute-done.2.left_ref
  22.4 1.2 collective-permute-done.3.right_ref
  23.5 0.0 copy-done.6
  23.5 0.0 copy-done.7
  23.5 0.7 copy-done.8
  24.2 5.4 %geometry.1 = (bf16[60,256,32]{2,1,0:T(8,128)(2,1)S(1)}, bf16[60,32,256]{2,1,0:T(8,128)(2,1)S(1)}, bf16[61,16,256]{2,1,0:T(8,128)(2,1)S(1)}, s32[304]{0:T(512)S(...) custom-call(s32[4,8,9]{2,1,0:T(8,128)S(1)} %copy-done.6, ...), custom_call_target="tpu_custom_call" | custom-call | tf_op jit(solution)/shard_map/geometry/pallas_call | solution.py:252
  29.6 16.1 %all_to_all.20.c_ref = f32[16,8,128]{2,1,0:T(8,128)S(1)} all-to-all(f32[16,8,128]{2,1,0:T(8,128)S(1)} %get-tuple-element.50), channel_id=1, replica_groups=mesh['gx'=16,'gy'=16] {'gy'}, dimensions={0} | all-to-all | bytes 131072 | tf_op jit(solution)/shard_map/all_to_all | solution.py:842
  45.7 0.8 row_tree.2
  46.5 9.8 %all_to_all.21.after_ref.x_ref = f32[16,8,128]{2,1,0:T(8,128)S(1)} all-to-all(f32[16,8,128]{2,1,0:T(8,128)S(1)} %get-tuple-element.53), channel_id=1, replica_groups=mesh['gx'=16,'gy'=16] {'gx'}, dimensions={0} | all-to-all | bytes 131072 | tf_op jit(solution)/shard_map/all_to_all | solution.py:842
  56.3 0.0 copy-done.2
  56.3 24.8 %near_build.1 = (f32[4,8192]{1,0:T(4,128)S(1)}, bf16[20,16,2,256,256]{4,3,2,1,0:T(8,128)(2,1)}) custom-call(s32[304]{0:T(512)S(1)} %get-tuple-element.47.long_ref, s32[304]{0:T(512)S(1)} %get-tuple-element.48.short_ref, s32[2]{0:T(128)S(1)} %get-tuple-element.49.groups_ref, bf16[61,16,256]{2,1,0:T(8,128)(2,1)S(1)} %get-tuple-element.56.v_ref, ...), custom_call_target="tpu_custom_call" | custom-call | tf_op jit(solution)/shard_map/near_build/pallas_call | solution.py:357
  81.0 2.7 %middle.1 = (f32[4,8192]{1,0:T(4,128)S(1)}, f32[32,4,256]{2,1,0:T(4,128)S(1)}, f32[8,4,256]{2,1,0:T(4,128)S(1)}, f32[8,4,256]{2,1,0:T(4,128)S(1)}, f32[8,128]{1,0:T(8,128)S(1)}, /*index=5*/f32[2,128]{1,0:T(2,128)S(1)}) custom-call(f32[16,8,128]{2,1,0:T(8,128)S(1)} %all_to_all.21.after_ref.x_ref, f32[8,64]{1,0:T(8,128)S(1)} %get-tuple-element.54.y_ref, ...), custom_call_target="tpu_custom_call" | custom-call | tf_op jit(solution)/shard_map/middle/pallas_call | solution.py:684
  83.7 0.0 collective-permute-start.4
  83.7 4.8 %collective-permute-start.5 = (f32[8,4,256]{2,1,0:T(4,128)S(1)}, f32[8,4,256]{2,1,0:T(4,128)S(1)}, u32[]{:S(2)}, u32[]{:S(2)}) collective-permute-start(f32[8,4,256]{2,1,0:T(4,128)S(1)} %get-tuple-element.63), channel_id=1, source_target_pairs={{16,0},{32,16},{48,32},{64,48},{80,64},{96,80},{112,96},{128,112},... | collective-permute-start | bytes 98312 | tf_op jit(solution)/shard_map/ppermute | solution.py:832
  88.5 1.5 %collective-permute-done.4.up_ref = f32[8,4,256]{2,1,0:T(4,128)S(1)} collective-permute-done((f32[8,4,256]{2,1,0:T(4,128)S(1)}, f32[8,4,256]{2,1,0:T(4,128)S(1)}, u32[]{:S(2)}, u32[]{:S(2)}) %collective-permute-start.4) | collective-permute-done | bytes 32800 | tf_op jit(solution)/shard_map/ppermute | solution.py:832
  90.0 0.0 collective-permute-done.5.down_ref
  90.0 1.3 collective-permute-start.6
  91.4 0.0 collective-permute-start.7
  91.4 0.9 collective-permute-done.6.left_ref
  92.3 2.3 %collective-permute-done.7.right_ref = f32[6,4,256]{2,1,0:T(4,128)S(1)} collective-permute-done((f32[6,4,256]{2,1,0:T(4,128)S(1)}, f32[6,4,256]{2,1,0:T(4,128)S(1)}, u32[]{:S(2)}, u32[]{:S(2)}) %collective-permute-start.7) | collective-permute-done | bytes 24608 | tf_op jit(solution)/shard_map/ppermute | solution.py:832
  94.6 14.4 %near_reuse.1 = (f32[4,8192]{1,0:T(4,128)S(1)}, f32[16,8,128]{2,1,0:T(8,128)S(1)}) custom-call(s32[304]{0:T(512)S(1)} %get-tuple-element.47.long_ref, s32[304]{0:T(512)S(1)} %get-tuple-element.48.short_ref, s32[2]{0:T(128)S(1)} %get-tuple-element.49.groups_ref, f32[32,4,256]{2,1,0:T(4,128)S(1)} %get-tuple-element.61.own_ref, ...), custom_call_target="tpu_custom_call" | custom-call | tf_op jit(solution)/shard_map/near_reuse/pallas_call | solution.py:443
  109.0 13.7 %all_to_all.22.c_ref = f32[16,8,128]{2,1,0:T(8,128)S(1)} all-to-all(f32[16,8,128]{2,1,0:T(8,128)S(1)} %get-tuple-element.68), channel_id=1, replica_groups=mesh['gx'=16,'gy'=16] {'gy'}, dimensions={0} | all-to-all | bytes 131072 | tf_op jit(solution)/shard_map/all_to_all | solution.py:842
  122.6 0.9 row_tree.3
  123.5 12.9 %all_to_all.23.c_ref = f32[16,8,128]{2,1,0:T(8,128)S(1)} all-to-all(f32[16,8,128]{2,1,0:T(8,128)S(1)} %get-tuple-element.69), channel_id=1, replica_groups=mesh['gx'=16,'gy'=16] {'gx'}, dimensions={0} | all-to-all | bytes 131072 | tf_op jit(solution)/shard_map/all_to_all | solution.py:842
  136.4 3.8 %final.1 = (f32[32,4,256]{2,1,0:T(4,128)}, f32[32,4,256]{2,1,0:T(4,128)}) custom-call(f32[16,8,128]{2,1,0:T(8,128)S(1)} %all_to_all.23.c_ref, f32[8,64]{1,0:T(8,128)S(1)} %get-tuple-element.70.y_ref, f32[2,64,64]{2,1,0:T(8,128)S(1)} %get-tuple-element.51.upper_ref, f32[7,64,64]{2,1,0:T(8,128)S(1)} %get-tuple-element.52.g_ref, ...), custom_call_target="tpu_custom_call" | custom-call | tf_op jit(solution)/shard_map/final/pallas_call | solution.py:817
  (6 shorter events, 0.0 us)
Async XLA Ops:
  0.6 55.6 %copy-start.2 = (bf16[9,32,256]{2,1,0:T(8,128)(2,1)S(1)}, bf16[9,32,256]{2,1,0:T(8,128)(2,1)}, u32[]{:S(2)}) copy-start(bf16[9,32,256]{2,1,0:T(8,128)(2,1)} %constant.6.clone.factor_ref) | copy-start | bytes 442372
  0.6 0.9 copy-start.3
  1.6 0.9 copy-start.4
  2.5 0.7 copy-start.9
  3.2 17.1 %copy-start.5 = (f32[2,64,64]{2,1,0:T(8,128)S(1)}, f32[2,64,64]{2,1,0:T(8,128)}, u32[]{:S(2)}) copy-start(f32[2,64,64]{2,1,0:T(8,128)} %upper_ref.1) | copy-start | bytes 98308
  3.2 20.4 %copy-start.6 = (s32[4,8,9]{2,1,0:T(8,128)S(1)}, s32[4,8,9]{2,1,0:T(8,128)}, u32[]{:S(2)}) copy-start(s32[4,8,9]{2,1,0:T(8,128)} %mask_ref.1) | copy-start | bytes 3460
  3.2 20.4 %copy-start.7 = (bf16[32,24]{1,0:T(8,128)(2,1)S(1)}, bf16[32,24]{1,0:T(8,128)(2,1)}, u32[]{:S(2)}) copy-start(bf16[32,24]{1,0:T(8,128)(2,1)} %constant.8.clone.source_ref) | copy-start | bytes 4612
  4.3 13.1 %collective-permute-start = (f32[8,8,256]{2,1,0:T(8,128)S(1)}, f32[8,8,256]{2,1,0:T(8,128)S(1)}, u32[]{:S(2)}, u32[]{:S(2)}) collective-permute-start(f32[8,8,256]{2,1,0:T(8,128)S(1)} %get-tuple-element.40), channel_id=1, source_target_pairs={{0,16},{16,32},{32,48},{48,64},{64,80},{80,96},{96,112},{112,128},... | collective-permute-start | bytes 196616 | tf_op jit(solution)/shard_map/ppermute | solution.py:832
  6.4 11.1 %collective-permute-start.1 = (f32[8,8,256]{2,1,0:T(8,128)S(1)}, f32[8,8,256]{2,1,0:T(8,128)S(1)}, u32[]{:S(2)}, u32[]{:S(2)}) collective-permute-start(f32[8,8,256]{2,1,0:T(8,128)S(1)} %get-tuple-element.41), channel_id=1, source_target_pairs={{16,0},{32,16},{48,32},{64,48},{80,64},{96,80},{112,96},{128,112},... | collective-permute-start | bytes 196616 | tf_op jit(solution)/shard_map/ppermute | solution.py:832
  10.2 1.6 %copy-start = (f32[4,8,64,256]{3,2,1,0:T(8,128)S(1)}, f32[4,8,64,256]{3,2,1,0:T(8,128)}, u32[]{:S(2)}) copy-start(f32[4,8,64,256]{3,2,1,0:T(8,128)} %param.15) | copy-start | bytes 6291460
  11.8 1.2 copy-start.1
  17.5 4.9 %collective-permute-start.2 = (f32[6,8,256]{2,1,0:T(8,128)S(1)}, f32[6,8,256]{2,1,0:T(8,128)S(1)}, u32[]{:S(2)}, u32[]{:S(2)}) collective-permute-start(f32[6,8,256]{2,1,0:T(8,128)S(1)} %get-tuple-element.44), channel_id=1, source_target_pairs={{0,1},{1,2},{2,3},{3,4},{4,5},{5,6},{6,7},{7,8},{8,9},{9,10},{10,1... | collective-permute-start | bytes 147464 | tf_op jit(solution)/shard_map/ppermute | solution.py:832
  20.0 3.5 %collective-permute-start.3 = (f32[6,8,256]{2,1,0:T(8,128)S(1)}, f32[6,8,256]{2,1,0:T(8,128)S(1)}, u32[]{:S(2)}, u32[]{:S(2)}) collective-permute-start(f32[6,8,256]{2,1,0:T(8,128)S(1)} %get-tuple-element.45), channel_id=1, source_target_pairs={{1,0},{2,1},{3,2},{4,3},{5,4},{6,5},{7,6},{8,7},{9,8},{10,9},{11,1... | collective-permute-start | bytes 147464 | tf_op jit(solution)/shard_map/ppermute | solution.py:832
  20.2 0.7 copy-start.10
  23.5 0.7 copy-start.8
  83.7 6.3 %collective-permute-start.4 = (f32[8,4,256]{2,1,0:T(4,128)S(1)}, f32[8,4,256]{2,1,0:T(4,128)S(1)}, u32[]{:S(2)}, u32[]{:S(2)}) collective-permute-start(f32[8,4,256]{2,1,0:T(4,128)S(1)} %get-tuple-element.62), channel_id=1, source_target_pairs={{0,16},{16,32},{32,48},{48,64},{64,80},{80,96},{96,112},{112,128},... | collective-permute-start | bytes 98312 | tf_op jit(solution)/shard_map/ppermute | solution.py:832
  83.7 6.3 %collective-permute-start.5 = (f32[8,4,256]{2,1,0:T(4,128)S(1)}, f32[8,4,256]{2,1,0:T(4,128)S(1)}, u32[]{:S(2)}, u32[]{:S(2)}) collective-permute-start(f32[8,4,256]{2,1,0:T(4,128)S(1)} %get-tuple-element.63), channel_id=1, source_target_pairs={{16,0},{32,16},{48,32},{64,48},{80,64},{96,80},{112,96},{128,112},... | collective-permute-start | bytes 98312 | tf_op jit(solution)/shard_map/ppermute | solution.py:832
  90.0 2.3 %collective-permute-start.6 = (f32[6,4,256]{2,1,0:T(4,128)S(1)}, f32[6,4,256]{2,1,0:T(4,128)S(1)}, u32[]{:S(2)}, u32[]{:S(2)}) collective-permute-start(f32[6,4,256]{2,1,0:T(4,128)S(1)} %get-tuple-element.65), channel_id=1, source_target_pairs={{0,1},{1,2},{2,3},{3,4},{4,5},{5,6},{6,7},{7,8},{8,9},{9,10},{10,1... | collective-permute-start | bytes 73736 | tf_op jit(solution)/shard_map/ppermute | solution.py:832
  91.4 3.3 %collective-permute-start.7 = (f32[6,4,256]{2,1,0:T(4,128)S(1)}, f32[6,4,256]{2,1,0:T(4,128)S(1)}, u32[]{:S(2)}, u32[]{:S(2)}) collective-permute-start(f32[6,4,256]{2,1,0:T(4,128)S(1)} %get-tuple-element.66), channel_id=1, source_target_pairs={{1,0},{2,1},{3,2},{4,3},{5,4},{6,5},{7,6},{8,7},{9,8},{10,9},{11,1... | collective-permute-start | bytes 73736 | tf_op jit(solution)/shard_map/ppermute | solution.py:832
